TPU v7x, 128 devices: a whole 4x4x4 slice. The times are simulated.
128 devices in a mesh: tile: 16 (over y, x_lo, core), lat: 8 (over x_hi, z).
Axes of the slice: x: 4 (x_hi: 2, x_lo: 2; x = x_hi * 2 + x_lo), y: 4, z: 4, core: 2. Of those that a mesh axis runs over, the one named last changes fastest.
Arguments:
- field: bfloat16 [384, 768, 256], P('lat', 'tile'), may hold values from -6 to 6
- cotangent: bfloat16 [384, 768, 256], P('lat', 'tile'), may hold values from -9 to 9
- first_weight: bfloat16 [3, 3, 256, 256], replicated, may hold values from -0.125 to 0.125
- second_weight: bfloat16 [3, 3, 256, 256], replicated, may hold values from -0.125 to 0.125
- side_links: int32 [8, 16, 4, 3], replicated, may hold values from 0 to 7, as said below
- corner_links: int32 [8, 16, 4, 3], replicated, may hold values from 0 to 8, as said below
Outputs:
- mixed: bfloat16 [384, 768, 256], P('lat', 'tile')
- input_grad: bfloat16 [384, 768, 256], P('lat', 'tile')
- first_weight_grad: float32 [3, 3, 256, 256], replicated
- second_weight_grad: float32 [3, 3, 256, 256], replicated
Inputs may be any that keep to these rules, and one draw needn't show every extreme that they name: `side_links`: entry [i, j, s] describes side s of tile (i, j) in that tile's frame (0 row above, 1 row below, 2 column left, 3 column right): [0] the slot of the neighbouring tile, [1] which of its edges fills the strip, [2] 1 where the strip runs in reverse order, else 0. The tiles' frames are quarter-turn rotations of one grid that wraps both ways, so each edge of a tile fills exactly one strip of one side neighbour. `corner_links`: entry [i, j, c] describes padded corner c of tile (i, j): [0] the slot of the diagonal neighbour, [1] which of its corners, [2] 1 where the padded corner is kept and 0 where it is missing. Each corner of a tile is named by exactly one diagonal neighbour.
All inputs are finite; a program needn't handle non-finite values.
Results may differ from a plain program's by a relative error of at most 0.0085.
Values may be sent and summed in bfloat16 or wider, within the bound.
No kernel may reach another device: no remote copies, remote signals or barrier semaphores. Data moves between devices by JAX's collectives and lax.ppermute only.
A program may use at most 192 MiB of HBM per device.

v0:
```python
import math

import jax
import jax.numpy as jnp
from jax import lax
from jax.sharding import PartitionSpec as P


def with_halo(cells, sides, width):
    for axis, dim in sides:
        count = lax.axis_size(axis)
        head = lax.slice_in_dim(cells, 0, width, axis=dim)
        tail = lax.slice_in_dim(cells, cells.shape[dim] - width, cells.shape[dim], axis=dim)
        cells = jnp.concatenate(
            [
                lax.ppermute(tail, axis, [(i, (i + 1) % count) for i in range(count)]),
                cells,
                lax.ppermute(head, axis, [((i + 1) % count, i) for i in range(count)]),
            ],
            axis=dim,
        )
    return cells


def gelu(values):
    return jax.nn.gelu(values, approximate=False)


def gelu_slope(values):
    return jax.jvp(gelu, (values,), (jnp.ones_like(values),))[1]


def edge_stack(patch):
    return jnp.stack([patch[0], patch[-1], patch[:, 0], patch[:, -1]])


def corner_stack(patch):
    return jnp.stack([patch[0, 0], patch[0, -1], patch[-1, 0], patch[-1, -1]])


def trade(edge_rows, corner_cells):
    side = edge_rows.shape[1]
    width = edge_rows.shape[2]
    filler = jnp.zeros((side - 4, width), corner_cells.dtype)
    packed = jnp.concatenate(
        [edge_rows, jnp.concatenate([corner_cells, filler], axis=0)[None]], axis=0
    )
    received = with_halo(packed[None, None], (("tile", 1), ("lat", 0)), 1).reshape(
        9, 5, side, width
    )
    return (received[:, :4].reshape(36, side, width), received[:, 4, :4].reshape(36, width))


def place_frame(middle, left_col, right_col, top_row, bottom_row, cells):
    center = jnp.concatenate([left_col[:, None], middle, right_col[:, None]], axis=1)
    upper = jnp.concatenate([cells[0:1], top_row, cells[1:2]], axis=0)
    lower = jnp.concatenate([cells[2:3], bottom_row, cells[3:4]], axis=0)
    return jnp.concatenate([upper[None], center, lower[None]], axis=0)


def extend(patch, own_links, own_corners):
    got_edges, got_corners = trade(edge_stack(patch), corner_stack(patch))
    strips = []
    for place in range(4):
        index = own_links[place, 0] * 4 + own_links[place, 1]
        strip = lax.dynamic_index_in_dim(got_edges, index, 0, keepdims=False)
        strips.append(jnp.where(own_links[place, 2] == 1, strip[::-1], strip))
    cells = []
    for place in range(4):
        index = own_corners[place, 0] * 4 + own_corners[place, 1]
        cell_value = lax.dynamic_index_in_dim(got_corners, index, 0, keepdims=False)
        cells.append(cell_value * own_corners[place, 2].astype(patch.dtype))
    return place_frame(patch, strips[2], strips[3], strips[0], strips[1], jnp.stack(cells))


def convolve(framed, weight):
    side = framed.shape[0] - 2
    width = framed.shape[2]
    total = jnp.zeros((side * side, weight.shape[3]), jnp.float32)
    for a in range(3):
        for b in range(3):
            window = framed[a : a + side, b : b + side].reshape(side * side, width)
            total = total + jnp.dot(window, weight[a, b], preferred_element_type=jnp.float32)
    return total


def kernel_total(framed, delta):
    side = framed.shape[0] - 2
    width = framed.shape[2]
    blocks = []
    for a in range(3):
        for b in range(3):
            window = framed[a : a + side, b : b + side].reshape(side * side, width)
            blocks.append(
                lax.dot_general(
                    window, delta, (((0,), (0,)), ((), ())), preferred_element_type=jnp.float32
                )
            )
    return jnp.stack(blocks).reshape(3, 3, width, delta.shape[1])


def spread(delta, weight, side):
    width = delta.shape[1]
    padded = jnp.pad(delta.reshape(side, side, width), ((2, 2), (2, 2), (0, 0)))
    turned = weight[::-1, ::-1].transpose(0, 1, 3, 2)
    return convolve(padded, turned).reshape(side + 2, side + 2, weight.shape[2])


def collect(framed, own_links, own_corners, near_links, near_corners):
    side = framed.shape[0] - 2
    width = framed.shape[2]
    rims = [framed[0, 1:-1], framed[-1, 1:-1], framed[1:-1, 0], framed[1:-1, -1]]
    rims = [
        jnp.where(own_links[place, 2] == 1, rims[place][::-1], rims[place]) for place in range(4)
    ]
    outer = [framed[0, 0], framed[0, -1], framed[-1, 0], framed[-1, -1]]
    outer = [outer[place] * own_corners[place, 2].astype(jnp.float32) for place in range(4)]
    got_edges, got_corners = trade(
        jnp.stack(rims).astype(jnp.bfloat16), jnp.stack(outer).astype(jnp.bfloat16)
    )
    back_slot = (8 - jnp.arange(9, dtype=jnp.int32))[None, :, None]
    which = jnp.arange(4, dtype=jnp.int32)[:, None, None]
    edge_hits = (
        ((near_links[None, :, :, 0] == back_slot) & (near_links[None, :, :, 1] == which))
        .reshape(4, 36)
        .astype(jnp.bfloat16)
    )
    edge_adds = jnp.dot(
        edge_hits, got_edges.reshape(36, side * width), preferred_element_type=jnp.float32
    ).reshape(4, side, width)
    corner_hits = (
        ((near_corners[None, :, :, 0] == back_slot) & (near_corners[None, :, :, 1] == which))
        .reshape(4, 36)
        .astype(jnp.bfloat16)
    )
    corner_adds = jnp.dot(corner_hits, got_corners, preferred_element_type=jnp.float32)
    interior = framed[1:-1, 1:-1]
    interior = interior.at[0].add(edge_adds[0]).at[-1].add(edge_adds[1])
    interior = interior.at[:, 0].add(edge_adds[2]).at[:, -1].add(edge_adds[3])
    interior = interior.at[0, 0].add(corner_adds[0]).at[0, -1].add(corner_adds[1])
    interior = interior.at[-1, 0].add(corner_adds[2]).at[-1, -1].add(corner_adds[3])
    return interior


def beside_all(table, lat_at, lon_at):
    lat_total = table.shape[0]
    lon_total = table.shape[1]
    lat_steps = jnp.array([k // 3 - 1 for k in range(9)], jnp.int32)
    lon_steps = jnp.array([k % 3 - 1 for k in range(9)], jnp.int32)
    return table[(lat_at + lat_steps) % lat_total, (lon_at + lon_steps) % lon_total]


def shards(field, cotangent, first_weight, second_weight, side_links, corner_links):
    lat_at = lax.axis_index("lat")
    lon_at = lax.axis_index("tile")
    own_links = side_links[lat_at, lon_at]
    own_corners = corner_links[lat_at, lon_at]
    near_links = beside_all(side_links, lat_at, lon_at)
    near_corners = beside_all(corner_links, lat_at, lon_at)
    side = field.shape[0]
    width = field.shape[2]
    first_frame = extend(field, own_links, own_corners)
    first_sum = convolve(first_frame, first_weight)
    hidden = gelu(first_sum).astype(jnp.bfloat16).reshape(side, side, width)
    second_frame = extend(hidden, own_links, own_corners)
    second_sum = convolve(second_frame, second_weight)
    mixed = gelu(second_sum).astype(jnp.bfloat16).reshape(side, side, width)
    upstream = cotangent.reshape(side * side, width).astype(jnp.float32)
    second_delta = (upstream * gelu_slope(second_sum)).astype(jnp.bfloat16)
    second_total = kernel_total(second_frame, second_delta)
    hidden_grad = collect(
        spread(second_delta, second_weight, side), own_links, own_corners, near_links, near_corners
    )
    first_delta = (hidden_grad.reshape(side * side, width) * gelu_slope(first_sum)).astype(
        jnp.bfloat16
    )
    first_total = kernel_total(first_frame, first_delta)
    input_grad = collect(
        spread(first_delta, first_weight, side), own_links, own_corners, near_links, near_corners
    )
    first_total, second_total = lax.psum((first_total, second_total), ("tile", "lat"))
    root = math.sqrt(side * side * lax.axis_size("lat") * lax.axis_size("tile"))
    return (mixed, input_grad.astype(jnp.bfloat16), first_total / root, second_total / root)


def solution(mesh):
    placed = (P("lat", "tile", None), P("lat", "tile", None), P(), P(), P(), P())
    return jax.shard_map(
        shards,
        mesh=mesh,
        in_specs=placed,
        out_specs=(P("lat", "tile", None), P("lat", "tile", None), P(), P()),
        check_vma=False,
    )
```

profile of v0, /device:TPU:1, one launch (start us, length us, event | category | flops | bytes accessed | tf_op | source)
XLA Modules:
  0.0 518.7 jit_solution(12864320272012477805)
XLA Ops:
  30.2 6.3 %collective-permute-start.3 = (bf16[1,3,5,48,256]{4,3,2,1,0:T(8,128)(2,1)S(1)}, bf16[1,3,5,48,256]{4,3,2,1,0:T(8,128)(2,1)S(1)}, u32[]{:S(2)}, u32[]{:S(2)}) collective-permute-start(bf16[1,3,5,48,256]{4,3,2,1,0:T(8,128)(2,1)S(1)} %pad_maximum_fusion.10), channel_id=1, source_target_pairs={{1,0},{2,1},{3,2},{4,3},{5,4},{6,5},{7,6},{0,7},{9,8},{10,9},{11,1... | collective-permute-start | bytes 1105928 | tf_op jit(solution)/shard_map/ppermute | solution.py:18
  44.7 3.4 collective-permute-done.2
  61.2 6.7 %multiply_convert_fusion.1 = (bf16[2304,256]{1,0:T(8,128)(2,1)S(1)}, f32[2304,256]{1,0:T(8,128)}, f32[2304,256]{1,0:T(8,128)}) fusion(f32[2304,256]{1,0:T(8,128)S(1)} %convolution_add_fusion.9, bf16[2304,256]{1,0:T(8,128)(2,1)S(1)} %bitcast.580, bf16[3,3,256,256]{3,2,1,0:T(8,128)(2,1)S(1)} %copy-done.50), kind=kOutput, calls=%fused_computation.55 | convolution fusion | flops 340918272 | bytes 9568256 | tf_op jit(solution)/shard_map/dot_general | solution.py:83
  75.1 3.2 collective-permute-start.5
  124.5 8.0 %fusion.2 = (bf16[2304,256]{1,0:T(8,128)(2,1)S(1)}, f32[2304,256]{1,0:T(8,128)}, f32[2304,256]{1,0:T(8,128)}) fusion(bf16[48,48,256]{2,1,0:T(8,128)(2,1)S(1)} %copy-done.76, f32[2304,256]{1,0:T(8,128)S(1)} %convolution_add_fusion.1, bf16[2304,256]{1,0:T(8,128)(2,1)S(1)} %bitcast.582, bf16[3,3,256,256]{3,2,1,0:T(8,128)(2,1)} %param.45), kind=kOutput, calls=%fused_computation.39 | convolution fusion | flops 343867392 | bytes 10747904 | tf_op jit(solution)/shard_map/dot_general | solution.py:83
  133.8 5.4 %pad_slice_fusion.9 = (bf16[50,50,256]{2,1,0:T(8,128)(2,1)}, bf16[50,50,256]{2,1,0:T(8,128)(2,1)}, bf16[50,50,256]{2,1,0:T(8,128)(2,1)}, bf16[50,50,256]{2,1,0:T...) fusion(bf16[48,48,256]{2,1,0:T(8,128)(2,1)S(1)} %bitcast.545), kind=kLoop, calls=%fused_computation.83 | loop fusion | bytes 12699648 | tf_op jit(solution)/shard_map/slice | solution.py:82
  139.2 3.2 reshape.907
  148.8 3.2 reshape.902
  151.9 3.3 reshape.903
  158.5 3.2 reshape.905
  181.3 3.7 reshape.908
  203.6 5.0 collective-permute-start.9
  226.1 5.0 collective-permute-done.10
  253.5 4.0 fusion.3
  258.7 5.3 %pad_slice_fusion = (bf16[50,50,256]{2,1,0:T(8,128)(2,1)}, bf16[50,50,256]{2,1,0:T(8,128)(2,1)}, bf16[50,50,256]{2,1,0:T(8,128)(2,1)}, bf16[50,50,256]{2,1,0:T(8...) fusion(bf16[48,48,256]{2,1,0:T(8,128)(2,1)S(1)} %bitcast.544), kind=kLoop, calls=%fused_computation.74 | loop fusion | bytes 12699648 | tf_op jit(solution)/shard_map/slice | solution.py:82
  264.0 3.2 reshape.930
  267.2 3.2 reshape.923
  270.4 3.2 reshape.924
  279.9 3.2 reshape.927
  286.3 3.3 reshape.929
  305.9 3.7 reshape.931
  329.5 4.1 collective-permute-start.13
  364.4 142.2 %all-reduce.7.cloned.1.call-done = (f32[3,3,256,256]{3,2,1,0:T(8,128)}, f32[3,3,256,256]{3,2,1,0:T(8,128)}) async-done(((f32[3,3,256,256]{3,2,1,0:T(8,128)}, f32[3,3,256,256]{3,2,1,0:T(8,128)}), (f32[3,3,256,256]{3,2,1,0:T(8,128)}, f32[3,3,256,256]{3,2,1,0:T(8,128)})) %all-reduce.7.cloned.1.call-update) | async-done | bytes 4718608 | tf_op jit(solution)/shard_map/psum | solution.py:181
  506.5 3.4 broadcast_multiply_fusion.1
  (416 shorter events, 247.0 us)
Async XLA Ops:
  7.2 35.6 %copy-start.50 = (bf16[3,3,256,256]{3,2,1,0:T(8,128)(2,1)S(1)}, bf16[3,3,256,256]{3,2,1,0:T(8,128)(2,1)}, u32[]{:S(2)}) copy-start(bf16[3,3,256,256]{3,2,1,0:T(8,128)(2,1)} %param.44) | copy-start | bytes 3538948
  7.2 499.4 %all-reduce.7.cloned.1.call-start = ((), (), s32[]{:S(2)}) async-start(), calls=%async_computation | async-start | bytes 9437184 | tf_op jit(solution)/shard_map/psum | solution.py:181
  11.3 31.5 %copy-start.55 = (bf16[5,48,256]{2,1,0:T(8,128)(2,1)}, bf16[5,48,256]{2,1,0:T(8,128)(2,1)S(1)}, u32[]{:S(2)}) copy-start(bf16[5,48,256]{2,1,0:T(8,128)(2,1)S(1)} %constant_dynamic-update-slice_fusion) | copy-start | bytes 368644
  11.3 18.8 %collective-permute-start.1 = (bf16[1,1,5,48,256]{4,3,2,1,0:T(8,128)(2,1)S(1)}, bf16[1,1,5,48,256]{4,3,2,1,0:T(8,128)(2,1)S(1)}, u32[]{:S(2)}, u32[]{:S(2)}) collective-permute-start(bf16[1,1,5,48,256]{4,3,2,1,0:T(8,128)(2,1)S(1)} %bitcast.603), channel_id=1, source_target_pairs={{8,0},{16,8},{24,16},{32,24},{40,32},{48,40},{56,48},{64,56},{72,6... | collective-permute-start | bytes 368648 | tf_op jit(solution)/shard_map/ppermute | solution.py:18
  12.7 17.4 %collective-permute-start = (bf16[1,1,5,48,256]{4,3,2,1,0:T(8,128)(2,1)S(1)}, bf16[1,1,5,48,256]{4,3,2,1,0:T(8,128)(2,1)S(1)}, u32[]{:S(2)}, u32[]{:S(2)}) collective-permute-start(bf16[1,1,5,48,256]{4,3,2,1,0:T(8,128)(2,1)S(1)} %bitcast.604), channel_id=1, source_target_pairs={{0,8},{8,16},{16,24},{24,32},{32,40},{40,48},{48,56},{56,64},{64,7... | collective-permute-start | bytes 368648 | tf_op jit(solution)/shard_map/ppermute | solution.py:16
  30.1 12.7 %copy-start.58 = (bf16[1,1,5,48,256]{4,3,2,1,0:T(8,128)(2,1)}, bf16[1,1,5,48,256]{4,3,2,1,0:T(8,128)(2,1)S(1)}, u32[]{:S(2)}) copy-start(bf16[1,1,5,48,256]{4,3,2,1,0:T(8,128)(2,1)S(1)} %collective-permute-done.1) | copy-start | bytes 368644
  30.1 12.7 %copy-start.59 = (bf16[1,1,5,48,256]{4,3,2,1,0:T(8,128)(2,1)}, bf16[1,1,5,48,256]{4,3,2,1,0:T(8,128)(2,1)S(1)}, u32[]{:S(2)}) copy-start(bf16[1,1,5,48,256]{4,3,2,1,0:T(8,128)(2,1)S(1)} %collective-permute-done) | copy-start | bytes 368644
  30.2 13.8 %collective-permute-start.3 = (bf16[1,3,5,48,256]{4,3,2,1,0:T(8,128)(2,1)S(1)}, bf16[1,3,5,48,256]{4,3,2,1,0:T(8,128)(2,1)S(1)}, u32[]{:S(2)}, u32[]{:S(2)}) collective-permute-start(bf16[1,3,5,48,256]{4,3,2,1,0:T(8,128)(2,1)S(1)} %pad_maximum_fusion.10), channel_id=1, source_target_pairs={{1,0},{2,1},{3,2},{4,3},{5,4},{6,5},{7,6},{0,7},{9,8},{10,9},{11,1... | collective-permute-start | bytes 1105928 | tf_op jit(solution)/shard_map/ppermute | solution.py:18
  36.4 11.7 %collective-permute-start.2 = (bf16[1,3,5,48,256]{4,3,2,1,0:T(8,128)(2,1)S(1)}, bf16[1,3,5,48,256]{4,3,2,1,0:T(8,128)(2,1)}, u32[]{:S(2)}, u32[]{:S(2)}) collective-permute-start(bf16[1,3,5,48,256]{4,3,2,1,0:T(8,128)(2,1)S(1)} %pad_maximum_fusion.10), channel_id=1, source_target_pairs={{0,1},{1,2},{2,3},{3,4},{4,5},{5,6},{6,7},{7,0},{8,9},{9,10},{10,1... | collective-permute-start | bytes 1105928 | tf_op jit(solution)/shard_map/ppermute | solution.py:16
  67.9 27.1 %copy-start.51 = (bf16[3,3,256,256]{3,2,1,0:T(8,128)(2,1)S(1)}, bf16[3,3,256,256]{3,2,1,0:T(8,128)(2,1)}, u32[]{:S(2)}) copy-start(bf16[3,3,256,256]{3,2,1,0:T(8,128)(2,1)} %param.45) | copy-start | bytes 3538948
  75.1 9.6 %collective-permute-start.5 = (bf16[1,1,5,48,256]{4,3,2,1,0:T(8,128)(2,1)}, bf16[1,1,5,48,256]{4,3,2,1,0:T(8,128)(2,1)}, u32[]{:S(2)}, u32[]{:S(2)}) collective-permute-start(bf16[1,1,5,48,256]{4,3,2,1,0:T(8,128)(2,1)} %bitcast.64), channel_id=1, source_target_pairs={{8,0},{16,8},{24,16},{32,24},{40,32},{48,40},{56,48},{64,56},{72,6... | collective-permute-start | bytes 368648 | tf_op jit(solution)/shard_map/ppermute | solution.py:18
  78.3 6.4 %collective-permute-start.4 = (bf16[1,1,5,48,256]{4,3,2,1,0:T(8,128)(2,1)}, bf16[1,1,5,48,256]{4,3,2,1,0:T(8,128)(2,1)}, u32[]{:S(2)}, u32[]{:S(2)}) collective-permute-start(bf16[1,1,5,48,256]{4,3,2,1,0:T(8,128)(2,1)} %bitcast.64), channel_id=1, source_target_pairs={{0,8},{8,16},{16,24},{24,32},{32,40},{40,48},{48,56},{56,64},{64,7... | collective-permute-start | bytes 368648 | tf_op jit(solution)/shard_map/ppermute | solution.py:16
  86.4 9.7 %collective-permute-start.7 = (bf16[1,3,5,48,256]{4,3,2,1,0:T(8,128)(2,1)}, bf16[1,3,5,48,256]{4,3,2,1,0:T(8,128)(2,1)}, u32[]{:S(2)}, u32[]{:S(2)}) collective-permute-start(bf16[1,3,5,48,256]{4,3,2,1,0:T(8,128)(2,1)} %pad_maximum_fusion.11), channel_id=1, source_target_pairs={{1,0},{2,1},{3,2},{4,3},{5,4},{6,5},{7,6},{0,7},{9,8},{10,9},{11,1... | collective-permute-start | bytes 1105928 | tf_op jit(solution)/shard_map/ppermute | solution.py:18
  87.5 10.7 %collective-permute-start.6 = (bf16[1,3,5,48,256]{4,3,2,1,0:T(8,128)(2,1)}, bf16[1,3,5,48,256]{4,3,2,1,0:T(8,128)(2,1)}, u32[]{:S(2)}, u32[]{:S(2)}) collective-permute-start(bf16[1,3,5,48,256]{4,3,2,1,0:T(8,128)(2,1)} %pad_maximum_fusion.11), channel_id=1, source_target_pairs={{0,1},{1,2},{2,3},{3,4},{4,5},{5,6},{6,7},{7,0},{8,9},{9,10},{10,1... | collective-permute-start | bytes 1105928 | tf_op jit(solution)/shard_map/ppermute | solution.py:16
  197.9 13.3 %copy-start.23 = (bf16[48,48,256]{2,1,0:T(8,128)(2,1)S(1)}, bf16[48,48,256]{2,1,0:T(8,128)(2,1)}, u32[]{:S(2)}) copy-start(bf16[48,48,256]{2,1,0:T(8,128)(2,1)} %copy-done.22) | copy-start | bytes 3538948
  203.6 15.1 %collective-permute-start.9 = (bf16[1,1,5,48,256]{4,3,2,1,0:T(8,128)(2,1)}, bf16[1,1,5,48,256]{4,3,2,1,0:T(8,128)(2,1)S(1)}, u32[]{:S(2)}, u32[]{:S(2)}) collective-permute-start(bf16[1,1,5,48,256]{4,3,2,1,0:T(8,128)(2,1)} %bitcast.611), channel_id=1, source_target_pairs={{8,0},{16,8},{24,16},{32,24},{40,32},{48,40},{56,48},{64,56},{72,6... | collective-permute-start | bytes 368648 | tf_op jit(solution)/shard_map/ppermute | solution.py:18
  208.7 10.0 %collective-permute-start.8 = (bf16[1,1,5,48,256]{4,3,2,1,0:T(8,128)(2,1)}, bf16[1,1,5,48,256]{4,3,2,1,0:T(8,128)(2,1)S(1)}, u32[]{:S(2)}, u32[]{:S(2)}) collective-permute-start(bf16[1,1,5,48,256]{4,3,2,1,0:T(8,128)(2,1)} %bitcast.612), channel_id=1, source_target_pairs={{0,8},{8,16},{16,24},{24,32},{32,40},{40,48},{48,56},{56,64},{64,7... | collective-permute-start | bytes 368648 | tf_op jit(solution)/shard_map/ppermute | solution.py:16
  218.8 7.3 %collective-permute-start.11 = (bf16[1,3,5,48,256]{4,3,2,1,0:T(8,128)(2,1)S(1)}, bf16[1,3,5,48,256]{4,3,2,1,0:T(8,128)(2,1)S(1)}, u32[]{:S(2)}, u32[]{:S(2)}) collective-permute-start(bf16[1,3,5,48,256]{4,3,2,1,0:T(8,128)(2,1)S(1)} %pad_maximum_fusion.12), channel_id=1, source_target_pairs={{1,0},{2,1},{3,2},{4,3},{5,4},{6,5},{7,6},{0,7},{9,8},{10,9},{11,1... | collective-permute-start | bytes 1105928 | tf_op jit(solution)/shard_map/ppermute | solution.py:18
  220.6 10.5 %collective-permute-start.10 = (bf16[1,3,5,48,256]{4,3,2,1,0:T(8,128)(2,1)S(1)}, bf16[1,3,5,48,256]{4,3,2,1,0:T(8,128)(2,1)S(1)}, u32[]{:S(2)}, u32[]{:S(2)}) collective-permute-start(bf16[1,3,5,48,256]{4,3,2,1,0:T(8,128)(2,1)S(1)} %pad_maximum_fusion.12), channel_id=1, source_target_pairs={{0,1},{1,2},{2,3},{3,4},{4,5},{5,6},{6,7},{7,0},{8,9},{9,10},{10,1... | collective-permute-start | bytes 1105928 | tf_op jit(solution)/shard_map/ppermute | solution.py:16
  309.6 26.8 %copy-start.12 = (bf16[48,48,256]{2,1,0:T(8,128)(2,1)S(1)}, bf16[48,48,256]{2,1,0:T(8,128)(2,1)}, u32[]{:S(2)}) copy-start(bf16[48,48,256]{2,1,0:T(8,128)(2,1)} %copy-done.11) | copy-start | bytes 3538948
  329.5 13.0 %collective-permute-start.13 = (bf16[1,1,5,48,256]{4,3,2,1,0:T(8,128)(2,1)}, bf16[1,1,5,48,256]{4,3,2,1,0:T(8,128)(2,1)S(1)}, u32[]{:S(2)}, u32[]{:S(2)}) collective-permute-start(bf16[1,1,5,48,256]{4,3,2,1,0:T(8,128)(2,1)} %bitcast.607), channel_id=1, source_target_pairs={{8,0},{16,8},{24,16},{32,24},{40,32},{48,40},{56,48},{64,56},{72,6... | collective-permute-start | bytes 368648 | tf_op jit(solution)/shard_map/ppermute | solution.py:18
  333.6 8.9 %collective-permute-start.12 = (bf16[1,1,5,48,256]{4,3,2,1,0:T(8,128)(2,1)}, bf16[1,1,5,48,256]{4,3,2,1,0:T(8,128)(2,1)S(1)}, u32[]{:S(2)}, u32[]{:S(2)}) collective-permute-start(bf16[1,1,5,48,256]{4,3,2,1,0:T(8,128)(2,1)} %bitcast.608), channel_id=1, source_target_pairs={{0,8},{8,16},{16,24},{24,32},{32,40},{40,48},{48,56},{56,64},{64,7... | collective-permute-start | bytes 368648 | tf_op jit(solution)/shard_map/ppermute | solution.py:16
  342.6 7.2 %collective-permute-start.15 = (bf16[1,3,5,48,256]{4,3,2,1,0:T(8,128)(2,1)S(1)}, bf16[1,3,5,48,256]{4,3,2,1,0:T(8,128)(2,1)S(1)}, u32[]{:S(2)}, u32[]{:S(2)}) collective-permute-start(bf16[1,3,5,48,256]{4,3,2,1,0:T(8,128)(2,1)S(1)} %pad_maximum_fusion.13), channel_id=1, source_target_pairs={{1,0},{2,1},{3,2},{4,3},{5,4},{6,5},{7,6},{0,7},{9,8},{10,9},{11,1... | collective-permute-start | bytes 1105928 | tf_op jit(solution)/shard_map/ppermute | solution.py:18
  342.6 10.0 %collective-permute-start.14 = (bf16[1,3,5,48,256]{4,3,2,1,0:T(8,128)(2,1)S(1)}, bf16[1,3,5,48,256]{4,3,2,1,0:T(8,128)(2,1)S(1)}, u32[]{:S(2)}, u32[]{:S(2)}) collective-permute-start(bf16[1,3,5,48,256]{4,3,2,1,0:T(8,128)(2,1)S(1)} %pad_maximum_fusion.13), channel_id=1, source_target_pairs={{0,1},{1,2},{2,3},{3,4},{4,5},{5,6},{6,7},{7,0},{8,9},{9,10},{10,1... | collective-permute-start | bytes 1105928 | tf_op jit(solution)/shard_map/ppermute | solution.py:16
  (70 other events, 203.9 us)
Sparse Core Ops, SparseCore 0:
  348.4 158.0 all-reduce.6
where the time goes:
time: 527 us; the launch traced here: 519 us
  local copies, waits for them, and re-layouts  179 us (34%)
  waiting for transfers between devices  158 us (30%)
  matrix products  63.4 us (12%)
  other arithmetic  58 us (11%)
  between operations  33.4 us (6%)
  starting transfers between devices  26.9 us (5%)
    psum x1, waiting for transfers between devices, shards(): lax.psum((first_total, second_total), ('tile', 'lat'))  142 us
    reshape x18, local copies, waits for them, and re-layouts, convolve(): window = framed[a:a + side, b:b + side].reshape(side * side, width)  57.4 us
    dot_general x36, matrix products, convolve(): jnp.dot(window, weight[a, b], preferred_element_type=jnp.float32)  38.1 us
    unnamed x172, local copies, waits for them, and re-layouts  28.2 us
    dot_general x18, matrix products, kernel_total(): lax.dot_general(window, delta, (((0,), (0,)), ((), ())), preferred_elemen...  24.5 us
    ppermute x8, starting transfers between devices, with_halo(): lax.ppermute(head, axis, [((i + 1) % count, i) for i in range(count)])  23 us
    slice x6, local copies, waits for them, and re-layouts, convolve(): window = framed[a:a + side, b:b + side].reshape(side * side, width)  14 us
    ppermute x8, waiting for transfers between devices, with_halo(): lax.ppermute(tail, axis, [(i, (i + 1) % count) for i in range(count)])  13.3 us
  transfers between devices with their start and end apart: 17, of which 7 were waited for; matrix products, arithmetic and copies ran while one was open for 11% of the time, Pallas kernels for 0%

commit v1 on v0

v1 whole, which is shorter than its diff:
```python
import functools
import math

import jax
import jax.numpy as jnp
from jax import lax
from jax.experimental import pallas as pl
from jax.experimental.pallas import tpu as pltpu
from jax.sharding import PartitionSpec as P

S = 48
C = 256
CELLS = S * S
ROWS = 8
BLK = ROWS * S
N_BLK = S // ROWS
PK = 64
F32 = jnp.float32
BF = jnp.bfloat16
MIB = 1 << 20


def side_slot(lk, s):
    return lk[s * 3]


def side_flip(lk, s):
    return lk[s * 3 + 2]


def corner_slot(lk, c):
    return lk[12 + c * 3]


def corner_keep(lk, c):
    return lk[12 + c * 3 + 2]


def side_facing(lk, slot):
    found = jnp.int32(0)
    for s in range(1, 4):
        found = jnp.where(side_slot(lk, s) == slot, jnp.int32(s), found)
    return found


def flip_facing(lk, slot):
    found = side_flip(lk, 0)
    for s in range(1, 4):
        found = jnp.where(side_slot(lk, s) == slot, side_flip(lk, s), found)
    return found


def corner_facing(lk, slot, values):
    found = values[0]
    for c in range(1, 4):
        found = jnp.where(corner_slot(lk, c) == slot, values[c], found)
    return found


def corner_home(lk, c):
    d = corner_slot(lk, c)
    home = jnp.where(d == 0, jnp.int32(S), jnp.int32(S + 1))
    home = jnp.where(d == 6, jnp.int32(3 * PK + S), home)
    return jnp.where(d == 8, jnp.int32(3 * PK + S + 1), home)


def side_home(lk, s):
    return (side_slot(lk, s) - 1) // 2 * PK


def grid_of(rows, cols):
    row = lax.broadcasted_iota(jnp.int32, (rows, cols), 0)
    col = lax.broadcasted_iota(jnp.int32, (rows, cols), 1)
    return row, col


def ones_at(hit):
    return jnp.where(hit, 1.0, 0.0).astype(BF)


def pick(hit, rows):
    return jnp.dot(ones_at(hit), rows, preferred_element_type=F32)


CORNERS_TO_SEND = {1: (0, 6), 2: (2, 8)}


def pack_edges(lk, edges):
    row, col = grid_of(PK, 4 * S)
    at = [jnp.int32(c // 2 * S + c % 2 * (S - 1)) for c in range(4)]
    hits = []
    for q, slot in enumerate((1, 3, 5, 7)):
        want = jnp.where(row < S, side_facing(lk, slot) * S + row, -1)
        if q in CORNERS_TO_SEND:
            for k, far in enumerate(CORNERS_TO_SEND[q]):
                want = jnp.where(row == S + k, corner_facing(lk, far, at), want)
        hits.append(col == want)
    return pick(jnp.concatenate(hits, axis=0), edges).astype(BF)


def pack_rims(lk, rims):
    row, col = grid_of(PK, 4 * PK)
    at = []
    for c in range(4):
        place = jnp.int32(c // 2 * PK + S + c % 2)
        at.append(jnp.where(corner_keep(lk, c) != 0, place, jnp.int32(-1)))
    hits = []
    for q, slot in enumerate((1, 3, 5, 7)):
        cell = jnp.where(flip_facing(lk, slot) == 1, S - 1 - row, row)
        want = jnp.where(row < S, side_facing(lk, slot) * PK + cell, -1)
        if q in CORNERS_TO_SEND:
            for k, far in enumerate(CORNERS_TO_SEND[q]):
                want = jnp.where(row == S + k, corner_facing(lk, far, at), want)
        hits.append(col == want)
    return pick(jnp.concatenate(hits, axis=0), rims).astype(BF)


def halo_rows(lk, got):
    row, col = grid_of(S, 4 * PK)
    sides = []
    for s in range(4):
        taps = []
        for t in range(3):
            at = row + (t - 1)
            cell = jnp.where(side_flip(lk, s) == 1, S - 1 - at, at)
            want = jnp.where((at >= 0) & (at < S), side_home(lk, s) + cell, -1)
            if s < 2:
                for end, c in ((-1, 2 * s), (S, 2 * s + 1)):
                    home = jnp.where(corner_keep(lk, c) != 0, corner_home(lk, c), -1)
                    want = jnp.where(at == end, home, want)
            taps.append(pick(col == want, got).astype(BF))
        sides.append(jnp.concatenate(taps, axis=1))
    return sides


def rim_adds(lk, got):
    row, col = grid_of(S, 4 * PK)
    adds = []
    for s in range(4):
        hit = col == side_home(lk, s) + row
        if s < 2:
            for end, c in ((0, 2 * s), (S - 1, 2 * s + 1)):
                hit = hit | ((row == end) & (col == corner_home(lk, c)))
        adds.append(pick(hit, got))
    return adds


def cross(adds):
    top, bottom, left, right = adds
    row = lax.broadcasted_iota(jnp.int32, (S, C), 0)
    first = row == 0
    last = row == S - 1

    def with_ends(base, head, tail):
        return base + jnp.where(first, head, 0.0) + jnp.where(last, tail, 0.0)

    return [
        with_ends(top, left[0:1], right[0:1]),
        with_ends(bottom, left[S - 1 :], right[S - 1 :]),
        with_ends(left, top[0:1], bottom[0:1]),
        with_ends(right, top[S - 1 :], bottom[S - 1 :]),
    ]


def gelu_both(z):
    phi = 0.5 + 0.5 * lax.erf(z * (1.0 / math.sqrt(2.0)))
    dens = jnp.exp(z * z * -0.5) * (1.0 / math.sqrt(2.0 * math.pi))
    return z * phi, phi + z * dens


def dot(a, b):
    return jnp.dot(a, b, preferred_element_type=F32)


def dot_nt(a, b):
    return lax.dot_general(a, b, (((1,), (1,)), ((), ())), preferred_element_type=F32)


def halo_sums(sides, w):
    out = [dot(sides[0], w[0]), dot(sides[1], w[2])]
    for s, b in ((2, 0), (3, 2)):
        total = None
        for a in range(3):
            term = dot(sides[s][:, a * C : (a + 1) * C], w[a, b * C : (b + 1) * C])
            total = term if total is None else total + term
        out.append(total)
    return cross(out)


def rims_of(edges, w):
    row, col = grid_of(PK, 4 * S)
    out = []
    for s in range(4):
        total = None
        for t in range(3):
            if s < 2:
                pos = jnp.where(row < S, row + 1, jnp.where(row == S, 0, S + 1))
                used = row < S + 2
                a, b = (0, 2)[s], t
            else:
                pos = row + 1
                used = row < S
                a, b = t, (0, 2)[s - 2]
            src = pos - t
            hit = used & (src >= 0) & (src < S) & (col == s * S + src)
            term = dot_nt(pick(hit, edges).astype(BF), w[a, b * C : (b + 1) * C])
            total = term if total is None else total + term
        out.append(total.astype(BF))
    return jnp.concatenate(out, axis=0)


def put_edges(x, edges):
    x[pl.ds(0, S)] = edges[pl.ds(0, S)]
    x[pl.ds(CELLS - S, S)] = edges[pl.ds(S, S)]
    for r in range(S):
        x[pl.ds(r * S, 1)] = edges[pl.ds(2 * S + r, 1)]
        x[pl.ds(r * S + S - 1, 1)] = edges[pl.ds(3 * S + r, 1)]


def take_edges(x, edges):
    edges[pl.ds(0, S)] = x[pl.ds(0, S)]
    edges[pl.ds(S, S)] = x[pl.ds(CELLS - S, S)]
    for r in range(S):
        edges[pl.ds(2 * S + r, 1)] = x[pl.ds(r * S, 1)]
        edges[pl.ds(3 * S + r, 1)] = x[pl.ds(r * S + S - 1, 1)]


def spread_columns(x, frame, left, right):
    zero = jnp.zeros((S, 3 * C), BF)
    frame[pl.ds(0, S)] = zero
    frame[pl.ds(CELLS + S, S)] = zero
    row = lax.broadcasted_iota(jnp.int32, (S, C), 0)

    @pl.loop(0, S, unroll=4)
    def _(r):
        cells = x[pl.ds(pl.multiple_of(r * S, S), S)]
        to = pl.ds(pl.multiple_of(r * S + S, S), S)
        before = jnp.where(row == 0, 0.0, pltpu.roll(cells, 1, 0))
        after = jnp.where(row == S - 1, 0.0, pltpu.roll(cells, S - 1, 0))
        frame[to, left * C : (left + 1) * C] = before.astype(BF)
        frame[to, C : 2 * C] = cells.astype(BF)
        frame[to, right * C : (right + 1) * C] = after.astype(BF)


def block_of(i):
    return pl.ds(pl.multiple_of(i * BLK, BLK), BLK)


def conv_block(frame, w, i):
    total = None
    for a in range(3):
        term = dot(frame[pl.ds(pl.multiple_of(i * BLK + a * S, S), BLK)], w[a])
        total = term if total is None else total + term
    return total


def back_block(frame, w, i):
    total = None
    for a in range(3):
        at = pl.ds(pl.multiple_of(i * BLK + (2 - a) * S, S), BLK)
        for b in range(3):
            part = frame[at, b * C : (b + 1) * C]
            term = dot_nt(part, w[a, b * C : (b + 1) * C])
            total = term if total is None else total + term
    return total


def weight_sums(xt, frame, halo, edges, out):
    side = []
    for s in range(4):
        side.append(
            lax.dot_general(
                halo[s * S : (s + 1) * S],
                edges[s * S : (s + 1) * S],
                (((0,), (0,)), ((), ())),
                preferred_element_type=F32,
            )
        )
    for a in range(3):
        whole = dot(xt[...], frame[pl.ds((2 - a) * S, CELLS)])
        for b in range(3):
            part = whole[:, b * C : (b + 1) * C]
            if a == 0:
                part = part + side[0][b * C : (b + 1) * C]
            if a == 2:
                part = part + side[1][b * C : (b + 1) * C]
            if b == 0:
                part = part + side[2][a * C : (a + 1) * C]
            if b == 2:
                part = part + side[3][a * C : (a + 1) * C]
            out[pl.ds((a * 3 + b) * C, C)] = part.astype(out.dtype)


def k_pack_field(lk, field, pk):
    def edge_column(at):
        lo = at // 16 * 16
        part = field[:, lo : lo + 16, :].astype(F32)
        row = lax.broadcasted_iota(jnp.int32, (S, 16, C), 1)
        return jnp.sum(jnp.where(row == at - lo, part, 0.0), axis=1)

    edges = jnp.concatenate(
        [field[0], field[S - 1], edge_column(0).astype(BF), edge_column(S - 1).astype(BF)],
        axis=0,
    )
    pk[...] = pack_edges(lk, edges)


def k_first(field, w, hidden, slope, e0, xt, x, frame):
    x[...] = field[...].astype(F32)
    spread_columns(x, frame, 0, 2)
    xt[...] = field[...].T

    @pl.loop(0, N_BLK)
    def _(i):
        at = block_of(i)
        z = conv_block(frame, w, i)
        x[at] = z
        value, grad = gelu_both(z)
        hidden[at] = value.astype(BF)
        slope[at] = grad

    take_edges(x, e0)


def join(got):
    return jnp.concatenate([g[...] for g in got], axis=0)


def k_first_edges(lk, up, left, right, down, e0, w, halo, slope, hidden, pk):
    sides = halo_rows(lk, join((up, left, right, down)))
    for s in range(4):
        halo[pl.ds(s * S, S)] = sides[s]
    z = e0[...] + jnp.concatenate(halo_sums(sides, w), axis=0)
    value, grad = gelu_both(z)
    slope[...] = grad
    hidden[...] = value.astype(BF)
    pk[...] = pack_edges(lk, value.astype(BF))


def k_second(hidden0, he, cot, w, xt, mixed, delta, e0, ec, x, frame, edges):
    x[...] = cot[...].astype(F32)
    take_edges(x, ec)
    x[...] = hidden0[...].astype(F32)
    edges[...] = he[...].astype(F32)
    put_edges(x, edges)
    spread_columns(x, frame, 0, 2)
    xt[...] = x[...].astype(BF).T

    @pl.loop(0, N_BLK)
    def _(i):
        at = block_of(i)
        z = conv_block(frame, w, i)
        x[at] = z
        value, grad = gelu_both(z)
        mixed[at] = value.astype(BF)
        delta[at] = (cot[at].astype(F32) * grad).astype(BF)

    take_edges(x, e0)


def k_second_edges(lk, up, left, right, down, e0, ec, w, halo, mixed, delta, pk):
    sides = halo_rows(lk, join((up, left, right, down)))
    for s in range(4):
        halo[pl.ds(s * S, S)] = sides[s]
    z = e0[...] + jnp.concatenate(halo_sums(sides, w), axis=0)
    value, grad = gelu_both(z)
    mixed[...] = value.astype(BF)
    edges = (ec[...] * grad).astype(BF)
    delta[...] = edges
    pk[...] = pack_rims(lk, rims_of(edges, w))


def k_second_back(mixed0, me, delta0, de, w, xt, halo, slope, mixed, total, fd, e0, x, frame, edges):
    x[...] = mixed0[...].astype(F32)
    edges[...] = me[...].astype(F32)
    put_edges(x, edges)
    mixed[...] = x[...].astype(BF)
    x[...] = delta0[...].astype(F32)
    edges[...] = de[...].astype(F32)
    put_edges(x, edges)
    spread_columns(x, frame, 2, 0)

    @pl.loop(0, N_BLK)
    def _(i):
        at = block_of(i)
        g = back_block(frame, w, i)
        x[at] = g
        fd[at] = (g * slope[at]).astype(BF)

    take_edges(x, e0)
    weight_sums(xt, frame, halo, de, total)


def k_first_delta_edges(lk, up, left, right, down, e0, slope, w, delta, pk):
    adds = cross(rim_adds(lk, join((up, left, right, down))))
    grad = e0[...] + jnp.concatenate(adds, axis=0)
    edges = (grad * slope[...]).astype(BF)
    delta[...] = edges
    pk[...] = pack_rims(lk, rims_of(edges, w))


def k_first_total(delta0, de, xt, halo, total, x, frame, edges):
    x[...] = delta0[...].astype(F32)
    edges[...] = de[...].astype(F32)
    put_edges(x, edges)
    spread_columns(x, frame, 2, 0)
    weight_sums(xt, frame, halo, de, total)


def k_input_grad(lk, up, left, right, down, delta0, de, w, out, x, frame, edges):
    x[...] = delta0[...].astype(F32)
    edges[...] = de[...].astype(F32)
    put_edges(x, edges)
    spread_columns(x, frame, 2, 0)

    @pl.loop(0, N_BLK)
    def _(i):
        x[block_of(i)] = back_block(frame, w, i)

    adds = cross(rim_adds(lk, join((up, left, right, down))))
    take_edges(x, edges)
    edges[...] += jnp.concatenate(adds, axis=0)
    put_edges(x, edges)
    out[...] = x[...].astype(BF)


VMEM = pl.BlockSpec(memory_space=pltpu.VMEM)
SMEM = pl.BlockSpec(memory_space=pltpu.SMEM)
WIDE = [pltpu.VMEM((CELLS, C), F32), pltpu.VMEM((CELLS + 2 * S, 3 * C), BF)]
WIDER = WIDE + [pltpu.VMEM((4 * S, C), F32)]


def call(kernel, args, outs, scratch=(), links=None, flops=0):
    given = ([links] if links is not None else []) + list(args)
    specs = ([SMEM] if links is not None else []) + [VMEM] * len(args)
    return pl.pallas_call(
        kernel,
        out_shape=[jax.ShapeDtypeStruct(shape, dtype) for shape, dtype in outs],
        in_specs=specs,
        out_specs=[VMEM] * len(outs),
        scratch_shapes=list(scratch),
        compiler_params=pltpu.CompilerParams(vmem_limit_bytes=40 * MIB),
        cost_estimate=pl.CostEstimate(
            flops=int(flops), bytes_accessed=4 * MIB, transcendentals=0
        ),
        name=kernel.__name__,
    )(*given)


def ring(count, step):
    return [(i, (i + step) % count) for i in range(count)]


def trade(pk):
    n_tile = lax.axis_size("tile")
    n_lat = lax.axis_size("lat")
    up, left, right, down = (pk[q * PK : (q + 1) * PK] for q in range(4))
    from_left = lax.ppermute(right, "tile", ring(n_tile, 1))
    from_right = lax.ppermute(left, "tile", ring(n_tile, -1))
    filler = jnp.zeros((PK - S - 2, C), BF)
    up = jnp.concatenate(
        [up[:S], from_left[S : S + 1], from_right[S : S + 1], filler], axis=0
    )
    down = jnp.concatenate(
        [down[:S], from_left[S + 1 : S + 2], from_right[S + 1 : S + 2], filler], axis=0
    )
    from_up = lax.ppermute(down, "lat", ring(n_lat, 1))
    from_down = lax.ppermute(up, "lat", ring(n_lat, -1))
    return from_up, from_left, from_right, from_down


def group_ring(kind, step):
    pairs = []
    for t in range(16):
        for l in range(8):
            y, xl, c, xh, z = t // 4, t // 2 % 2, t % 2, l // 4, l % 4
            x = xh * 2 + xl
            if kind == "core":
                c = (c + step) % 2
            elif kind == "z":
                z = (z + step) % 4
            elif kind == "y":
                y = (y + step) % 4
            else:
                x = (x + step) % 4
            to = (y * 4 + x % 2 * 2 + c) * 8 + x // 2 * 4 + z
            pairs.append((t * 8 + l, to))
    return pairs


def move(x, kind, step):
    return lax.ppermute(x, ("tile", "lat"), group_ring(kind, step))


def scatter4(x, kind, place):
    k = x.shape[0] // 4
    got = [
        move(lax.dynamic_slice_in_dim(x, (place + s) % 4 * k, k, 0), kind, s) for s in (1, 3, 2)
    ]
    total = lax.dynamic_slice_in_dim(x, place * k, k, 0).astype(F32)
    for g in got:
        total = total + g.astype(F32)
    return total.astype(BF)


def gather4(x, kind, place):
    k = x.shape[0]
    out = jnp.zeros((4 * k, C), x.dtype)
    parts = [(0, x)] + [(s, move(x, kind, 4 - s)) for s in (1, 3, 2)]
    for s, part in parts:
        out = lax.dynamic_update_slice_in_dim(out, part, (place + s) % 4 * k, 0)
    return out


def sum_all(first, second, root):
    tile_at = lax.axis_index("tile")
    lat_at = lax.axis_index("lat")
    core, z_at, y_at = tile_at % 2, lat_at % 4, tile_at // 4
    keep = jnp.where(core == 0, first, second)
    send = jnp.where(core == 0, second, first)
    part = (keep.astype(F32) + move(send, "core", 1).astype(F32)).astype(BF)
    part = scatter4(part, "z", z_at)
    part = scatter4(part, "y", y_at)
    total = part.astype(F32)
    for s in (1, 3, 2):
        total = total + move(part, "x", s).astype(F32)
    part = (total * (1.0 / root)).astype(BF)
    part = gather4(part, "y", y_at)
    part = gather4(part, "z", z_at)
    other = move(part, "core", 1)
    return (
        jnp.where(core == 0, part, other).astype(F32),
        jnp.where(core == 0, other, part).astype(F32),
    )


def shards(field, cotangent, first_weight, second_weight, side_links, corner_links):
    lat_at = lax.axis_index("lat")
    lon_at = lax.axis_index("tile")
    lk = jnp.concatenate(
        [side_links[lat_at, lon_at].reshape(12), corner_links[lat_at, lon_at].reshape(12)]
    )
    w1 = first_weight.reshape(3, 3 * C, C)
    w2 = second_weight.reshape(3, 3 * C, C)
    cells = field.reshape(CELLS, C)
    cot = cotangent.reshape(CELLS, C)
    cell_bf, cell_f32 = ((CELLS, C), BF), ((CELLS, C), F32)
    edge_bf, edge_f32 = ((4 * S, C), BF), ((4 * S, C), F32)
    halo_bf, turned, packs = ((4 * S, 3 * C), BF), ((C, CELLS), BF), ((4 * PK, C), BF)
    work = 2 * CELLS * 9 * C * C

    (pk,) = call(k_pack_field, [field], [packs], links=lk)
    got = trade(pk)
    hidden0, slope0, e0, xt1 = call(
        k_first, [cells, w1], [cell_bf, cell_f32, edge_f32, turned], WIDE, flops=work
    )
    halo1, slope_e, hidden_e, pk = call(
        k_first_edges, [*got, e0, w1], [halo_bf, edge_f32, edge_bf, packs], links=lk
    )
    got = trade(pk)
    xt2, mixed0, delta0, e0, ec = call(
        k_second,
        [hidden0, hidden_e, cot, w2],
        [turned, cell_bf, cell_bf, edge_f32, edge_f32],
        WIDER,
        flops=work,
    )
    halo2, mixed_e, delta_e, pk = call(
        k_second_edges, [*got, e0, ec, w2], [halo_bf, edge_bf, edge_bf, packs], links=lk
    )
    got = trade(pk)
    mixed, total2, fd0, e0 = call(
        k_second_back,
        [mixed0, mixed_e, delta0, delta_e, w2, xt2, halo2, slope0],
        [cell_bf, cell_bf, cell_bf, edge_f32],
        WIDER,
        flops=2 * work,
    )
    fd_e, pk = call(
        k_first_delta_edges, [*got, e0, slope_e, w1], [edge_bf, packs], links=lk
    )
    got = trade(pk)
    (total1,) = call(
        k_first_total, [fd0, fd_e, xt1, halo1], [cell_bf], WIDER, flops=work
    )
    root = math.sqrt(CELLS * lax.axis_size("lat") * lax.axis_size("tile"))
    first, second = sum_all(total1, total2, root)
    (grad,) = call(
        k_input_grad, [*got, fd0, fd_e, w1], [cell_bf], WIDER, links=lk, flops=work
    )
    return (
        mixed.reshape(S, S, C),
        grad.reshape(S, S, C),
        first.reshape(3, 3, C, C),
        second.reshape(3, 3, C, C),
    )


def solution(mesh):
    placed = (P("lat", "tile", None), P("lat", "tile", None), P(), P(), P(), P())
    return jax.shard_map(
        shards,
        mesh=mesh,
        in_specs=placed,
        out_specs=(P("lat", "tile", None), P("lat", "tile", None), P(), P()),
        check_vma=False,
    )
```

time: 527 us -> 167 us (0.32); the launches traced: 519 us -> 166 us
  local copies, waits for them, and re-layouts: 179 us -> 10.7 us
  waiting for transfers between devices: 158 us -> 51.2 us
  matrix products: 63.4 us -> 0 us
  other arithmetic: 58 us -> 7.9 us
  Pallas kernels: 0 us -> 37.1 us
  between operations: 33.4 us -> 1.09 us
  starting transfers between devices: 26.9 us -> 58 us
    psum x1 -> x0, waiting for transfers between devices: 142 us -> none  [shards(): lax.psum((first_total, second_total), ('tile', 'lat'))]
    reshape x20 -> x0, local copies, waits for them, and re-layouts: 64.8 us -> none  [the longest x18 57.4 us: convolve(): window = framed[a:a + side, b:b + side].reshape(side * side, width)]
    dot_general x58 -> x0, matrix products: 63.4 us -> none  [the longest x36 38.1 us: convolve(): jnp.dot(window, weight[a, b], preferred_element_type=jnp.float32)]
    pallas_call x0 -> x9, Pallas kernels: none -> 37.1 us  [call(): pl.pallas_call(kernel, out_shape=[jax.ShapeDtypeStruct(shape, dtype) for...]
    ppermute x16 -> x33, waiting for transfers between devices: 16.1 us -> 51.2 us  [the longest x17 39.3 us: move(): return lax.ppermute(x, ('tile', 'lat'), group_ring(kind, step))]
    ppermute x16 -> x33, starting transfers between devices: 26.9 us -> 58 us  [the longest x17 22.4 us: move(): return lax.ppermute(x, ('tile', 'lat'), group_ring(kind, step))]
    slice x26 -> x16, local copies, waits for them, and re-layouts: 28.9 us -> 0.09 us  [the longest x4 0.03 us: trade(): up, left, right, down = (pk[q * PK:(q + 1) * PK] for q in range(4))]
    unnamed x172 -> x34, local copies, waits for them, and re-layouts: 28.2 us -> 8.95 us
  transfers between devices with their start and end apart: 17 -> 33, of which waited for: 7 -> 18; matrix products, arithmetic and copies ran while one was open for 11% -> 0% of each run, Pallas kernels for 0% -> 16%
where the time goes in v1:
time: 167 us; the launch traced here: 166 us
  starting transfers between devices  58 us (35%)
  waiting for transfers between devices  51.2 us (31%)
  Pallas kernels  37.1 us (22%)
  local copies, waits for them, and re-layouts  10.7 us (6%)
  other arithmetic  7.9 us (5%)
    ppermute x17, waiting for transfers between devices, move(): return lax.ppermute(x, ('tile', 'lat'), group_ring(kind, step))  39.3 us
    pallas_call x9, Pallas kernels, call(): pl.pallas_call(kernel, out_shape=[jax.ShapeDtypeStruct(shape, dtype) for...  37.1 us
    ppermute x17, starting transfers between devices, move(): return lax.ppermute(x, ('tile', 'lat'), group_ring(kind, step))  22.4 us
    ppermute x4, starting transfers between devices, trade(): from_down = lax.ppermute(up, 'lat', ring(n_lat, -1))  19.6 us
    ppermute x4, starting transfers between devices, trade(): from_left = lax.ppermute(right, 'tile', ring(n_tile, 1))  9.23 us
    unnamed x34, local copies, waits for them, and re-layouts  8.95 us
    ppermute x4, waiting for transfers between devices, trade(): from_right = lax.ppermute(left, 'tile', ring(n_tile, -1))  8.36 us
    ppermute x4, starting transfers between devices, trade(): from_right = lax.ppermute(left, 'tile', ring(n_tile, -1))  4.91 us
  transfers between devices with their start and end apart: 33, of which 18 were waited for; matrix products, arithmetic and copies ran while one was open for 0% of the time, Pallas kernels for 16%

profile of v1, /device:TPU:1, one launch (start us, length us, event | category | flops | bytes accessed | tf_op | source)
XLA Modules:
  0.0 166.0 jit_solution(7163065985488579457)
XLA Ops:
  4.3 2.7 %collective-permute-start = (bf16[64,256]{1,0:T(8,128)(2,1)S(1)}, bf16[64,256]{1,0:T(8,128)(2,1)S(1)}, u32[]{:S(2)}, u32[]{:S(2)}) collective-permute-start(bf16[64,256]{1,0:T(8,128)(2,1)S(1)} %get-tuple-element.74), channel_id=1, source_target_pairs={{0,8},{8,16},{16,24},{24,32},{32,40},{40,48},{48,56},{56,64},{64,7... | collective-permute-start | bytes 98312 | tf_op jit(solution)/shard_map/ppermute | solution.py:458
  8.0 2.6 %collective-permute-done.1.right = bf16[64,256]{1,0:T(8,128)(2,1)S(1)} collective-permute-done((bf16[64,256]{1,0:T(8,128)(2,1)S(1)}, bf16[64,256]{1,0:T(8,128)(2,1)S(1)}, u32[]{:S(2)}, u32[]{:S(2)}) %collective-permute-start.1) | collective-permute-done | bytes 32800 | tf_op jit(solution)/shard_map/ppermute | solution.py:459
  12.4 4.4 %collective-permute-start.3 = (bf16[64,256]{1,0:T(8,128)(2,1)S(1)}, bf16[64,256]{1,0:T(8,128)(2,1)S(1)}, u32[]{:S(2)}, u32[]{:S(2)}) collective-permute-start(bf16[64,256]{1,0:T(8,128)(2,1)S(1)} %get-tuple-element.98), channel_id=1, source_target_pairs={{0,7},{1,0},{2,1},{3,2},{4,3},{5,4},{6,5},{7,6},{8,15},{9,8},{10,9... | collective-permute-start | bytes 98312 | tf_op jit(solution)/shard_map/ppermute | solution.py:468
  16.8 5.4 %k_first.1 = (bf16[2304,256]{1,0:T(8,128)(2,1)S(1)}, f32[2304,256]{1,0:T(8,128)S(1)}, f32[192,256]{1,0:T(8,128)S(1)}, bf16[256,2304]{1,0:T(8,128)(2,1)S(1)}) custom-call(bf16[2304,256]{1,0:T(8,128)(2,1)S(1)} %bitcast.14, bf16[3,768,256]{2,1,0:T(8,128)(2,1)S(1)} %bitcast.10), custom_call_target="tpu_custom_call" | custom-call | flops 2717908992 | bytes 4194304 | tf_op jit(solution)/shard_map/k_first/pallas_call | solution.py:436
  31.0 5.1 %collective-permute-start.7 = (bf16[64,256]{1,0:T(8,128)(2,1)S(1)}, bf16[64,256]{1,0:T(8,128)(2,1)S(1)}, u32[]{:S(2)}, u32[]{:S(2)}) collective-permute-start(bf16[64,256]{1,0:T(8,128)(2,1)S(1)} %get-tuple-element.96), channel_id=1, source_target_pairs={{0,7},{1,0},{2,1},{3,2},{4,3},{5,4},{6,5},{7,6},{8,15},{9,8},{10,9... | collective-permute-start | bytes 98312 | tf_op jit(solution)/shard_map/ppermute | solution.py:468
  38.6 5.7 %k_second.1 = (bf16[256,2304]{1,0:T(8,128)(2,1)S(1)}, bf16[2304,256]{1,0:T(8,128)(2,1)S(1)}, bf16[2304,256]{1,0:T(8,128)(2,1)S(1)}, f32[192,256]{1,0:T(8,128)S(1)}, f32[192,256]{1,0:T(8,128)S(1)}) custom-call(bf16[2304,256]{1,0:T(8,128)(2,1)S(1)} %copy-done.15, bf16[192,256]{1,0:T(8,128)(2,1)S(1)} %get-tuple-element.29.he, bf16[2304,256]{1,0:T(8,128)(2,1)S(1)} %bitcast.18, ...), custom_call_target="tpu_custom_call" | custom-call | flops 2717908992 | bytes 4194304 | tf_op jit(solution)/shard_map/k_second/pallas_call | solution.py:436
  44.4 2.4 %k_second_edges.1 = (bf16[192,768]{1,0:T(8,128)(2,1)S(1)}, bf16[192,256]{1,0:T(8,128)(2,1)S(1)}, bf16[192,256]{1,0:T(8,128)(2,1)S(1)}, bf16[256,256]{1,0:T(8,128)(2,1)S(1)}) custom-call(s32[24]{0:T(128)S(1)} %pad_add_fusion.lk, bf16[64,256]{1,0:T(8,128)(2,1)S(1)} %collective-permute-done.6.up, bf16[64,256]{1,0:T(8,128)(2,1)S(1)} %collective-permute-done.4.left, ...), custom_call_target="tpu_custom_call" | custom-call | bytes 4194304 | tf_op jit(solution)/shard_map/k_second_edges/pallas_call | solution.py:436
  47.3 3.4 %collective-permute-start.9 = (bf16[64,256]{1,0:T(8,128)(2,1)S(1)}, bf16[64,256]{1,0:T(8,128)(2,1)S(1)}, u32[]{:S(2)}, u32[]{:S(2)}) collective-permute-start(bf16[64,256]{1,0:T(8,128)(2,1)S(1)} %get-tuple-element.67), channel_id=1, source_target_pairs={{0,120},{8,0},{16,8},{24,16},{32,24},{40,32},{48,40},{56,48},{64,5... | collective-permute-start | bytes 98312 | tf_op jit(solution)/shard_map/ppermute | solution.py:459
  52.4 5.1 %collective-permute-start.11 = (bf16[64,256]{1,0:T(8,128)(2,1)S(1)}, bf16[64,256]{1,0:T(8,128)(2,1)S(1)}, u32[]{:S(2)}, u32[]{:S(2)}) collective-permute-start(bf16[64,256]{1,0:T(8,128)(2,1)S(1)} %get-tuple-element.94), channel_id=1, source_target_pairs={{0,7},{1,0},{2,1},{3,2},{4,3},{5,4},{6,5},{7,6},{8,15},{9,8},{10,9... | collective-permute-start | bytes 98312 | tf_op jit(solution)/shard_map/ppermute | solution.py:468
  57.5 8.4 %k_second_back.1 = (bf16[2304,256]{1,0:T(8,128)(2,1)}, bf16[2304,256]{1,0:T(8,128)(2,1)S(1)}, bf16[2304,256]{1,0:T(8,128)(2,1)S(1)}, f32[192,256]{1,0:T(8,128)S(1)}) custom-call(bf16[2304,256]{1,0:T(8,128)(2,1)S(1)} %get-tuple-element.30.mixed0, bf16[192,256]{1,0:T(8,128)(2,1)S(1)} %get-tuple-element.34.me, bf16[2304,256]{1,0:T(8,128)(2,1)S(1)} %get-tuple-element.35.delta0, ...), custom_call_target="tpu_custom_call" | custom-call | flops 5435817984 | bytes 4194304 | tf_op jit(solution)/shard_map/k_second_back/pallas_call | solution.py:436
  68.5 4.2 %k_first_total.1 = bf16[2304,256]{1,0:T(8,128)(2,1)S(1)} custom-call(bf16[2304,256]{1,0:T(8,128)(2,1)S(1)} %get-tuple-element.45.delta0, bf16[192,256]{1,0:T(8,128)(2,1)S(1)} %get-tuple-element.46.de, bf16[256,2304]{1,0:T(8,128)(2,1)S(1)} %copy-done.13, bf16[192,768]{1,0:T(8,128)(2,1)S(1)} %get-tuple-element.48.halo), custom_call_target="tpu_custom_call" | custom-call | flops 2717908992 | bytes 4194304 | tf_op jit(solution)/shard_map/k_first_total/pallas_call | solution.py:436
  73.9 4.8 %collective-permute-start.16 = (bf16[2304,256]{1,0:T(8,128)(2,1)}, bf16[2304,256]{1,0:T(8,128)(2,1)}, u32[]{:S(2)}, u32[]{:S(2)}) collective-permute-start(bf16[2304,256]{1,0:T(8,128)(2,1)} %broadcast_select_fusion.2), channel_id=1, source_target_pairs={{0,8},{1,9},{2,10},{3,11},{4,12},{5,13},{6,14},{7,15},{8,0},{9,1},... | collective-permute-start | bytes 3538952 | tf_op jit(solution)/shard_map/ppermute | solution.py:492
  78.7 2.8 %collective-permute-done.16 = bf16[2304,256]{1,0:T(8,128)(2,1)} collective-permute-done((bf16[2304,256]{1,0:T(8,128)(2,1)}, bf16[2304,256]{1,0:T(8,128)(2,1)}, u32[]{:S(2)}, u32[]{:S(2)}) %collective-permute-start.16) | collective-permute-done | bytes 1179680 | tf_op jit(solution)/shard_map/ppermute | solution.py:492
  84.4 2.7 %collective-permute-start.18 = (bf16[576,256]{1,0:T(8,128)(2,1)S(1)}, bf16[576,256]{1,0:T(8,128)(2,1)S(1)}, u32[]{:S(2)}, u32[]{:S(2)}) collective-permute-start(bf16[576,256]{1,0:T(8,128)(2,1)S(1)} %get-tuple-element.56), channel_id=1, source_target_pairs={{0,3},{1,0},{2,1},{3,2},{4,7},{5,4},{6,5},{7,6},{8,11},{9,8},{10,9... | collective-permute-start | bytes 884744 | tf_op jit(solution)/shard_map/ppermute | solution.py:492
  87.0 13.1 %collective-permute-done.17 = bf16[576,256]{1,0:T(8,128)(2,1)S(1)} collective-permute-done((bf16[576,256]{1,0:T(8,128)(2,1)S(1)}, bf16[576,256]{1,0:T(8,128)(2,1)S(1)}, u32[]{:S(2)}, u32[]{:S(2)}) %collective-permute-start.17) | collective-permute-done | bytes 294944 | tf_op jit(solution)/shard_map/ppermute | solution.py:492
  101.4 2.7 %collective-permute-start.21 = (bf16[144,256]{1,0:T(8,128)(2,1)S(1)}, bf16[144,256]{1,0:T(8,128)(2,1)S(1)}, u32[]{:S(2)}, u32[]{:S(2)}) collective-permute-start(bf16[144,256]{1,0:T(8,128)(2,1)S(1)} %get-tuple-element.59), channel_id=1, source_target_pairs={{0,96},{1,97},{2,98},{3,99},{4,100},{5,101},{6,102},{7,103},{8,104... | collective-permute-start | bytes 221192 | tf_op jit(solution)/shard_map/ppermute | solution.py:492
  105.8 3.0 %collective-permute-done.22 = bf16[144,256]{1,0:T(8,128)(2,1)S(1)} collective-permute-done((bf16[144,256]{1,0:T(8,128)(2,1)S(1)}, bf16[144,256]{1,0:T(8,128)(2,1)S(1)}, u32[]{:S(2)}, u32[]{:S(2)}) %collective-permute-start.22) | collective-permute-done | bytes 73760 | tf_op jit(solution)/shard_map/ppermute | solution.py:492
  113.3 3.8 %collective-permute-done.25 = bf16[144,256]{1,0:T(8,128)(2,1)S(1)} collective-permute-done((bf16[144,256]{1,0:T(8,128)(2,1)S(1)}, bf16[144,256]{1,0:T(8,128)(2,1)S(1)}, u32[]{:S(2)}, u32[]{:S(2)}) %collective-permute-start.25) | collective-permute-done | bytes 73760 | tf_op jit(solution)/shard_map/ppermute | solution.py:492
  125.5 6.0 %collective-permute-start.12 = (bf16[64,256]{1,0:T(8,128)(2,1)S(1)}, bf16[64,256]{1,0:T(8,128)(2,1)S(1)}, u32[]{:S(2)}, u32[]{:S(2)}) collective-permute-start(bf16[64,256]{1,0:T(8,128)(2,1)S(1)} %get-tuple-element.62), channel_id=1, source_target_pairs={{0,8},{8,16},{16,24},{24,32},{32,40},{40,48},{48,56},{56,64},{64,7... | collective-permute-start | bytes 98312 | tf_op jit(solution)/shard_map/ppermute | solution.py:458
  133.0 9.1 %collective-permute-done.31 = bf16[576,256]{1,0:T(8,128)(2,1)S(1)} collective-permute-done((bf16[576,256]{1,0:T(8,128)(2,1)S(1)}, bf16[576,256]{1,0:T(8,128)(2,1)S(1)}, u32[]{:S(2)}, u32[]{:S(2)}) %collective-permute-start.31) | collective-permute-done | bytes 294944 | tf_op jit(solution)/shard_map/ppermute | solution.py:492
  142.1 3.9 %collective-permute-start.32 = (bf16[2304,256]{1,0:T(8,128)(2,1)S(1)}, bf16[2304,256]{1,0:T(8,128)(2,1)S(1)}, u32[]{:S(2)}, u32[]{:S(2)}) collective-permute-start(bf16[2304,256]{1,0:T(8,128)(2,1)S(1)} %constant_dynamic-update-slice_fusion), channel_id=1, source_target_pairs={{0,8},{1,9},{2,10},{3,11},{4,12},{5,13},{6,14},{7,15},{8,0},{9,1},... | collective-permute-start | bytes 3538952 | tf_op jit(solution)/shard_map/ppermute | solution.py:492
  146.1 3.2 %collective-permute-done.13.right = bf16[64,256]{1,0:T(8,128)(2,1)S(1)} collective-permute-done((bf16[64,256]{1,0:T(8,128)(2,1)S(1)}, bf16[64,256]{1,0:T(8,128)(2,1)S(1)}, u32[]{:S(2)}, u32[]{:S(2)}) %collective-permute-start.13) | collective-permute-done | bytes 32800 | tf_op jit(solution)/shard_map/ppermute | solution.py:459
  149.6 5.1 %collective-permute-start.15 = (bf16[64,256]{1,0:T(8,128)(2,1)S(1)}, bf16[64,256]{1,0:T(8,128)(2,1)S(1)}, u32[]{:S(2)}, u32[]{:S(2)}) collective-permute-start(bf16[64,256]{1,0:T(8,128)(2,1)S(1)} %get-tuple-element.92), channel_id=1, source_target_pairs={{0,7},{1,0},{2,1},{3,2},{4,3},{5,4},{6,5},{7,6},{8,15},{9,8},{10,9... | collective-permute-start | bytes 98312 | tf_op jit(solution)/shard_map/ppermute | solution.py:468
  155.9 6.6 %k_input_grad.1 = bf16[2304,256]{1,0:T(8,128)(2,1)} custom-call(s32[24]{0:T(128)S(1)} %pad_add_fusion.lk, bf16[64,256]{1,0:T(8,128)(2,1)S(1)} %collective-permute-done.14.up, bf16[64,256]{1,0:T(8,128)(2,1)S(1)} %collective-permute-done.12.left, bf16[64,256]{1,0:T(8,128)(2,1)S(1)} %collective-permute-done.13.right, ...), custom_call_target="tpu_custom_call" | custom-call | flops 2717908992 | bytes 4194304 | tf_op jit(solution)/shard_map/k_input_grad/pallas_call | solution.py:436
  (132 shorter events, 48.8 us)
Async XLA Ops:
  10.7 14.9 %collective-permute-start.2 = (bf16[64,256]{1,0:T(8,128)(2,1)S(1)}, bf16[64,256]{1,0:T(8,128)(2,1)S(1)}, u32[]{:S(2)}, u32[]{:S(2)}) collective-permute-start(bf16[64,256]{1,0:T(8,128)(2,1)S(1)} %get-tuple-element.99), channel_id=1, source_target_pairs={{0,1},{1,2},{2,3},{3,4},{4,5},{5,6},{6,7},{7,0},{8,9},{9,10},{10,1... | collective-permute-start | bytes 98312 | tf_op jit(solution)/shard_map/ppermute | solution.py:467
  12.4 13.2 %collective-permute-start.3 = (bf16[64,256]{1,0:T(8,128)(2,1)S(1)}, bf16[64,256]{1,0:T(8,128)(2,1)S(1)}, u32[]{:S(2)}, u32[]{:S(2)}) collective-permute-start(bf16[64,256]{1,0:T(8,128)(2,1)S(1)} %get-tuple-element.98), channel_id=1, source_target_pairs={{0,7},{1,0},{2,1},{3,2},{4,3},{5,4},{6,5},{7,6},{8,15},{9,8},{10,9... | collective-permute-start | bytes 98312 | tf_op jit(solution)/shard_map/ppermute | solution.py:468
  30.9 13.4 %collective-permute-start.6 = (bf16[64,256]{1,0:T(8,128)(2,1)S(1)}, bf16[64,256]{1,0:T(8,128)(2,1)S(1)}, u32[]{:S(2)}, u32[]{:S(2)}) collective-permute-start(bf16[64,256]{1,0:T(8,128)(2,1)S(1)} %get-tuple-element.97), channel_id=1, source_target_pairs={{0,1},{1,2},{2,3},{3,4},{4,5},{5,6},{6,7},{7,0},{8,9},{9,10},{10,1... | collective-permute-start | bytes 98312 | tf_op jit(solution)/shard_map/ppermute | solution.py:467
  31.0 13.4 %collective-permute-start.7 = (bf16[64,256]{1,0:T(8,128)(2,1)S(1)}, bf16[64,256]{1,0:T(8,128)(2,1)S(1)}, u32[]{:S(2)}, u32[]{:S(2)}) collective-permute-start(bf16[64,256]{1,0:T(8,128)(2,1)S(1)} %get-tuple-element.96), channel_id=1, source_target_pairs={{0,7},{1,0},{2,1},{3,2},{4,3},{5,4},{6,5},{7,6},{8,15},{9,8},{10,9... | collective-permute-start | bytes 98312 | tf_op jit(solution)/shard_map/ppermute | solution.py:468
  46.8 4.6 %collective-permute-start.8 = (bf16[64,256]{1,0:T(8,128)(2,1)S(1)}, bf16[64,256]{1,0:T(8,128)(2,1)S(1)}, u32[]{:S(2)}, u32[]{:S(2)}) collective-permute-start(bf16[64,256]{1,0:T(8,128)(2,1)S(1)} %get-tuple-element.66), channel_id=1, source_target_pairs={{0,8},{8,16},{16,24},{24,32},{32,40},{40,48},{48,56},{56,64},{64,7... | collective-permute-start | bytes 98312 | tf_op jit(solution)/shard_map/ppermute | solution.py:458
  47.3 4.9 %collective-permute-start.9 = (bf16[64,256]{1,0:T(8,128)(2,1)S(1)}, bf16[64,256]{1,0:T(8,128)(2,1)S(1)}, u32[]{:S(2)}, u32[]{:S(2)}) collective-permute-start(bf16[64,256]{1,0:T(8,128)(2,1)S(1)} %get-tuple-element.67), channel_id=1, source_target_pairs={{0,120},{8,0},{16,8},{24,16},{32,24},{40,32},{48,40},{56,48},{64,5... | collective-permute-start | bytes 98312 | tf_op jit(solution)/shard_map/ppermute | solution.py:459
  52.3 13.6 %collective-permute-start.10 = (bf16[64,256]{1,0:T(8,128)(2,1)S(1)}, bf16[64,256]{1,0:T(8,128)(2,1)S(1)}, u32[]{:S(2)}, u32[]{:S(2)}) collective-permute-start(bf16[64,256]{1,0:T(8,128)(2,1)S(1)} %get-tuple-element.95), channel_id=1, source_target_pairs={{0,1},{1,2},{2,3},{3,4},{4,5},{5,6},{6,7},{7,0},{8,9},{9,10},{10,1... | collective-permute-start | bytes 98312 | tf_op jit(solution)/shard_map/ppermute | solution.py:467
  52.4 13.6 %collective-permute-start.11 = (bf16[64,256]{1,0:T(8,128)(2,1)S(1)}, bf16[64,256]{1,0:T(8,128)(2,1)S(1)}, u32[]{:S(2)}, u32[]{:S(2)}) collective-permute-start(bf16[64,256]{1,0:T(8,128)(2,1)S(1)} %get-tuple-element.94), channel_id=1, source_target_pairs={{0,7},{1,0},{2,1},{3,2},{4,3},{5,4},{6,5},{7,6},{8,15},{9,8},{10,9... | collective-permute-start | bytes 98312 | tf_op jit(solution)/shard_map/ppermute | solution.py:468
  73.9 7.6 %collective-permute-start.16 = (bf16[2304,256]{1,0:T(8,128)(2,1)}, bf16[2304,256]{1,0:T(8,128)(2,1)}, u32[]{:S(2)}, u32[]{:S(2)}) collective-permute-start(bf16[2304,256]{1,0:T(8,128)(2,1)} %broadcast_select_fusion.2), channel_id=1, source_target_pairs={{0,8},{1,9},{2,10},{3,11},{4,12},{5,13},{6,14},{7,15},{8,0},{9,1},... | collective-permute-start | bytes 3538952 | tf_op jit(solution)/shard_map/ppermute | solution.py:492
  84.3 15.8 %collective-permute-start.17 = (bf16[576,256]{1,0:T(8,128)(2,1)S(1)}, bf16[576,256]{1,0:T(8,128)(2,1)S(1)}, u32[]{:S(2)}, u32[]{:S(2)}) collective-permute-start(bf16[576,256]{1,0:T(8,128)(2,1)S(1)} %get-tuple-element.54), channel_id=1, source_target_pairs={{0,1},{1,2},{2,3},{3,0},{4,5},{5,6},{6,7},{7,4},{8,9},{9,10},{10,1... | collective-permute-start | bytes 884744 | tf_op jit(solution)/shard_map/ppermute | solution.py:492
  84.4 15.7 %collective-permute-start.18 = (bf16[576,256]{1,0:T(8,128)(2,1)S(1)}, bf16[576,256]{1,0:T(8,128)(2,1)S(1)}, u32[]{:S(2)}, u32[]{:S(2)}) collective-permute-start(bf16[576,256]{1,0:T(8,128)(2,1)S(1)} %get-tuple-element.56), channel_id=1, source_target_pairs={{0,3},{1,0},{2,1},{3,2},{4,7},{5,4},{6,5},{7,6},{8,11},{9,8},{10,9... | collective-permute-start | bytes 884744 | tf_op jit(solution)/shard_map/ppermute | solution.py:492
  87.0 13.1 %collective-permute-start.19 = (bf16[576,256]{1,0:T(8,128)(2,1)S(1)}, bf16[576,256]{1,0:T(8,128)(2,1)S(1)}, u32[]{:S(2)}, u32[]{:S(2)}) collective-permute-start(bf16[576,256]{1,0:T(8,128)(2,1)S(1)} %get-tuple-element.55), channel_id=1, source_target_pairs={{0,2},{1,3},{2,0},{3,1},{4,6},{5,7},{6,4},{7,5},{8,10},{9,11},{10,... | collective-permute-start | bytes 884744 | tf_op jit(solution)/shard_map/ppermute | solution.py:492
  101.3 4.5 %collective-permute-start.20 = (bf16[144,256]{1,0:T(8,128)(2,1)S(1)}, bf16[144,256]{1,0:T(8,128)(2,1)S(1)}, u32[]{:S(2)}, u32[]{:S(2)}) collective-permute-start(bf16[144,256]{1,0:T(8,128)(2,1)S(1)} %get-tuple-element.57), channel_id=1, source_target_pairs={{0,32},{1,33},{2,34},{3,35},{4,36},{5,37},{6,38},{7,39},{8,40},{9,... | collective-permute-start | bytes 221192 | tf_op jit(solution)/shard_map/ppermute | solution.py:492
  104.0 4.7 %collective-permute-start.22 = (bf16[144,256]{1,0:T(8,128)(2,1)S(1)}, bf16[144,256]{1,0:T(8,128)(2,1)S(1)}, u32[]{:S(2)}, u32[]{:S(2)}) collective-permute-start(bf16[144,256]{1,0:T(8,128)(2,1)S(1)} %get-tuple-element.58), channel_id=1, source_target_pairs={{0,64},{1,65},{2,66},{3,67},{4,68},{5,69},{6,70},{7,71},{8,72},{9,... | collective-permute-start | bytes 221192 | tf_op jit(solution)/shard_map/ppermute | solution.py:492
  108.8 4.5 %collective-permute-start.23 = (bf16[144,256]{1,0:T(8,128)(2,1)S(1)}, bf16[144,256]{1,0:T(8,128)(2,1)S(1)}, u32[]{:S(2)}, u32[]{:S(2)}) collective-permute-start(bf16[144,256]{1,0:T(8,128)(2,1)S(1)} %add_convert_fusion.2), channel_id=1, source_target_pairs={{0,16},{1,17},{2,18},{3,19},{4,20},{5,21},{6,22},{7,23},{8,24},{9,... | collective-permute-start | bytes 221192 | tf_op jit(solution)/shard_map/ppermute | solution.py:492
  111.5 5.6 %collective-permute-start.25 = (bf16[144,256]{1,0:T(8,128)(2,1)S(1)}, bf16[144,256]{1,0:T(8,128)(2,1)S(1)}, u32[]{:S(2)}, u32[]{:S(2)}) collective-permute-start(bf16[144,256]{1,0:T(8,128)(2,1)S(1)} %add_convert_fusion.2), channel_id=1, source_target_pairs={{0,4},{1,5},{2,6},{3,7},{4,0},{5,1},{6,2},{7,3},{8,12},{9,13},{10,... | collective-permute-start | bytes 221192 | tf_op jit(solution)/shard_map/ppermute | solution.py:492
  118.7 4.7 %collective-permute-start.28 = (bf16[144,256]{1,0:T(8,128)(2,1)S(1)}, bf16[144,256]{1,0:T(8,128)(2,1)S(1)}, u32[]{:S(2)}, u32[]{:S(2)}) collective-permute-start(bf16[144,256]{1,0:T(8,128)(2,1)S(1)} %get-tuple-element.51), channel_id=1, source_target_pairs={{0,64},{1,65},{2,66},{3,67},{4,68},{5,69},{6,70},{7,71},{8,72},{9,... | collective-permute-start | bytes 221192 | tf_op jit(solution)/shard_map/ppermute | solution.py:492
  123.4 9.4 %collective-permute-start.29 = (bf16[576,256]{1,0:T(8,128)(2,1)S(1)}, bf16[576,256]{1,0:T(8,128)(2,1)S(1)}, u32[]{:S(2)}, u32[]{:S(2)}) collective-permute-start(bf16[576,256]{1,0:T(8,128)(2,1)S(1)} %constant_dynamic-update-slice_fusion.4), channel_id=1, source_target_pairs={{0,3},{1,0},{2,1},{3,2},{4,7},{5,4},{6,5},{7,6},{8,11},{9,8},{10,9... | collective-permute-start | bytes 884744 | tf_op jit(solution)/shard_map/ppermute | solution.py:492
  125.5 7.4 %collective-permute-start.30 = (bf16[576,256]{1,0:T(8,128)(2,1)S(1)}, bf16[576,256]{1,0:T(8,128)(2,1)S(1)}, u32[]{:S(2)}, u32[]{:S(2)}) collective-permute-start(bf16[576,256]{1,0:T(8,128)(2,1)S(1)} %constant_dynamic-update-slice_fusion.4), channel_id=1, source_target_pairs={{0,1},{1,2},{2,3},{3,0},{4,5},{5,6},{6,7},{7,4},{8,9},{9,10},{10,1... | collective-permute-start | bytes 884744 | tf_op jit(solution)/shard_map/ppermute | solution.py:492
  125.5 20.6 %collective-permute-start.12 = (bf16[64,256]{1,0:T(8,128)(2,1)S(1)}, bf16[64,256]{1,0:T(8,128)(2,1)S(1)}, u32[]{:S(2)}, u32[]{:S(2)}) collective-permute-start(bf16[64,256]{1,0:T(8,128)(2,1)S(1)} %get-tuple-element.62), channel_id=1, source_target_pairs={{0,8},{8,16},{16,24},{24,32},{32,40},{40,48},{48,56},{56,64},{64,7... | collective-permute-start | bytes 98312 | tf_op jit(solution)/shard_map/ppermute | solution.py:458
  131.5 10.6 %collective-permute-start.31 = (bf16[576,256]{1,0:T(8,128)(2,1)S(1)}, bf16[576,256]{1,0:T(8,128)(2,1)S(1)}, u32[]{:S(2)}, u32[]{:S(2)}) collective-permute-start(bf16[576,256]{1,0:T(8,128)(2,1)S(1)} %constant_dynamic-update-slice_fusion.4), channel_id=1, source_target_pairs={{0,2},{1,3},{2,0},{3,1},{4,6},{5,7},{6,4},{7,5},{8,10},{9,11},{10,... | collective-permute-start | bytes 884744 | tf_op jit(solution)/shard_map/ppermute | solution.py:492
  142.1 20.5 %collective-permute-start.32 = (bf16[2304,256]{1,0:T(8,128)(2,1)S(1)}, bf16[2304,256]{1,0:T(8,128)(2,1)S(1)}, u32[]{:S(2)}, u32[]{:S(2)}) collective-permute-start(bf16[2304,256]{1,0:T(8,128)(2,1)S(1)} %constant_dynamic-update-slice_fusion), channel_id=1, source_target_pairs={{0,8},{1,9},{2,10},{3,11},{4,12},{5,13},{6,14},{7,15},{8,0},{9,1},... | collective-permute-start | bytes 3538952 | tf_op jit(solution)/shard_map/ppermute | solution.py:492
  149.5 6.4 %collective-permute-start.14 = (bf16[64,256]{1,0:T(8,128)(2,1)S(1)}, bf16[64,256]{1,0:T(8,128)(2,1)S(1)}, u32[]{:S(2)}, u32[]{:S(2)}) collective-permute-start(bf16[64,256]{1,0:T(8,128)(2,1)S(1)} %get-tuple-element.93), channel_id=1, source_target_pairs={{0,1},{1,2},{2,3},{3,4},{4,5},{5,6},{6,7},{7,0},{8,9},{9,10},{10,1... | collective-permute-start | bytes 98312 | tf_op jit(solution)/shard_map/ppermute | solution.py:467
  149.6 6.4 %collective-permute-start.15 = (bf16[64,256]{1,0:T(8,128)(2,1)S(1)}, bf16[64,256]{1,0:T(8,128)(2,1)S(1)}, u32[]{:S(2)}, u32[]{:S(2)}) collective-permute-start(bf16[64,256]{1,0:T(8,128)(2,1)S(1)} %get-tuple-element.92), channel_id=1, source_target_pairs={{0,7},{1,0},{2,1},{3,2},{4,3},{5,4},{6,5},{7,6},{8,15},{9,8},{10,9... | collective-permute-start | bytes 98312 | tf_op jit(solution)/shard_map/ppermute | solution.py:468
  (26 other events, 170.2 us)

commit v2 on v1

--- a/solution.py
+++ b/solution.py
@@ -265,7 +265,7 @@
     return total
 
 
-def weight_sums(xt, frame, halo, edges, out):
+def weight_sums(xt, frame, halo, edges, store):
     side = []
     for s in range(4):
         side.append(
@@ -288,27 +288,34 @@
                 part = part + side[2][a * C : (a + 1) * C]
             if b == 2:
                 part = part + side[3][a * C : (a + 1) * C]
-            out[pl.ds((a * 3 + b) * C, C)] = part.astype(out.dtype)
-
-
-def k_pack_field(lk, field, pk):
+            store((a * 3 + b) * C, part.astype(BF))
+
+
+def edges_of(field):
     def edge_column(at):
         lo = at // 16 * 16
         part = field[:, lo : lo + 16, :].astype(F32)
         row = lax.broadcasted_iota(jnp.int32, (S, 16, C), 1)
         return jnp.sum(jnp.where(row == at - lo, part, 0.0), axis=1)
 
-    edges = jnp.concatenate(
+    return jnp.concatenate(
         [field[0], field[S - 1], edge_column(0).astype(BF), edge_column(S - 1).astype(BF)],
         axis=0,
     )
-    pk[...] = pack_edges(lk, edges)
-
-
-def k_first(field, w, hidden, slope, e0, xt, x, frame):
+
+
+def k_pack_field(lk, field, pk):
+    pk[...] = pack_edges(lk, edges_of(field))
+
+
+def k_edges(cells, edges):
+    edges[...] = edges_of(cells)
+
+
+def k_first(field, w, after, hidden, slope, e0, xt, x, frame):
     x[...] = field[...].astype(F32)
+    xt[...] = field[...].T
     spread_columns(x, frame, 0, 2)
-    xt[...] = field[...].T
 
     @pl.loop(0, N_BLK)
     def _(i):
@@ -337,14 +344,12 @@
     pk[...] = pack_edges(lk, value.astype(BF))
 
 
-def k_second(hidden0, he, cot, w, xt, mixed, delta, e0, ec, x, frame, edges):
-    x[...] = cot[...].astype(F32)
-    take_edges(x, ec)
+def k_second(he, hidden0, cot, w, after, xt, mixed, delta, e0, x, frame, edges):
+    edges[...] = he[...].astype(F32)
     x[...] = hidden0[...].astype(F32)
-    edges[...] = he[...].astype(F32)
     put_edges(x, edges)
+    xt[...] = x[...].astype(BF).T
     spread_columns(x, frame, 0, 2)
-    xt[...] = x[...].astype(BF).T
 
     @pl.loop(0, N_BLK)
     def _(i):
@@ -365,18 +370,16 @@
     z = e0[...] + jnp.concatenate(halo_sums(sides, w), axis=0)
     value, grad = gelu_both(z)
     mixed[...] = value.astype(BF)
-    edges = (ec[...] * grad).astype(BF)
+    edges = (ec[...].astype(F32) * grad).astype(BF)
     delta[...] = edges
     pk[...] = pack_rims(lk, rims_of(edges, w))
 
 
-def k_second_back(mixed0, me, delta0, de, w, xt, halo, slope, mixed, total, fd, e0, x, frame, edges):
-    x[...] = mixed0[...].astype(F32)
-    edges[...] = me[...].astype(F32)
-    put_edges(x, edges)
-    mixed[...] = x[...].astype(BF)
+def k_second_back(
+    de, halo, delta0, w, xt, slope, after, total, fd, e0, x, frame, edges
+):
+    edges[...] = de[...].astype(F32)
     x[...] = delta0[...].astype(F32)
-    edges[...] = de[...].astype(F32)
     put_edges(x, edges)
     spread_columns(x, frame, 2, 0)
 
@@ -388,7 +391,11 @@
         fd[at] = (g * slope[at]).astype(BF)
 
     take_edges(x, e0)
-    weight_sums(xt, frame, halo, de, total)
+
+    def store(row, part):
+        total[pl.ds(row, C)] = part
+
+    weight_sums(xt, frame, halo, de, store)
 
 
 def k_first_delta_edges(lk, up, left, right, down, e0, slope, w, delta, pk):
@@ -399,51 +406,136 @@
     pk[...] = pack_rims(lk, rims_of(edges, w))
 
 
-def k_first_total(delta0, de, xt, halo, total, x, frame, edges):
+def k_first_total(at, de, halo, delta0, xt, other, keep, send, x, frame, edges, tv):
+    edges[...] = de[...].astype(F32)
+    x[...] = delta0[...].astype(F32)
+    put_edges(x, edges)
+    spread_columns(x, frame, 2, 0)
+
+    def store(row, part):
+        tv[pl.ds(row, C)] = part
+
+    weight_sums(xt, frame, halo, de, store)
+    here = at[0] == 0
+    keep[...] = jnp.where(here, tv[...], other[...])
+    send[...] = jnp.where(here, other[...], tv[...])
+
+
+def k_input_middle(de, delta0, w, after, out, x, frame, edges):
     x[...] = delta0[...].astype(F32)
     edges[...] = de[...].astype(F32)
     put_edges(x, edges)
     spread_columns(x, frame, 2, 0)
-    weight_sums(xt, frame, halo, de, total)
-
-
-def k_input_grad(lk, up, left, right, down, delta0, de, w, out, x, frame, edges):
-    x[...] = delta0[...].astype(F32)
-    edges[...] = de[...].astype(F32)
-    put_edges(x, edges)
-    spread_columns(x, frame, 2, 0)
 
     @pl.loop(0, N_BLK)
     def _(i):
-        x[block_of(i)] = back_block(frame, w, i)
-
+        out[block_of(i)] = back_block(frame, w, i)
+
+
+def k_input_grad(lk, up, left, right, down, middle, mixed0, me, after, out, mixed, x, edges):
     adds = cross(rim_adds(lk, join((up, left, right, down))))
+    x[...] = middle[...]
     take_edges(x, edges)
     edges[...] += jnp.concatenate(adds, axis=0)
     put_edges(x, edges)
     out[...] = x[...].astype(BF)
+    x[...] = mixed0[...].astype(F32)
+    edges[...] = me[...].astype(F32)
+    put_edges(x, edges)
+    mixed[...] = x[...].astype(BF)
+
+
+STEPS = (0, 1, 3, 2)
+
+
+def quarter(place, step, rows):
+    return pl.ds(pl.multiple_of((place + step) % 4 * rows, 16), rows)
+
+
+def k_core_sum(at, keep, got, pk, own, s1, s3, s2, pk_out):
+    rows = own.shape[0]
+    for step, out in zip(STEPS, (own, s1, s3, s2)):
+        part = quarter(at[1], step, rows)
+        out[...] = (keep[part].astype(F32) + got[part].astype(F32)).astype(out.dtype)
+    pk_out[...] = pk[...]
+
+
+def k_z_sum(at, own, g1, g3, g2, pk, left, right, after, o, s1, s3, s2, up_out, down_out, x):
+    rows = o.shape[0]
+    x[...] = (own[...] + g2[...].astype(F32)) + (g1[...].astype(F32) + g3[...].astype(F32))
+    for step, out in zip(STEPS, (o, s1, s3, s2)):
+        out[...] = x[quarter(at[2], step, rows)].astype(out.dtype)
+    up_out[...] = with_corners(pk[0:PK], left[...], right[...], 0)
+    down_out[...] = with_corners(pk[3 * PK :], left[...], right[...], 1)
+
+
+def with_corners(edge, left, right, k):
+    row = lax.broadcasted_iota(jnp.int32, (PK, C), 0)
+    out = jnp.where(row == S, left[S + k : S + k + 1].astype(F32), edge.astype(F32))
+    return jnp.where(row == S + 1, right[S + k : S + k + 1].astype(F32), out).astype(BF)
+
+
+def k_y_sum(own, g1, g3, g2, out):
+    total = (own[...] + g2[...].astype(F32)) + (g1[...].astype(F32) + g3[...].astype(F32))
+    out[...] = total.astype(BF)
+
+
+def k_x_sum(scale, own, g1, g3, g2, out):
+    total = (own[...].astype(F32) + g2[...].astype(F32)) + (
+        g1[...].astype(F32) + g3[...].astype(F32)
+    )
+    out[...] = (total * scale).astype(BF)
+
+
+def k_join(at, own, g1, g3, g2, up, down, out):
+    rows = own.shape[0]
+    for step, part in zip(STEPS, (own, g1, g3, g2)):
+        out[quarter(at[2], step, rows)] = part[...]
+
+
+def k_unpack(at, a0, a1, a3, a2, b0, b1, b3, b2, after, first, second):
+    rows = a0.shape[0]
+    here = at[0] == 0
+    for step, a, b in zip(STEPS, (a0, a1, a3, a2), (b0, b1, b3, b2)):
+        part = quarter(at[1], step, rows)
+
+        @pl.when(here)
+        def _():
+            first[part] = a[...].astype(F32)
+            second[part] = b[...].astype(F32)
+
+        @pl.when(jnp.logical_not(here))
+        def _():
+            first[part] = b[...].astype(F32)
+            second[part] = a[...].astype(F32)
 
 
 VMEM = pl.BlockSpec(memory_space=pltpu.VMEM)
 SMEM = pl.BlockSpec(memory_space=pltpu.SMEM)
+ANY = pl.BlockSpec(memory_space=pl.ANY)
+CELL_BF = pltpu.VMEM((CELLS, C), BF)
 WIDE = [pltpu.VMEM((CELLS, C), F32), pltpu.VMEM((CELLS + 2 * S, 3 * C), BF)]
 WIDER = WIDE + [pltpu.VMEM((4 * S, C), F32)]
 
 
-def call(kernel, args, outs, scratch=(), links=None, flops=0):
-    given = ([links] if links is not None else []) + list(args)
+def call(kernel, args, outs, scratch=(), links=None, flops=0, after=(), limit=8):
+    given = ([links] if links is not None else []) + [*args, *after]
     specs = ([SMEM] if links is not None else []) + [VMEM] * len(args)
+    specs += [ANY] * len(after)
+    name = getattr(kernel, "__name__", "k_x_sum")
     return pl.pallas_call(
         kernel,
-        out_shape=[jax.ShapeDtypeStruct(shape, dtype) for shape, dtype in outs],
+        out_shape=[
+            (pltpu.VMEM if len(out) > 2 else jax.ShapeDtypeStruct)(out[0], out[1]) for out in outs
+        ],
         in_specs=specs,
         out_specs=[VMEM] * len(outs),
         scratch_shapes=list(scratch),
-        compiler_params=pltpu.CompilerParams(vmem_limit_bytes=40 * MIB),
+        compiler_params=pltpu.CompilerParams(vmem_limit_bytes=limit * MIB),
         cost_estimate=pl.CostEstimate(
             flops=int(flops), bytes_accessed=4 * MIB, transcendentals=0
         ),
-        name=kernel.__name__,
+        name=name,
     )(*given)
 
 
@@ -451,12 +543,24 @@
     return [(i, (i + step) % count) for i in range(count)]
 
 
-def trade(pk):
+def trade_tile(pk):
     n_tile = lax.axis_size("tile")
-    n_lat = lax.axis_size("lat")
-    up, left, right, down = (pk[q * PK : (q + 1) * PK] for q in range(4))
+    left, right = pk[PK : 2 * PK], pk[2 * PK : 3 * PK]
     from_left = lax.ppermute(right, "tile", ring(n_tile, 1))
     from_right = lax.ppermute(left, "tile", ring(n_tile, -1))
+    return from_left, from_right
+
+
+def trade_lat(up, down):
+    n_lat = lax.axis_size("lat")
+    from_up = lax.ppermute(down, "lat", ring(n_lat, 1))
+    from_down = lax.ppermute(up, "lat", ring(n_lat, -1))
+    return from_up, from_down
+
+
+def trade(pk):
+    from_left, from_right = trade_tile(pk)
+    up, down = pk[:PK], pk[3 * PK :]
     filler = jnp.zeros((PK - S - 2, C), BF)
     up = jnp.concatenate(
         [up[:S], from_left[S : S + 1], from_right[S : S + 1], filler], axis=0
@@ -464,8 +568,7 @@
     down = jnp.concatenate(
         [down[:S], from_left[S + 1 : S + 2], from_right[S + 1 : S + 2], filler], axis=0
     )
-    from_up = lax.ppermute(down, "lat", ring(n_lat, 1))
-    from_down = lax.ppermute(up, "lat", ring(n_lat, -1))
+    from_up, from_down = trade_lat(up, down)
     return from_up, from_left, from_right, from_down
 
 
@@ -492,46 +595,12 @@
     return lax.ppermute(x, ("tile", "lat"), group_ring(kind, step))
 
 
-def scatter4(x, kind, place):
-    k = x.shape[0] // 4
-    got = [
-        move(lax.dynamic_slice_in_dim(x, (place + s) % 4 * k, k, 0), kind, s) for s in (1, 3, 2)
-    ]
-    total = lax.dynamic_slice_in_dim(x, place * k, k, 0).astype(F32)
-    for g in got:
-        total = total + g.astype(F32)
-    return total.astype(BF)
-
-
-def gather4(x, kind, place):
-    k = x.shape[0]
-    out = jnp.zeros((4 * k, C), x.dtype)
-    parts = [(0, x)] + [(s, move(x, kind, 4 - s)) for s in (1, 3, 2)]
-    for s, part in parts:
-        out = lax.dynamic_update_slice_in_dim(out, part, (place + s) % 4 * k, 0)
-    return out
-
-
-def sum_all(first, second, root):
-    tile_at = lax.axis_index("tile")
-    lat_at = lax.axis_index("lat")
-    core, z_at, y_at = tile_at % 2, lat_at % 4, tile_at // 4
-    keep = jnp.where(core == 0, first, second)
-    send = jnp.where(core == 0, second, first)
-    part = (keep.astype(F32) + move(send, "core", 1).astype(F32)).astype(BF)
-    part = scatter4(part, "z", z_at)
-    part = scatter4(part, "y", y_at)
-    total = part.astype(F32)
-    for s in (1, 3, 2):
-        total = total + move(part, "x", s).astype(F32)
-    part = (total * (1.0 / root)).astype(BF)
-    part = gather4(part, "y", y_at)
-    part = gather4(part, "z", z_at)
-    other = move(part, "core", 1)
-    return (
-        jnp.where(core == 0, part, other).astype(F32),
-        jnp.where(core == 0, other, part).astype(F32),
-    )
+def moves(parts, kind):
+    return [move(part, kind, step) for part, step in zip(parts, (1, 3, 2))]
+
+
+def gathers(part, kind):
+    return [move(part, kind, 4 - step) for step in (1, 3, 2)]
 
 
 def shards(field, cotangent, first_weight, second_weight, side_links, corner_links):
@@ -549,44 +618,103 @@
     halo_bf, turned, packs = ((4 * S, 3 * C), BF), ((C, CELLS), BF), ((4 * PK, C), BF)
     work = 2 * CELLS * 9 * C * C
 
+    far_bf, far_f32 = ((CELLS, C), BF, 1), ((CELLS, C), F32, 1)
+    far_turned = ((C, CELLS), BF, 1)
+
     (pk,) = call(k_pack_field, [field], [packs], links=lk)
     got = trade(pk)
+    (cot_e,) = call(k_edges, [cotangent], [edge_bf])
     hidden0, slope0, e0, xt1 = call(
-        k_first, [cells, w1], [cell_bf, cell_f32, edge_f32, turned], WIDE, flops=work
+        k_first,
+        [cells, w1],
+        [far_bf, far_f32, edge_f32, far_turned],
+        WIDE,
+        after=[got[1]],
+        flops=work,
+        limit=20,
     )
     halo1, slope_e, hidden_e, pk = call(
         k_first_edges, [*got, e0, w1], [halo_bf, edge_f32, edge_bf, packs], links=lk
     )
     got = trade(pk)
-    xt2, mixed0, delta0, e0, ec = call(
+    xt2, mixed0, delta0, e0 = call(
         k_second,
-        [hidden0, hidden_e, cot, w2],
-        [turned, cell_bf, cell_bf, edge_f32, edge_f32],
+        [hidden_e, hidden0, cot, w2],
+        [far_turned, far_bf, far_bf, edge_f32],
         WIDER,
+        after=[got[1]],
         flops=work,
+        limit=20,
     )
     halo2, mixed_e, delta_e, pk = call(
-        k_second_edges, [*got, e0, ec, w2], [halo_bf, edge_bf, edge_bf, packs], links=lk
+        k_second_edges, [*got, e0, cot_e, w2], [halo_bf, edge_bf, edge_bf, packs], links=lk
     )
     got = trade(pk)
-    mixed, total2, fd0, e0 = call(
+    total2, fd0, e0 = call(
         k_second_back,
-        [mixed0, mixed_e, delta0, delta_e, w2, xt2, halo2, slope0],
-        [cell_bf, cell_bf, cell_bf, edge_f32],
+        [delta_e, halo2, delta0, w2, xt2, slope0],
+        [far_bf, far_bf, edge_f32],
         WIDER,
+        after=[got[1]],
         flops=2 * work,
+        limit=22,
     )
     fd_e, pk = call(
         k_first_delta_edges, [*got, e0, slope_e, w1], [edge_bf, packs], links=lk
     )
-    got = trade(pk)
-    (total1,) = call(
-        k_first_total, [fd0, fd_e, xt1, halo1], [cell_bf], WIDER, flops=work
-    )
+    core, z_at, y_at = lon_at % 2, lat_at % 4, lon_at // 4
+    at = jnp.stack([core, z_at, y_at]).astype(jnp.int32)
+    rows_z, rows_y = CELLS // 4, CELLS // 16
+    keep, send = call(
+        k_first_total,
+        [fd_e, halo1, fd0, xt1, total2],
+        [cell_bf, cell_bf],
+        WIDER + [CELL_BF],
+        links=at,
+        flops=work,
+        limit=20,
+    )
+    quad_z = [((rows_z, C), F32)] + [((rows_z, C), BF)] * 3
+    own, *parts, pk = call(
+        k_core_sum, [keep, move(send, "core", 1), pk], quad_z + [packs], links=at
+    )
+    left, right = trade_tile(pk)
+    (middle,) = call(
+        k_input_middle, [fd_e, fd0, w1], [cell_f32], WIDER, flops=work, after=[own], limit=18
+    )
+    quad_y = [((rows_y, C), F32)] + [((rows_y, C), BF)] * 3
+    one_pack = ((PK, C), BF)
+    own, *parts, up, down = call(
+        k_z_sum,
+        [own, *moves(parts, "z"), pk, left, right],
+        quad_y + [one_pack, one_pack],
+        [pltpu.VMEM((rows_z, C), F32)],
+        links=at,
+        after=[middle],
+    )
+    up, down = trade_lat(up, down)
+    piece_bf = ((rows_y, C), BF)
+    (part,) = call(k_y_sum, [own, *moves(parts, "y")], [piece_bf])
     root = math.sqrt(CELLS * lax.axis_size("lat") * lax.axis_size("tile"))
-    first, second = sum_all(total1, total2, root)
-    (grad,) = call(
-        k_input_grad, [*got, fd0, fd_e, w1], [cell_bf], WIDER, links=lk, flops=work
+    (part,) = call(
+        functools.partial(k_x_sum, 1.0 / root), [part, *moves([part] * 3, "x")], [piece_bf]
+    )
+    (part,) = call(
+        k_join, [part, *gathers(part, "y")], [((rows_z, C), BF)], links=at, after=[up, down]
+    )
+    parts = [part, *gathers(part, "z")]
+    grad, mixed = call(
+        k_input_grad,
+        [up, left, right, down, middle, mixed0, mixed_e],
+        [cell_bf, cell_bf],
+        [WIDE[0], WIDER[2]],
+        links=lk,
+        after=[part],
+        limit=16,
+    )
+    others = [move(part, "core", 1) for part in parts]
+    first, second = call(
+        k_unpack, [*parts, *others], [cell_f32, cell_f32], links=at, after=[grad], limit=12
     )
     return (
         mixed.reshape(S, S, C),

time: 167 us -> 144 us (0.86)
  waiting for transfers between devices: 51.2 us -> 25.8 us
  starting transfers between devices: 58 us -> 68.5 us
  other arithmetic: 7.9 us -> 0.41 us
  Pallas kernels: 37.1 us -> 43 us
  local copies, waits for them, and re-layouts: 10.7 us -> 5.17 us
    ppermute x17 -> x20, waiting for transfers between devices: 39.3 us -> 18.4 us  [move(): return lax.ppermute(x, ('tile', 'lat'), group_ring(kind, step))]
    ppermute x17 -> x20, starting transfers between devices: 22.4 us -> 37.4 us  [move(): return lax.ppermute(x, ('tile', 'lat'), group_ring(kind, step))]
    pallas_call x9 -> x17, Pallas kernels: 37.1 us -> 43 us  [call(): pl.pallas_call(kernel, out_shape=[(pltpu.VMEM if len(out) > 2 else jax.Sh...]
    unnamed x34 -> x14, local copies, waits for them, and re-layouts: 8.95 us -> 3.84 us
    ppermute x16, starting transfers between devices: 35.6 us -> 31.1 us  [the longest x4 18.6 us: trade_lat(): from_down = lax.ppermute(up, 'lat', ring(n_lat, -1))]
    ppermute x16, waiting for transfers between devices: 11.8 us -> 7.32 us  [the longest x4 3.23 us: trade_lat(): from_up = lax.ppermute(down, 'lat', ring(n_lat, 1))]
    reshape x2 -> x0, other arithmetic: 3.25 us -> none  [the longest x1 1.63 us: shards(): first.reshape(3, 3, C, C)]
    convert_element_type x3 -> x0, other arithmetic: 2.88 us -> none  [the longest x1 1.72 us: sum_all(): part = (keep.astype(F32) + move(send, 'core', 1).astype(F32)).astype(BF)]
  transfers between devices with their start and end apart: 33 -> 36, of which waited for: 18 -> 16; matrix products, arithmetic and copies ran while one was open for 0% -> 0% of each run, Pallas kernels for 16% -> 18%
where the time goes in v2:
time: 144 us
  starting transfers between devices  68.5 us (48%)
  Pallas kernels  43 us (30%)
  waiting for transfers between devices  25.8 us (18%)
  local copies, waits for them, and re-layouts  5.17 us (4%)
    pallas_call x17, Pallas kernels, call(): pl.pallas_call(kernel, out_shape=[(pltpu.VMEM if len(out) > 2 else jax.Sh...  43 us
    ppermute x20, starting transfers between devices, move(): return lax.ppermute(x, ('tile', 'lat'), group_ring(kind, step))  37.4 us
    ppermute x4, starting transfers between devices, trade_lat(): from_down = lax.ppermute(up, 'lat', ring(n_lat, -1))  18.6 us
    ppermute x20, waiting for transfers between devices, move(): return lax.ppermute(x, ('tile', 'lat'), group_ring(kind, step))  18.4 us
    ppermute x4, starting transfers between devices, trade_tile(): from_right = lax.ppermute(left, 'tile', ring(n_tile, -1))  6.84 us
    ppermute x4, starting transfers between devices, trade_tile(): from_left = lax.ppermute(right, 'tile', ring(n_tile, 1))  4.97 us
    unnamed x14, local copies, waits for them, and re-layouts  3.84 us
    ppermute x4, waiting for transfers between devices, trade_lat(): from_up = lax.ppermute(down, 'lat', ring(n_lat, 1))  3.23 us
  transfers between devices with their start and end apart: 36, of which 16 were waited for; matrix products, arithmetic and copies ran while one was open for 0% of the time, Pallas kernels for 18%

profile of v2, /device:TPU:1, one launch (start us, length us, event | category | flops | bytes accessed | tf_op | source)
XLA Modules:
  0.0 143.8 jit_solution(17604726413090361773)
XLA Ops:
  4.2 2.7 %collective-permute-start = (bf16[64,256]{1,0:T(8,128)(2,1)S(1)}, bf16[64,256]{1,0:T(8,128)(2,1)S(1)}, u32[]{:S(2)}, u32[]{:S(2)}) collective-permute-start(bf16[64,256]{1,0:T(8,128)(2,1)S(1)} %get-tuple-element.92), channel_id=1, source_target_pairs={{0,8},{8,16},{16,24},{24,32},{32,40},{40,48},{48,56},{56,64},{64,7... | collective-permute-start | bytes 98312 | tf_op jit(solution)/shard_map/ppermute | solution.py:549
  10.6 6.0 %collective-permute-start.3 = (bf16[64,256]{1,0:T(8,128)(2,1)S(1)}, bf16[64,256]{1,0:T(8,128)(2,1)S(1)}, u32[]{:S(2)}, u32[]{:S(2)}) collective-permute-start(bf16[64,256]{1,0:T(8,128)(2,1)S(1)} %get-tuple-element.110), channel_id=1, source_target_pairs={{0,7},{1,0},{2,1},{3,2},{4,3},{5,4},{6,5},{7,6},{8,15},{9,8},{10,9... | collective-permute-start | bytes 98312 | tf_op jit(solution)/shard_map/ppermute | solution.py:557
  16.6 5.3 %k_first.1 = (bf16[2304,256]{1,0:T(8,128)(2,1)S(1)}, f32[2304,256]{1,0:T(8,128)S(1)}, f32[192,256]{1,0:T(8,128)S(1)}, bf16[256,2304]{1,0:T(8,128)(2,1)S(1)}) custom-call(bf16[2304,256]{1,0:T(8,128)(2,1)S(1)} %bitcast.15, bf16[3,768,256]{2,1,0:T(8,128)(2,1)S(1)} %bitcast.11, bf16[64,256]{1,0:T(8,128)(2,1)S(1)} %collective-permute-done.after.left), custom_call_target="tpu_custom_call" | custom-call | flops 2717908992 | bytes 4194304 | tf_op jit(solution)/shard_map/k_first/pallas_call | solution.py:526
  28.6 4.6 %collective-permute-start.7 = (bf16[64,256]{1,0:T(8,128)(2,1)S(1)}, bf16[64,256]{1,0:T(8,128)(2,1)S(1)}, u32[]{:S(2)}, u32[]{:S(2)}) collective-permute-start(bf16[64,256]{1,0:T(8,128)(2,1)S(1)} %get-tuple-element.108), channel_id=1, source_target_pairs={{0,7},{1,0},{2,1},{3,2},{4,3},{5,4},{6,5},{7,6},{8,15},{9,8},{10,9... | collective-permute-start | bytes 98312 | tf_op jit(solution)/shard_map/ppermute | solution.py:557
  33.2 5.4 %k_second.1 = (bf16[256,2304]{1,0:T(8,128)(2,1)S(1)}, bf16[2304,256]{1,0:T(8,128)(2,1)S(1)}, bf16[2304,256]{1,0:T(8,128)(2,1)S(1)}, f32[192,256]{1,0:T(8,128)S(1)}) custom-call(bf16[192,256]{1,0:T(8,128)(2,1)S(1)} %get-tuple-element.44.he, bf16[2304,256]{1,0:T(8,128)(2,1)S(1)} %get-tuple-element.45.hidden0, bf16[2304,256]{1,0:T(8,128)(2,1)S(1)} %bitcast.16, ...), custom_call_target="tpu_custom_call" | custom-call | flops 2717908992 | bytes 4194304 | tf_op jit(solution)/shard_map/k_second/pallas_call | solution.py:526
  42.7 3.9 %collective-permute-start.9 = (bf16[64,256]{1,0:T(8,128)(2,1)S(1)}, bf16[64,256]{1,0:T(8,128)(2,1)S(1)}, u32[]{:S(2)}, u32[]{:S(2)}) collective-permute-start(bf16[64,256]{1,0:T(8,128)(2,1)S(1)} %get-tuple-element.85), channel_id=1, source_target_pairs={{0,120},{8,0},{16,8},{24,16},{32,24},{40,32},{48,40},{56,48},{64,5... | collective-permute-start | bytes 98312 | tf_op jit(solution)/shard_map/ppermute | solution.py:550
  47.6 3.6 %collective-permute-start.11 = (bf16[64,256]{1,0:T(8,128)(2,1)S(1)}, bf16[64,256]{1,0:T(8,128)(2,1)S(1)}, u32[]{:S(2)}, u32[]{:S(2)}) collective-permute-start(bf16[64,256]{1,0:T(8,128)(2,1)S(1)} %get-tuple-element.106), channel_id=1, source_target_pairs={{0,7},{1,0},{2,1},{3,2},{4,3},{5,4},{6,5},{7,6},{8,15},{9,8},{10,9... | collective-permute-start | bytes 98312 | tf_op jit(solution)/shard_map/ppermute | solution.py:557
  51.2 8.1 %k_second_back.1 = (bf16[2304,256]{1,0:T(8,128)(2,1)S(1)}, bf16[2304,256]{1,0:T(8,128)(2,1)S(1)}, f32[192,256]{1,0:T(8,128)S(1)}) custom-call(bf16[192,256]{1,0:T(8,128)(2,1)S(1)} %get-tuple-element.48.de, bf16[192,768]{1,0:T(8,128)(2,1)S(1)} %get-tuple-element.49.halo, bf16[2304,256]{1,0:T(8,128)(2,1)S(1)} %get-tuple-element.50.delta0, ...), custom_call_target="tpu_custom_call" | custom-call | flops 5435817984 | bytes 4194304 | tf_op jit(solution)/shard_map/k_second_back/pallas_call | solution.py:526
  61.2 4.7 %k_first_total.1 = (bf16[2304,256]{1,0:T(8,128)(2,1)S(1)}, bf16[2304,256]{1,0:T(8,128)(2,1)S(1)}) custom-call(s32[3]{0:T(128)S(1)} %pad_add_fusion.1.at, bf16[192,256]{1,0:T(8,128)(2,1)S(1)} %get-tuple-element.55.de, bf16[192,768]{1,0:T(8,128)(2,1)S(1)} %get-tuple-element.56.halo, bf16[2304,256]{1,0:T(8,128)(2,1)S(1)} %get-tuple-element.57.delta0, ...), custom_call_target="tpu_custom_call" | custom-call | flops 2717908992 | bytes 4194304 | tf_op jit(solution)/shard_map/k_first_total/pallas_call | solution.py:526
  65.9 4.8 %collective-permute-start.12 = (bf16[2304,256]{1,0:T(8,128)(2,1)S(1)}, bf16[2304,256]{1,0:T(8,128)(2,1)S(1)}, u32[]{:S(2)}, u32[]{:S(2)}) collective-permute-start(bf16[2304,256]{1,0:T(8,128)(2,1)S(1)} %get-tuple-element.61), channel_id=1, source_target_pairs={{0,8},{1,9},{2,10},{3,11},{4,12},{5,13},{6,14},{7,15},{8,0},{9,1},... | collective-permute-start | bytes 3538952 | tf_op jit(solution)/shard_map/ppermute | solution.py:595
  74.0 3.0 %collective-permute-start.14 = (bf16[576,256]{1,0:T(8,128)(2,1)S(1)}, bf16[576,256]{1,0:T(8,128)(2,1)S(1)}, u32[]{:S(2)}, u32[]{:S(2)}) collective-permute-start(bf16[576,256]{1,0:T(8,128)(2,1)S(1)} %get-tuple-element.65), channel_id=1, source_target_pairs={{0,3},{1,0},{2,1},{3,2},{4,7},{5,4},{6,5},{7,6},{8,11},{9,8},{10,9... | collective-permute-start | bytes 884744 | tf_op jit(solution)/shard_map/ppermute | solution.py:595
  79.8 4.7 %k_input_middle.1.after.middle = f32[2304,256]{1,0:T(8,128)S(1)} custom-call(bf16[192,256]{1,0:T(8,128)(2,1)S(1)} %get-tuple-element.55.de, bf16[2304,256]{1,0:T(8,128)(2,1)S(1)} %get-tuple-element.57.delta0, bf16[3,768,256]{2,1,0:T(8,128)(2,1)S(1)} %bitcast.14, f32[576,256]{1,0:T(8,128)S(1)} %get-tuple-element.63.after.own), custom_call_target="tpu_custom_call" | custom-call | flops 2717908992 | bytes 4194304 | tf_op jit(solution)/shard_map/k_input_middle/pallas_call | solution.py:526
  84.6 4.6 %collective-permute-done.14.g3 = bf16[576,256]{1,0:T(8,128)(2,1)S(1)} collective-permute-done((bf16[576,256]{1,0:T(8,128)(2,1)S(1)}, bf16[576,256]{1,0:T(8,128)(2,1)S(1)}, u32[]{:S(2)}, u32[]{:S(2)}) %collective-permute-start.14) | collective-permute-done | bytes 294944 | tf_op jit(solution)/shard_map/ppermute | solution.py:595
  92.0 2.7 %collective-permute-start.21 = (bf16[144,256]{1,0:T(8,128)(2,1)S(1)}, bf16[144,256]{1,0:T(8,128)(2,1)S(1)}, u32[]{:S(2)}, u32[]{:S(2)}) collective-permute-start(bf16[144,256]{1,0:T(8,128)(2,1)S(1)} %get-tuple-element.74), channel_id=1, source_target_pairs={{0,96},{1,97},{2,98},{3,99},{4,100},{5,101},{6,102},{7,103},{8,104... | collective-permute-start | bytes 221192 | tf_op jit(solution)/shard_map/ppermute | solution.py:595
  96.4 3.0 %collective-permute-done.22.g2 = bf16[144,256]{1,0:T(8,128)(2,1)S(1)} collective-permute-done((bf16[144,256]{1,0:T(8,128)(2,1)S(1)}, bf16[144,256]{1,0:T(8,128)(2,1)S(1)}, u32[]{:S(2)}, u32[]{:S(2)}) %collective-permute-start.22) | collective-permute-done | bytes 73760 | tf_op jit(solution)/shard_map/ppermute | solution.py:595
  99.5 2.8 %collective-permute-start.25 = (bf16[144,256]{1,0:T(8,128)(2,1)S(1)}, bf16[144,256]{1,0:T(8,128)(2,1)S(1)}, u32[]{:S(2)}, u32[]{:S(2)}) collective-permute-start(bf16[144,256]{1,0:T(8,128)(2,1)S(1)} %k_y_sum.1.own), channel_id=1, source_target_pairs={{0,4},{1,5},{2,6},{3,7},{4,0},{5,1},{6,2},{7,3},{8,12},{9,13},{10,... | collective-permute-start | bytes 221192 | tf_op jit(solution)/shard_map/ppermute | solution.py:595
  105.6 2.8 %collective-permute-done.23.g1 = bf16[144,256]{1,0:T(8,128)(2,1)S(1)} collective-permute-done((bf16[144,256]{1,0:T(8,128)(2,1)S(1)}, bf16[144,256]{1,0:T(8,128)(2,1)S(1)}, u32[]{:S(2)}, u32[]{:S(2)}) %collective-permute-start.23) | collective-permute-done | bytes 73760 | tf_op jit(solution)/shard_map/ppermute | solution.py:595
  112.2 4.4 %collective-permute-start.19 = (bf16[64,256]{1,0:T(8,128)(2,1)S(1)}, bf16[64,256]{1,0:T(8,128)(2,1)S(1)}, u32[]{:S(2)}, u32[]{:S(2)}) collective-permute-start(bf16[64,256]{1,0:T(8,128)(2,1)S(1)} %get-tuple-element.69), channel_id=1, source_target_pairs={{0,7},{1,0},{2,1},{3,2},{4,3},{5,4},{6,5},{7,6},{8,15},{9,8},{10,9... | collective-permute-start | bytes 98312 | tf_op jit(solution)/shard_map/ppermute | solution.py:557
  118.6 3.1 %collective-permute-start.30 = (bf16[576,256]{1,0:T(8,128)(2,1)S(1)}, bf16[576,256]{1,0:T(8,128)(2,1)S(1)}, u32[]{:S(2)}, u32[]{:S(2)}) collective-permute-start(bf16[576,256]{1,0:T(8,128)(2,1)S(1)} %k_join.1.after.a0), channel_id=1, source_target_pairs={{0,1},{1,2},{2,3},{3,0},{4,5},{5,6},{6,7},{7,4},{8,9},{9,10},{10,1... | collective-permute-start | bytes 884744 | tf_op jit(solution)/shard_map/ppermute | solution.py:595
  121.6 7.4 %collective-permute-start.32 = (bf16[576,256]{1,0:T(8,128)(2,1)S(1)}, bf16[576,256]{1,0:T(8,128)(2,1)S(1)}, u32[]{:S(2)}, u32[]{:S(2)}) collective-permute-start(bf16[576,256]{1,0:T(8,128)(2,1)S(1)} %k_join.1.after.a0), channel_id=1, source_target_pairs={{0,8},{1,9},{2,10},{3,11},{4,12},{5,13},{6,14},{7,15},{8,0},{9,1},... | collective-permute-start | bytes 884744 | tf_op jit(solution)/shard_map/ppermute | solution.py:595
  129.0 4.2 %collective-permute-start.35 = (bf16[576,256]{1,0:T(8,128)(2,1)S(1)}, bf16[576,256]{1,0:T(8,128)(2,1)S(1)}, u32[]{:S(2)}, u32[]{:S(2)}) collective-permute-start(bf16[576,256]{1,0:T(8,128)(2,1)S(1)} %collective-permute-done.31.a2), channel_id=1, source_target_pairs={{0,8},{1,9},{2,10},{3,11},{4,12},{5,13},{6,14},{7,15},{8,0},{9,1},... | collective-permute-start | bytes 884744 | tf_op jit(solution)/shard_map/ppermute | solution.py:595
  133.2 2.9 %collective-permute-start.34 = (bf16[576,256]{1,0:T(8,128)(2,1)S(1)}, bf16[576,256]{1,0:T(8,128)(2,1)S(1)}, u32[]{:S(2)}, u32[]{:S(2)}) collective-permute-start(bf16[576,256]{1,0:T(8,128)(2,1)S(1)} %collective-permute-done.30.a3), channel_id=1, source_target_pairs={{0,8},{1,9},{2,10},{3,11},{4,12},{5,13},{6,14},{7,15},{8,0},{9,1},... | collective-permute-start | bytes 884744 | tf_op jit(solution)/shard_map/ppermute | solution.py:595
  136.9 2.6 %k_input_grad.1 = (bf16[2304,256]{1,0:T(8,128)(2,1)}, bf16[2304,256]{1,0:T(8,128)(2,1)}) custom-call(s32[24]{0:T(128)S(1)} %pad_add_fusion.lk, bf16[64,256]{1,0:T(8,128)(2,1)S(1)} %collective-permute-done.18.up, bf16[64,256]{1,0:T(8,128)(2,1)S(1)} %collective-permute-done.16.left, bf16[64,256]{1,0:T(8,128)(2,1)S(1)} %collective-permute-done.17.right, ...), custom_call_target="tpu_custom_call" | custom-call | bytes 4194304 | tf_op jit(solution)/shard_map/k_input_grad/pallas_call | solution.py:526
  140.8 3.1 %k_unpack.1 = (f32[2304,256]{1,0:T(8,128)}, f32[2304,256]{1,0:T(8,128)}) custom-call(s32[3]{0:T(128)S(1)} %pad_add_fusion.1.at, bf16[576,256]{1,0:T(8,128)(2,1)S(1)} %k_join.1.after.a0, bf16[576,256]{1,0:T(8,128)(2,1)S(1)} %collective-permute-done.29.a1, bf16[576,256]{1,0:T(8,128)(2,1)S(1)} %collective-permute-done.30.a3, ...), custom_call_target="tpu_custom_call" | custom-call | bytes 4194304 | tf_op jit(solution)/shard_map/k_unpack/pallas_call | solution.py:526
  (104 shorter events, 42.8 us)
Async XLA Ops:
  10.6 11.4 %collective-permute-start.3 = (bf16[64,256]{1,0:T(8,128)(2,1)S(1)}, bf16[64,256]{1,0:T(8,128)(2,1)S(1)}, u32[]{:S(2)}, u32[]{:S(2)}) collective-permute-start(bf16[64,256]{1,0:T(8,128)(2,1)S(1)} %get-tuple-element.110), channel_id=1, source_target_pairs={{0,7},{1,0},{2,1},{3,2},{4,3},{5,4},{6,5},{7,6},{8,15},{9,8},{10,9... | collective-permute-start | bytes 98312 | tf_op jit(solution)/shard_map/ppermute | solution.py:557
  16.6 6.4 %collective-permute-start.2 = (bf16[64,256]{1,0:T(8,128)(2,1)S(1)}, bf16[64,256]{1,0:T(8,128)(2,1)S(1)}, u32[]{:S(2)}, u32[]{:S(2)}) collective-permute-start(bf16[64,256]{1,0:T(8,128)(2,1)S(1)} %get-tuple-element.111), channel_id=1, source_target_pairs={{0,1},{1,2},{2,3},{3,4},{4,5},{5,6},{6,7},{7,0},{8,9},{9,10},{10,1... | collective-permute-start | bytes 98312 | tf_op jit(solution)/shard_map/ppermute | solution.py:556
  28.6 10.0 %collective-permute-start.7 = (bf16[64,256]{1,0:T(8,128)(2,1)S(1)}, bf16[64,256]{1,0:T(8,128)(2,1)S(1)}, u32[]{:S(2)}, u32[]{:S(2)}) collective-permute-start(bf16[64,256]{1,0:T(8,128)(2,1)S(1)} %get-tuple-element.108), channel_id=1, source_target_pairs={{0,7},{1,0},{2,1},{3,2},{4,3},{5,4},{6,5},{7,6},{8,15},{9,8},{10,9... | collective-permute-start | bytes 98312 | tf_op jit(solution)/shard_map/ppermute | solution.py:557
  33.2 6.4 %collective-permute-start.6 = (bf16[64,256]{1,0:T(8,128)(2,1)S(1)}, bf16[64,256]{1,0:T(8,128)(2,1)S(1)}, u32[]{:S(2)}, u32[]{:S(2)}) collective-permute-start(bf16[64,256]{1,0:T(8,128)(2,1)S(1)} %get-tuple-element.109), channel_id=1, source_target_pairs={{0,1},{1,2},{2,3},{3,4},{4,5},{5,6},{6,7},{7,0},{8,9},{9,10},{10,1... | collective-permute-start | bytes 98312 | tf_op jit(solution)/shard_map/ppermute | solution.py:556
  42.0 5.2 %collective-permute-start.8 = (bf16[64,256]{1,0:T(8,128)(2,1)S(1)}, bf16[64,256]{1,0:T(8,128)(2,1)S(1)}, u32[]{:S(2)}, u32[]{:S(2)}) collective-permute-start(bf16[64,256]{1,0:T(8,128)(2,1)S(1)} %get-tuple-element.84), channel_id=1, source_target_pairs={{0,8},{8,16},{16,24},{24,32},{32,40},{40,48},{48,56},{56,64},{64,7... | collective-permute-start | bytes 98312 | tf_op jit(solution)/shard_map/ppermute | solution.py:549
  47.6 11.7 %collective-permute-start.11 = (bf16[64,256]{1,0:T(8,128)(2,1)S(1)}, bf16[64,256]{1,0:T(8,128)(2,1)S(1)}, u32[]{:S(2)}, u32[]{:S(2)}) collective-permute-start(bf16[64,256]{1,0:T(8,128)(2,1)S(1)} %get-tuple-element.106), channel_id=1, source_target_pairs={{0,7},{1,0},{2,1},{3,2},{4,3},{5,4},{6,5},{7,6},{8,15},{9,8},{10,9... | collective-permute-start | bytes 98312 | tf_op jit(solution)/shard_map/ppermute | solution.py:557
  51.2 8.1 %collective-permute-start.10 = (bf16[64,256]{1,0:T(8,128)(2,1)S(1)}, bf16[64,256]{1,0:T(8,128)(2,1)S(1)}, u32[]{:S(2)}, u32[]{:S(2)}) collective-permute-start(bf16[64,256]{1,0:T(8,128)(2,1)S(1)} %get-tuple-element.107), channel_id=1, source_target_pairs={{0,1},{1,2},{2,3},{3,4},{4,5},{5,6},{6,7},{7,0},{8,9},{9,10},{10,1... | collective-permute-start | bytes 98312 | tf_op jit(solution)/shard_map/ppermute | solution.py:556
  65.9 7.3 %collective-permute-start.12 = (bf16[2304,256]{1,0:T(8,128)(2,1)S(1)}, bf16[2304,256]{1,0:T(8,128)(2,1)S(1)}, u32[]{:S(2)}, u32[]{:S(2)}) collective-permute-start(bf16[2304,256]{1,0:T(8,128)(2,1)S(1)} %get-tuple-element.61), channel_id=1, source_target_pairs={{0,8},{1,9},{2,10},{3,11},{4,12},{5,13},{6,14},{7,15},{8,0},{9,1},... | collective-permute-start | bytes 3538952 | tf_op jit(solution)/shard_map/ppermute | solution.py:595
  73.9 10.6 %collective-permute-start.13 = (bf16[576,256]{1,0:T(8,128)(2,1)S(1)}, bf16[576,256]{1,0:T(8,128)(2,1)S(1)}, u32[]{:S(2)}, u32[]{:S(2)}) collective-permute-start(bf16[576,256]{1,0:T(8,128)(2,1)S(1)} %get-tuple-element.64), channel_id=1, source_target_pairs={{0,1},{1,2},{2,3},{3,0},{4,5},{5,6},{6,7},{7,4},{8,9},{9,10},{10,1... | collective-permute-start | bytes 884744 | tf_op jit(solution)/shard_map/ppermute | solution.py:595
  74.0 15.2 %collective-permute-start.14 = (bf16[576,256]{1,0:T(8,128)(2,1)S(1)}, bf16[576,256]{1,0:T(8,128)(2,1)S(1)}, u32[]{:S(2)}, u32[]{:S(2)}) collective-permute-start(bf16[576,256]{1,0:T(8,128)(2,1)S(1)} %get-tuple-element.65), channel_id=1, source_target_pairs={{0,3},{1,0},{2,1},{3,2},{4,7},{5,4},{6,5},{7,6},{8,11},{9,8},{10,9... | collective-permute-start | bytes 884744 | tf_op jit(solution)/shard_map/ppermute | solution.py:595
  77.0 14.2 %collective-permute-start.15 = (bf16[576,256]{1,0:T(8,128)(2,1)S(1)}, bf16[576,256]{1,0:T(8,128)(2,1)S(1)}, u32[]{:S(2)}, u32[]{:S(2)}) collective-permute-start(bf16[576,256]{1,0:T(8,128)(2,1)S(1)} %get-tuple-element.66), channel_id=1, source_target_pairs={{0,2},{1,3},{2,0},{3,1},{4,6},{5,7},{6,4},{7,5},{8,10},{9,11},{10,... | collective-permute-start | bytes 884744 | tf_op jit(solution)/shard_map/ppermute | solution.py:595
  78.1 6.5 %collective-permute-start.17 = (bf16[64,256]{1,0:T(8,128)(2,1)S(1)}, bf16[64,256]{1,0:T(8,128)(2,1)S(1)}, u32[]{:S(2)}, u32[]{:S(2)}) collective-permute-start(bf16[64,256]{1,0:T(8,128)(2,1)S(1)} %get-tuple-element.80), channel_id=1, source_target_pairs={{0,120},{8,0},{16,8},{24,16},{32,24},{40,32},{48,40},{56,48},{64,5... | collective-permute-start | bytes 98312 | tf_op jit(solution)/shard_map/ppermute | solution.py:550
  79.0 5.5 %collective-permute-start.16 = (bf16[64,256]{1,0:T(8,128)(2,1)S(1)}, bf16[64,256]{1,0:T(8,128)(2,1)S(1)}, u32[]{:S(2)}, u32[]{:S(2)}) collective-permute-start(bf16[64,256]{1,0:T(8,128)(2,1)S(1)} %get-tuple-element.81), channel_id=1, source_target_pairs={{0,8},{8,16},{16,24},{24,32},{32,40},{40,48},{48,56},{56,64},{64,7... | collective-permute-start | bytes 98312 | tf_op jit(solution)/shard_map/ppermute | solution.py:549
  108.4 9.4 %collective-permute-start.28 = (bf16[144,256]{1,0:T(8,128)(2,1)S(1)}, bf16[144,256]{1,0:T(8,128)(2,1)S(1)}, u32[]{:S(2)}, u32[]{:S(2)}) collective-permute-start(bf16[144,256]{1,0:T(8,128)(2,1)S(1)} %k_x_sum.1.own), channel_id=1, source_target_pairs={{0,64},{1,65},{2,66},{3,67},{4,68},{5,69},{6,70},{7,71},{8,72},{9,... | collective-permute-start | bytes 221192 | tf_op jit(solution)/shard_map/ppermute | solution.py:595
  108.8 9.1 %collective-permute-start.27 = (bf16[144,256]{1,0:T(8,128)(2,1)S(1)}, bf16[144,256]{1,0:T(8,128)(2,1)S(1)}, u32[]{:S(2)}, u32[]{:S(2)}) collective-permute-start(bf16[144,256]{1,0:T(8,128)(2,1)S(1)} %k_x_sum.1.own), channel_id=1, source_target_pairs={{0,32},{1,33},{2,34},{3,35},{4,36},{5,37},{6,38},{7,39},{8,40},{9,... | collective-permute-start | bytes 221192 | tf_op jit(solution)/shard_map/ppermute | solution.py:595
  109.8 8.0 %collective-permute-start.26 = (bf16[144,256]{1,0:T(8,128)(2,1)S(1)}, bf16[144,256]{1,0:T(8,128)(2,1)S(1)}, u32[]{:S(2)}, u32[]{:S(2)}) collective-permute-start(bf16[144,256]{1,0:T(8,128)(2,1)S(1)} %k_x_sum.1.own), channel_id=1, source_target_pairs={{0,96},{1,97},{2,98},{3,99},{4,100},{5,101},{6,102},{7,103},{8,104... | collective-permute-start | bytes 221192 | tf_op jit(solution)/shard_map/ppermute | solution.py:595
  111.5 6.4 %collective-permute-start.18 = (bf16[64,256]{1,0:T(8,128)(2,1)S(1)}, bf16[64,256]{1,0:T(8,128)(2,1)S(1)}, u32[]{:S(2)}, u32[]{:S(2)}) collective-permute-start(bf16[64,256]{1,0:T(8,128)(2,1)S(1)} %get-tuple-element.68), channel_id=1, source_target_pairs={{0,1},{1,2},{2,3},{3,4},{4,5},{5,6},{6,7},{7,0},{8,9},{9,10},{10,1... | collective-permute-start | bytes 98312 | tf_op jit(solution)/shard_map/ppermute | solution.py:556
  112.2 5.7 %collective-permute-start.19 = (bf16[64,256]{1,0:T(8,128)(2,1)S(1)}, bf16[64,256]{1,0:T(8,128)(2,1)S(1)}, u32[]{:S(2)}, u32[]{:S(2)}) collective-permute-start(bf16[64,256]{1,0:T(8,128)(2,1)S(1)} %get-tuple-element.69), channel_id=1, source_target_pairs={{0,7},{1,0},{2,1},{3,2},{4,3},{5,4},{6,5},{7,6},{8,15},{9,8},{10,9... | collective-permute-start | bytes 98312 | tf_op jit(solution)/shard_map/ppermute | solution.py:557
  118.5 10.5 %collective-permute-start.31 = (bf16[576,256]{1,0:T(8,128)(2,1)S(1)}, bf16[576,256]{1,0:T(8,128)(2,1)S(1)}, u32[]{:S(2)}, u32[]{:S(2)}) collective-permute-start(bf16[576,256]{1,0:T(8,128)(2,1)S(1)} %k_join.1.after.a0), channel_id=1, source_target_pairs={{0,2},{1,3},{2,0},{3,1},{4,6},{5,7},{6,4},{7,5},{8,10},{9,11},{10,... | collective-permute-start | bytes 884744 | tf_op jit(solution)/shard_map/ppermute | solution.py:595
  118.6 14.7 %collective-permute-start.30 = (bf16[576,256]{1,0:T(8,128)(2,1)S(1)}, bf16[576,256]{1,0:T(8,128)(2,1)S(1)}, u32[]{:S(2)}, u32[]{:S(2)}) collective-permute-start(bf16[576,256]{1,0:T(8,128)(2,1)S(1)} %k_join.1.after.a0), channel_id=1, source_target_pairs={{0,1},{1,2},{2,3},{3,0},{4,5},{5,6},{6,7},{7,4},{8,9},{9,10},{10,1... | collective-permute-start | bytes 884744 | tf_op jit(solution)/shard_map/ppermute | solution.py:595
  121.6 14.5 %collective-permute-start.29 = (bf16[576,256]{1,0:T(8,128)(2,1)S(1)}, bf16[576,256]{1,0:T(8,128)(2,1)S(1)}, u32[]{:S(2)}, u32[]{:S(2)}) collective-permute-start(bf16[576,256]{1,0:T(8,128)(2,1)S(1)} %k_join.1.after.a0), channel_id=1, source_target_pairs={{0,3},{1,0},{2,1},{3,2},{4,7},{5,4},{6,5},{7,6},{8,11},{9,8},{10,9... | collective-permute-start | bytes 884744 | tf_op jit(solution)/shard_map/ppermute | solution.py:595
  121.6 17.8 %collective-permute-start.32 = (bf16[576,256]{1,0:T(8,128)(2,1)S(1)}, bf16[576,256]{1,0:T(8,128)(2,1)S(1)}, u32[]{:S(2)}, u32[]{:S(2)}) collective-permute-start(bf16[576,256]{1,0:T(8,128)(2,1)S(1)} %k_join.1.after.a0), channel_id=1, source_target_pairs={{0,8},{1,9},{2,10},{3,11},{4,12},{5,13},{6,14},{7,15},{8,0},{9,1},... | collective-permute-start | bytes 884744 | tf_op jit(solution)/shard_map/ppermute | solution.py:595
  129.0 10.5 %collective-permute-start.35 = (bf16[576,256]{1,0:T(8,128)(2,1)S(1)}, bf16[576,256]{1,0:T(8,128)(2,1)S(1)}, u32[]{:S(2)}, u32[]{:S(2)}) collective-permute-start(bf16[576,256]{1,0:T(8,128)(2,1)S(1)} %collective-permute-done.31.a2), channel_id=1, source_target_pairs={{0,8},{1,9},{2,10},{3,11},{4,12},{5,13},{6,14},{7,15},{8,0},{9,1},... | collective-permute-start | bytes 884744 | tf_op jit(solution)/shard_map/ppermute | solution.py:595
  133.2 6.3 %collective-permute-start.34 = (bf16[576,256]{1,0:T(8,128)(2,1)S(1)}, bf16[576,256]{1,0:T(8,128)(2,1)S(1)}, u32[]{:S(2)}, u32[]{:S(2)}) collective-permute-start(bf16[576,256]{1,0:T(8,128)(2,1)S(1)} %collective-permute-done.30.a3), channel_id=1, source_target_pairs={{0,8},{1,9},{2,10},{3,11},{4,12},{5,13},{6,14},{7,15},{8,0},{9,1},... | collective-permute-start | bytes 884744 | tf_op jit(solution)/shard_map/ppermute | solution.py:595
  (19 other events, 107.3 us)

commit v3 on v2

--- a/solution.py
+++ b/solution.py
@@ -14,6 +14,7 @@
 ROWS = 8
 BLK = ROWS * S
 N_BLK = S // ROWS
+HALF = 9 * C // 2
 PK = 64
 F32 = jnp.float32
 BF = jnp.bfloat16
@@ -57,15 +58,36 @@
     return found
 
 
+def slot_at(lat_step, tile_step):
+    return (lat_step + 1) * 3 + tile_step + 1
+
+
+def package_slots(lk):
+    la, ta = lk[24], lk[25]
+    return slot_at(la, 0), slot_at(0, ta), slot_at(0, -ta), slot_at(-la, 0)
+
+
+def package_corners(lk, q):
+    la, ta = lk[24], lk[25]
+    if q == 1:
+        return slot_at(la, ta), slot_at(-la, ta)
+    if q == 2:
+        return slot_at(la, -ta), slot_at(-la, -ta)
+    return ()
+
+
 def corner_home(lk, c):
     d = corner_slot(lk, c)
-    home = jnp.where(d == 0, jnp.int32(S), jnp.int32(S + 1))
-    home = jnp.where(d == 6, jnp.int32(3 * PK + S), home)
-    return jnp.where(d == 8, jnp.int32(3 * PK + S + 1), home)
+    row = jnp.where(d % 3 - 1 == lk[25], jnp.int32(S), jnp.int32(S + 1))
+    return row + jnp.where(d // 3 - 1 == lk[24], jnp.int32(0), jnp.int32(3 * PK))
 
 
 def side_home(lk, s):
-    return (side_slot(lk, s) - 1) // 2 * PK
+    slots = package_slots(lk)
+    home = jnp.int32(3 * PK)
+    for q in range(3):
+        home = jnp.where(side_slot(lk, s) == slots[q], jnp.int32(q * PK), home)
+    return home
 
 
 def grid_of(rows, cols):
@@ -82,18 +104,14 @@
     return jnp.dot(ones_at(hit), rows, preferred_element_type=F32)
 
 
-CORNERS_TO_SEND = {1: (0, 6), 2: (2, 8)}
-
-
 def pack_edges(lk, edges):
     row, col = grid_of(PK, 4 * S)
     at = [jnp.int32(c // 2 * S + c % 2 * (S - 1)) for c in range(4)]
     hits = []
-    for q, slot in enumerate((1, 3, 5, 7)):
+    for q, slot in enumerate(package_slots(lk)):
         want = jnp.where(row < S, side_facing(lk, slot) * S + row, -1)
-        if q in CORNERS_TO_SEND:
-            for k, far in enumerate(CORNERS_TO_SEND[q]):
-                want = jnp.where(row == S + k, corner_facing(lk, far, at), want)
+        for k, far in enumerate(package_corners(lk, q)):
+            want = jnp.where(row == S + k, corner_facing(lk, far, at), want)
         hits.append(col == want)
     return pick(jnp.concatenate(hits, axis=0), edges).astype(BF)
 
@@ -105,12 +123,11 @@
         place = jnp.int32(c // 2 * PK + S + c % 2)
         at.append(jnp.where(corner_keep(lk, c) != 0, place, jnp.int32(-1)))
     hits = []
-    for q, slot in enumerate((1, 3, 5, 7)):
+    for q, slot in enumerate(package_slots(lk)):
         cell = jnp.where(flip_facing(lk, slot) == 1, S - 1 - row, row)
         want = jnp.where(row < S, side_facing(lk, slot) * PK + cell, -1)
-        if q in CORNERS_TO_SEND:
-            for k, far in enumerate(CORNERS_TO_SEND[q]):
-                want = jnp.where(row == S + k, corner_facing(lk, far, at), want)
+        for k, far in enumerate(package_corners(lk, q)):
+            want = jnp.where(row == S + k, corner_facing(lk, far, at), want)
         hits.append(col == want)
     return pick(jnp.concatenate(hits, axis=0), rims).astype(BF)
 
@@ -242,14 +259,18 @@
         frame[to, right * C : (right + 1) * C] = after.astype(BF)
 
 
+def half(i):
+    return pl.ds(pl.multiple_of(i * HALF, HALF), HALF)
+
+
 def block_of(i):
-    return pl.ds(pl.multiple_of(i * BLK, BLK), BLK)
+    return pl.ds(i * BLK, BLK)
 
 
 def conv_block(frame, w, i):
     total = None
     for a in range(3):
-        term = dot(frame[pl.ds(pl.multiple_of(i * BLK + a * S, S), BLK)], w[a])
+        term = dot(frame[pl.ds(i * BLK + a * S, BLK)], w[a])
         total = term if total is None else total + term
     return total
 
@@ -257,7 +278,7 @@
 def back_block(frame, w, i):
     total = None
     for a in range(3):
-        at = pl.ds(pl.multiple_of(i * BLK + (2 - a) * S, S), BLK)
+        at = pl.ds(i * BLK + (2 - a) * S, BLK)
         for b in range(3):
             part = frame[at, b * C : (b + 1) * C]
             term = dot_nt(part, w[a, b * C : (b + 1) * C])
@@ -291,25 +312,45 @@
             store((a * 3 + b) * C, part.astype(BF))
 
 
+def column_of(strip, at):
+    row = lax.broadcasted_iota(jnp.int32, (S, 16, C), 1)
+    return jnp.sum(jnp.where(row == at, strip.astype(F32), 0.0), axis=1).astype(BF)
+
+
 def edges_of(field):
-    def edge_column(at):
-        lo = at // 16 * 16
-        part = field[:, lo : lo + 16, :].astype(F32)
-        row = lax.broadcasted_iota(jnp.int32, (S, 16, C), 1)
-        return jnp.sum(jnp.where(row == at - lo, part, 0.0), axis=1)
-
+    right = column_of(field[:, S - 16 :, :], 15)
     return jnp.concatenate(
-        [field[0], field[S - 1], edge_column(0).astype(BF), edge_column(S - 1).astype(BF)],
-        axis=0,
-    )
-
-
-def k_pack_field(lk, field, pk):
-    pk[...] = pack_edges(lk, edges_of(field))
-
-
-def k_edges(cells, edges):
-    edges[...] = edges_of(cells)
+        [field[0], field[S - 1], column_of(field[:, 0:16, :], 0), right], axis=0
+    )
+
+
+def k_pack_field(at, side, corner, field, pk, links):
+    links[24] = 1 - at[3] % 2 * 2
+    links[25] = 1 - at[4] % 2 * 2
+    for s in range(4):
+        for k in range(3):
+            links[s * 3 + k] = side[s, k]
+            links[12 + s * 3 + k] = corner[s, k]
+    pk[...] = pack_edges(links, edges_of(field))
+
+
+def k_edges(field, after, edges):
+    edges[...] = edges_of(field)
+
+
+def k_second_frame(he, hidden0, frame, xt, x, edges):
+    edges[...] = he[...].astype(F32)
+    x[...] = hidden0[...].astype(F32)
+    put_edges(x, edges)
+    xt[...] = x[...].astype(BF).T
+    spread_columns(x, frame, 0, 2)
+
+
+def k_delta_frame(de, delta0, frame, x, edges):
+    edges[...] = de[...].astype(F32)
+    x[...] = delta0[...].astype(F32)
+    put_edges(x, edges)
+    spread_columns(x, frame, 2, 0)
 
 
 def k_first(field, w, after, hidden, slope, e0, xt, x, frame):
@@ -317,14 +358,13 @@
     xt[...] = field[...].T
     spread_columns(x, frame, 0, 2)
 
-    @pl.loop(0, N_BLK)
-    def _(i):
-        at = block_of(i)
+    for i in range(N_BLK):
+        to = block_of(i)
         z = conv_block(frame, w, i)
-        x[at] = z
+        x[to] = z
         value, grad = gelu_both(z)
-        hidden[at] = value.astype(BF)
-        slope[at] = grad
+        hidden[to] = value.astype(BF)
+        slope[to] = grad
 
     take_edges(x, e0)
 
@@ -344,21 +384,14 @@
     pk[...] = pack_edges(lk, value.astype(BF))
 
 
-def k_second(he, hidden0, cot, w, after, xt, mixed, delta, e0, x, frame, edges):
-    edges[...] = he[...].astype(F32)
-    x[...] = hidden0[...].astype(F32)
-    put_edges(x, edges)
-    xt[...] = x[...].astype(BF).T
-    spread_columns(x, frame, 0, 2)
-
-    @pl.loop(0, N_BLK)
-    def _(i):
-        at = block_of(i)
+def k_second(frame, cot, w, after, mixed, delta, e0, x):
+    for i in range(N_BLK):
+        to = block_of(i)
         z = conv_block(frame, w, i)
-        x[at] = z
+        x[to] = z
         value, grad = gelu_both(z)
-        mixed[at] = value.astype(BF)
-        delta[at] = (cot[at].astype(F32) * grad).astype(BF)
+        mixed[to] = value.astype(BF)
+        delta[to] = (cot[to].astype(F32) * grad).astype(BF)
 
     take_edges(x, e0)
 
@@ -376,26 +409,22 @@
 
 
 def k_second_back(
-    de, halo, delta0, w, xt, slope, after, total, fd, e0, x, frame, edges
+    at, de, halo, frame, w, xt, slope, after, keep, send, fd, e0, x, tv
 ):
-    edges[...] = de[...].astype(F32)
-    x[...] = delta0[...].astype(F32)
-    put_edges(x, edges)
-    spread_columns(x, frame, 2, 0)
-
-    @pl.loop(0, N_BLK)
-    def _(i):
-        at = block_of(i)
+    for i in range(N_BLK):
+        to = block_of(i)
         g = back_block(frame, w, i)
-        x[at] = g
-        fd[at] = (g * slope[at]).astype(BF)
+        x[to] = g
+        fd[to] = (g * slope[to]).astype(BF)
 
     take_edges(x, e0)
 
     def store(row, part):
-        total[pl.ds(row, C)] = part
+        tv[pl.ds(row, C)] = part
 
     weight_sums(xt, frame, halo, de, store)
+    keep[...] = tv[half(at[0])]
+    send[...] = tv[half(1 - at[0])]
 
 
 def k_first_delta_edges(lk, up, left, right, down, e0, slope, w, delta, pk):
@@ -406,7 +435,7 @@
     pk[...] = pack_rims(lk, rims_of(edges, w))
 
 
-def k_first_total(at, de, halo, delta0, xt, other, keep, send, x, frame, edges, tv):
+def k_first_total(at, de, halo, delta0, xt, keep, send, x, frame, edges, tv):
     edges[...] = de[...].astype(F32)
     x[...] = delta0[...].astype(F32)
     put_edges(x, edges)
@@ -416,9 +445,8 @@
         tv[pl.ds(row, C)] = part
 
     weight_sums(xt, frame, halo, de, store)
-    here = at[0] == 0
-    keep[...] = jnp.where(here, tv[...], other[...])
-    send[...] = jnp.where(here, other[...], tv[...])
+    keep[...] = tv[half(at[0])]
+    send[...] = tv[half(1 - at[0])]
 
 
 def k_input_middle(de, delta0, w, after, out, x, frame, edges):
@@ -427,12 +455,11 @@
     put_edges(x, edges)
     spread_columns(x, frame, 2, 0)
 
-    @pl.loop(0, N_BLK)
-    def _(i):
+    for i in range(N_BLK):
         out[block_of(i)] = back_block(frame, w, i)
 
 
-def k_input_grad(lk, up, left, right, down, middle, mixed0, me, after, out, mixed, x, edges):
+def k_input_grad(lk, up, left, right, down, middle, mixed0, me, after, out, mixed, token, x, edges):
     adds = cross(rim_adds(lk, join((up, left, right, down))))
     x[...] = middle[...]
     take_edges(x, edges)
@@ -443,20 +470,23 @@
     edges[...] = me[...].astype(F32)
     put_edges(x, edges)
     mixed[...] = x[...].astype(BF)
+    token[...] = jnp.zeros_like(token)
 
 
 STEPS = (0, 1, 3, 2)
 
 
 def quarter(place, step, rows):
-    return pl.ds(pl.multiple_of((place + step) % 4 * rows, 16), rows)
-
-
-def k_core_sum(at, keep, got, pk, own, s1, s3, s2, pk_out):
-    rows = own.shape[0]
+    return pl.ds(pl.multiple_of((place ^ step) * rows, 16), rows)
+
+
+def k_core_sum(at, keep1, got1, keep2, got2, pk, own, s1, s3, s2, pk_out):
+    rows = own.shape[0] // 2
     for step, out in zip(STEPS, (own, s1, s3, s2)):
         part = quarter(at[1], step, rows)
-        out[...] = (keep[part].astype(F32) + got[part].astype(F32)).astype(out.dtype)
+        for k, (keep, got) in enumerate(((keep1, got1), (keep2, got2))):
+            total = keep[part].astype(F32) + got[part].astype(F32)
+            out[pl.ds(k * rows, rows)] = total.astype(out.dtype)
     pk_out[...] = pk[...]
 
 
@@ -475,7 +505,7 @@
     return jnp.where(row == S + 1, right[S + k : S + k + 1].astype(F32), out).astype(BF)
 
 
-def k_y_sum(own, g1, g3, g2, out):
+def k_y_sum(own, g1, g3, g2, up, down, out):
     total = (own[...] + g2[...].astype(F32)) + (g1[...].astype(F32) + g3[...].astype(F32))
     out[...] = total.astype(BF)
 
@@ -487,49 +517,59 @@
     out[...] = (total * scale).astype(BF)
 
 
-def k_join(at, own, g1, g3, g2, up, down, out):
+def k_join(at, own, g1, g3, g2, after, out):
     rows = own.shape[0]
     for step, part in zip(STEPS, (own, g1, g3, g2)):
         out[quarter(at[2], step, rows)] = part[...]
 
 
-def k_unpack(at, a0, a1, a3, a2, b0, b1, b3, b2, after, first, second):
-    rows = a0.shape[0]
-    here = at[0] == 0
-    for step, a, b in zip(STEPS, (a0, a1, a3, a2), (b0, b1, b3, b2)):
-        part = quarter(at[1], step, rows)
-
-        @pl.when(here)
-        def _():
-            first[part] = a[...].astype(F32)
-            second[part] = b[...].astype(F32)
-
-        @pl.when(jnp.logical_not(here))
-        def _():
-            first[part] = b[...].astype(F32)
-            second[part] = a[...].astype(F32)
+def unpack(core, at, parts, first, second, buf, sems):
+    rows = HALF // 4
+    copies = []
+    for q, (step, part) in enumerate(zip(STEPS, parts)):
+        place = core * HALF + (at[1] ^ step) * rows
+        to = pl.ds(pl.multiple_of(place, 16), rows)
+        buf[q] = part[...].astype(F32)
+        for k, out in enumerate((first, second)):
+            copy = pltpu.make_async_copy(
+                buf.at[q, pl.ds(k * rows, rows)], out.at[to], sems.at[2 * q + k]
+            )
+            copy.start()
+            copies.append(copy)
+    for copy in copies:
+        copy.wait()
+
+
+def k_unpack_own(at, a0, a1, a3, a2, after, first, second, buf, sems):
+    unpack(at[0], at, (a0, a1, a3, a2), first, second, buf, sems)
+
+
+def k_unpack_other(at, b0, b1, b3, b2, first_in, second_in, first, second, buf, sems):
+    unpack(1 - at[0], at, (b0, b1, b3, b2), first, second, buf, sems)
 
 
 VMEM = pl.BlockSpec(memory_space=pltpu.VMEM)
 SMEM = pl.BlockSpec(memory_space=pltpu.SMEM)
 ANY = pl.BlockSpec(memory_space=pl.ANY)
+HBM = pl.BlockSpec(memory_space=pltpu.HBM)
 CELL_BF = pltpu.VMEM((CELLS, C), BF)
 WIDE = [pltpu.VMEM((CELLS, C), F32), pltpu.VMEM((CELLS + 2 * S, 3 * C), BF)]
 WIDER = WIDE + [pltpu.VMEM((4 * S, C), F32)]
 
 
-def call(kernel, args, outs, scratch=(), links=None, flops=0, after=(), limit=8):
-    given = ([links] if links is not None else []) + [*args, *after]
+def call(kernel, args, outs, scratch=(), links=None, flops=0, after=(), limit=8, hbm=(), alias=None, out_specs=None):
+    given = ([links] if links is not None else []) + [*args, *hbm, *after]
     specs = ([SMEM] if links is not None else []) + [VMEM] * len(args)
-    specs += [ANY] * len(after)
-    name = getattr(kernel, "__name__", "k_x_sum")
+    specs += [HBM] * len(hbm) + [ANY] * len(after)
+    name = getattr(kernel, "__name__", None) or kernel.func.__name__
     return pl.pallas_call(
         kernel,
         out_shape=[
             (pltpu.VMEM if len(out) > 2 else jax.ShapeDtypeStruct)(out[0], out[1]) for out in outs
         ],
         in_specs=specs,
-        out_specs=[VMEM] * len(outs),
+        out_specs=out_specs or [VMEM] * len(outs),
+        input_output_aliases=alias or {},
         scratch_shapes=list(scratch),
         compiler_params=pltpu.CompilerParams(vmem_limit_bytes=limit * MIB),
         cost_estimate=pl.CostEstimate(
@@ -539,76 +579,74 @@
     )(*given)
 
 
-def ring(count, step):
-    return [(i, (i + step) % count) for i in range(count)]
+def pairs_a(count):
+    return [(i, i ^ 1) for i in range(count)]
+
+
+def pairs_b(count):
+    return [(i, (i + 1 if i % 2 else i - 1) % count) for i in range(count)]
 
 
 def trade_tile(pk):
-    n_tile = lax.axis_size("tile")
-    left, right = pk[PK : 2 * PK], pk[2 * PK : 3 * PK]
-    from_left = lax.ppermute(right, "tile", ring(n_tile, 1))
-    from_right = lax.ppermute(left, "tile", ring(n_tile, -1))
-    return from_left, from_right
-
-
-def trade_lat(up, down):
-    n_lat = lax.axis_size("lat")
-    from_up = lax.ppermute(down, "lat", ring(n_lat, 1))
-    from_down = lax.ppermute(up, "lat", ring(n_lat, -1))
-    return from_up, from_down
+    n = lax.axis_size("tile")
+    from_a = lax.ppermute(pk[PK : 2 * PK], "tile", pairs_a(n))
+    from_b = lax.ppermute(pk[2 * PK : 3 * PK], "tile", pairs_b(n))
+    return from_a, from_b
+
+
+def trade_lat(to_a, to_b):
+    n = lax.axis_size("lat")
+    return lax.ppermute(to_a, "lat", pairs_a(n)), lax.ppermute(to_b, "lat", pairs_b(n))
 
 
 def trade(pk):
-    from_left, from_right = trade_tile(pk)
-    up, down = pk[:PK], pk[3 * PK :]
+    tile_a, tile_b = trade_tile(pk)
     filler = jnp.zeros((PK - S - 2, C), BF)
-    up = jnp.concatenate(
-        [up[:S], from_left[S : S + 1], from_right[S : S + 1], filler], axis=0
-    )
-    down = jnp.concatenate(
-        [down[:S], from_left[S + 1 : S + 2], from_right[S + 1 : S + 2], filler], axis=0
-    )
-    from_up, from_down = trade_lat(up, down)
-    return from_up, from_left, from_right, from_down
-
-
-def group_ring(kind, step):
+
+    def with_cells(edge, k):
+        cells = [tile_a[S + k : S + k + 1], tile_b[S + k : S + k + 1]]
+        return jnp.concatenate([edge[:S], *cells, filler], axis=0)
+
+    lat_a, lat_b = trade_lat(with_cells(pk[:PK], 0), with_cells(pk[3 * PK :], 1))
+    return lat_a, tile_a, tile_b, lat_b
+
+
+def exchange(kind, step):
     pairs = []
     for t in range(16):
         for l in range(8):
             y, xl, c, xh, z = t // 4, t // 2 % 2, t % 2, l // 4, l % 4
             x = xh * 2 + xl
             if kind == "core":
-                c = (c + step) % 2
+                c ^= step
             elif kind == "z":
-                z = (z + step) % 4
+                z ^= step
             elif kind == "y":
-                y = (y + step) % 4
+                y ^= step
             else:
-                x = (x + step) % 4
+                x ^= step
             to = (y * 4 + x % 2 * 2 + c) * 8 + x // 2 * 4 + z
             pairs.append((t * 8 + l, to))
     return pairs
 
 
 def move(x, kind, step):
-    return lax.ppermute(x, ("tile", "lat"), group_ring(kind, step))
+    return lax.ppermute(x, ("tile", "lat"), exchange(kind, step))
 
 
 def moves(parts, kind):
-    return [move(part, kind, step) for part, step in zip(parts, (1, 3, 2))]
+    return [move(part, kind, step) for part, step in zip(parts, STEPS[1:])]
 
 
 def gathers(part, kind):
-    return [move(part, kind, 4 - step) for step in (1, 3, 2)]
+    return [move(part, kind, step) for step in STEPS[1:]]
 
 
 def shards(field, cotangent, first_weight, second_weight, side_links, corner_links):
     lat_at = lax.axis_index("lat")
     lon_at = lax.axis_index("tile")
-    lk = jnp.concatenate(
-        [side_links[lat_at, lon_at].reshape(12), corner_links[lat_at, lon_at].reshape(12)]
-    )
+    core, z_at, y_at = lon_at % 2, lat_at % 4, lon_at // 4
+    at = jnp.stack([core, z_at, y_at, lat_at, lon_at]).astype(jnp.int32)
     w1 = first_weight.reshape(3, 3 * C, C)
     w2 = second_weight.reshape(3, 3 * C, C)
     cells = field.reshape(CELLS, C)
@@ -621,9 +659,21 @@
     far_bf, far_f32 = ((CELLS, C), BF, 1), ((CELLS, C), F32, 1)
     far_turned = ((C, CELLS), BF, 1)
 
-    (pk,) = call(k_pack_field, [field], [packs], links=lk)
+    frame_bf = ((CELLS + 2 * S, 3 * C), BF, 1)
+    half_bf = ((HALF, C), BF)
+
+    own_side = side_links[lat_at, lon_at]
+    own_corner = corner_links[lat_at, lon_at]
+    pk, lk = pl.pallas_call(
+        k_pack_field,
+        out_shape=[jax.ShapeDtypeStruct(*packs), jax.ShapeDtypeStruct((26,), jnp.int32)],
+        in_specs=[SMEM, SMEM, SMEM, VMEM],
+        out_specs=[VMEM, SMEM],
+        compiler_params=pltpu.CompilerParams(vmem_limit_bytes=8 * MIB),
+        name="k_pack_field",
+    )(at, own_side, own_corner, field)
     got = trade(pk)
-    (cot_e,) = call(k_edges, [cotangent], [edge_bf])
+    (cot_e,) = call(k_edges, [cotangent], [edge_bf], after=[got[1]])
     hidden0, slope0, e0, xt1 = call(
         k_first,
         [cells, w1],
@@ -631,52 +681,59 @@
         WIDE,
         after=[got[1]],
         flops=work,
-        limit=20,
+        limit=18,
     )
     halo1, slope_e, hidden_e, pk = call(
         k_first_edges, [*got, e0, w1], [halo_bf, edge_f32, edge_bf, packs], links=lk
     )
     got = trade(pk)
-    xt2, mixed0, delta0, e0 = call(
+    frame, xt2 = call(
+        k_second_frame, [hidden_e, hidden0], [frame_bf, far_turned], [WIDE[0], WIDER[2]], limit=14
+    )
+    mixed0, delta0, e0 = call(
         k_second,
-        [hidden_e, hidden0, cot, w2],
-        [far_turned, far_bf, far_bf, edge_f32],
-        WIDER,
+        [frame, cot, w2],
+        [far_bf, far_bf, edge_f32],
+        WIDE[:1],
         after=[got[1]],
         flops=work,
-        limit=20,
+        limit=18,
     )
     halo2, mixed_e, delta_e, pk = call(
         k_second_edges, [*got, e0, cot_e, w2], [halo_bf, edge_bf, edge_bf, packs], links=lk
     )
     got = trade(pk)
-    total2, fd0, e0 = call(
+    (frame,) = call(
+        k_delta_frame, [delta_e, delta0], [frame_bf], [WIDE[0], WIDER[2]], limit=12
+    )
+    keep2, send2, fd0, e0 = call(
         k_second_back,
-        [delta_e, halo2, delta0, w2, xt2, slope0],
-        [far_bf, far_bf, edge_f32],
-        WIDER,
+        [delta_e, halo2, frame, w2, xt2, slope0],
+        [half_bf, half_bf, far_bf, edge_f32],
+        [WIDE[0], CELL_BF],
+        links=at,
         after=[got[1]],
         flops=2 * work,
         limit=22,
     )
+    got2 = move(send2, "core", 1)
     fd_e, pk = call(
         k_first_delta_edges, [*got, e0, slope_e, w1], [edge_bf, packs], links=lk
     )
-    core, z_at, y_at = lon_at % 2, lat_at % 4, lon_at // 4
-    at = jnp.stack([core, z_at, y_at]).astype(jnp.int32)
-    rows_z, rows_y = CELLS // 4, CELLS // 16
-    keep, send = call(
+    keep1, send1 = call(
         k_first_total,
-        [fd_e, halo1, fd0, xt1, total2],
-        [cell_bf, cell_bf],
+        [fd_e, halo1, fd0, xt1],
+        [half_bf, half_bf],
         WIDER + [CELL_BF],
         links=at,
         flops=work,
         limit=20,
     )
+    got1 = move(send1, "core", 1)
+    rows_z, rows_y = CELLS // 4, CELLS // 16
     quad_z = [((rows_z, C), F32)] + [((rows_z, C), BF)] * 3
     own, *parts, pk = call(
-        k_core_sum, [keep, move(send, "core", 1), pk], quad_z + [packs], links=at
+        k_core_sum, [keep1, got1, keep2, got2, pk], quad_z + [packs], links=at
     )
     left, right = trade_tile(pk)
     (middle,) = call(
@@ -694,27 +751,39 @@
     )
     up, down = trade_lat(up, down)
     piece_bf = ((rows_y, C), BF)
-    (part,) = call(k_y_sum, [own, *moves(parts, "y")], [piece_bf])
-    root = math.sqrt(CELLS * lax.axis_size("lat") * lax.axis_size("tile"))
-    (part,) = call(
-        functools.partial(k_x_sum, 1.0 / root), [part, *moves([part] * 3, "x")], [piece_bf]
-    )
-    (part,) = call(
-        k_join, [part, *gathers(part, "y")], [((rows_z, C), BF)], links=at, after=[up, down]
-    )
-    parts = [part, *gathers(part, "z")]
-    grad, mixed = call(
+    (part,) = call(k_y_sum, [own, *moves(parts, "y")], [piece_bf], after=[up, down])
+    grad, mixed, token = call(
         k_input_grad,
         [up, left, right, down, middle, mixed0, mixed_e],
-        [cell_bf, cell_bf],
+        [cell_bf, cell_bf, ((8, 128), F32)],
         [WIDE[0], WIDER[2]],
         links=lk,
         after=[part],
         limit=16,
     )
+    root = math.sqrt(CELLS * lax.axis_size("lat") * lax.axis_size("tile"))
+    (part,) = call(
+        functools.partial(k_x_sum, 1.0 / root), [part, *moves([part] * 3, "x")], [piece_bf]
+    )
+    (part,) = call(
+        k_join, [part, *gathers(part, "y")], [((rows_z, C), BF)], links=at, after=[token]
+    )
+    parts = [part, *gathers(part, "z")]
     others = [move(part, "core", 1) for part in parts]
+    buffers = [pltpu.VMEM((4, rows_z, C), F32), pltpu.SemaphoreType.DMA((8,))]
+    sums = call(
+        k_unpack_own, parts, [cell_f32, cell_f32], buffers, links=at, out_specs=[HBM, HBM],
+        after=[parts[0]],
+    )
     first, second = call(
-        k_unpack, [*parts, *others], [cell_f32, cell_f32], links=at, after=[grad], limit=12
+        k_unpack_other,
+        others,
+        [cell_f32, cell_f32],
+        buffers,
+        links=at,
+        hbm=sums,
+        alias={5: 0, 6: 1},
+        out_specs=[HBM, HBM],
     )
     return (
         mixed.reshape(S, S, C),

time: 144 us -> 129 us (0.90)
  starting transfers between devices: 68.5 us -> 56.8 us
    ppermute x36 -> x37, starting transfers between devices: 68.5 us -> 56.8 us  [the longest x21 32.7 us: move(): return lax.ppermute(x, ('tile', 'lat'), exchange(kind, step))]
    pallas_call x17 -> x19, Pallas kernels: 43 us -> 40.2 us  [call(): pl.pallas_call(kernel, out_shape=[(pltpu.VMEM if len(out) > 2 else jax.Sh...]
    pallas_call x0 -> x1, Pallas kernels: none -> 1.48 us  [shards(): pl.pallas_call(k_pack_field, out_shape=[jax.ShapeDtypeStruct(*packs), jax...]
    unnamed x14 -> x10, local copies, waits for them, and re-layouts: 3.84 us -> 2.56 us
    ppermute x36 -> x37, waiting for transfers between devices: 25.8 us -> 25.4 us  [the longest x21 14.6 us: move(): return lax.ppermute(x, ('tile', 'lat'), exchange(kind, step))]
  transfers between devices with their start and end apart: 36 -> 37, of which waited for: 16 -> 12; matrix products, arithmetic and copies ran while one was open for 0% -> 0% of each run, Pallas kernels for 18% -> 25%
where the time goes in v3:
time: 129 us
  starting transfers between devices  56.8 us (44%)
  Pallas kernels  41.7 us (32%)
  waiting for transfers between devices  25.4 us (20%)
  local copies, waits for them, and re-layouts  3.9 us (3%)
    pallas_call x19, Pallas kernels, call(): pl.pallas_call(kernel, out_shape=[(pltpu.VMEM if len(out) > 2 else jax.Sh...  40.2 us
    ppermute x21, starting transfers between devices, move(): return lax.ppermute(x, ('tile', 'lat'), exchange(kind, step))  32.7 us
    ppermute x21, waiting for transfers between devices, move(): return lax.ppermute(x, ('tile', 'lat'), exchange(kind, step))  14.6 us
    ppermute x4, starting transfers between devices, trade_lat(): lax.ppermute(to_b, 'lat', pairs_b(n))  12.8 us
    ppermute x4, starting transfers between devices, trade_tile(): from_a = lax.ppermute(pk[PK:2 * PK], 'tile', pairs_a(n))  9.39 us
    ppermute x4, waiting for transfers between devices, trade_tile(): from_b = lax.ppermute(pk[2 * PK:3 * PK], 'tile', pairs_b(n))  6.8 us
    ppermute x4, waiting for transfers between devices, trade_lat(): lax.ppermute(to_b, 'lat', pairs_b(n))  3.9 us
  transfers between devices with their start and end apart: 37, of which 12 were waited for; matrix products, arithmetic and copies ran while one was open for 0% of the time, Pallas kernels for 25%

profile of v3, /device:TPU:1, one launch (start us, length us, event | category | flops | bytes accessed | tf_op | source)
XLA Modules:
  0.0 129.2 jit_solution(1354637506343508675)
XLA Ops:
  9.6 6.4 %collective-permute-start.3 = (bf16[64,256]{1,0:T(8,128)(2,1)S(1)}, bf16[64,256]{1,0:T(8,128)(2,1)S(1)}, u32[]{:S(2)}, u32[]{:S(2)}) collective-permute-start(bf16[64,256]{1,0:T(8,128)(2,1)S(1)} %get-tuple-element.124), channel_id=1, source_target_pairs={{0,7},{1,2},{2,1},{3,4},{4,3},{5,6},{6,5},{7,0},{8,15},{9,10},{10,... | collective-permute-start | bytes 98312 | tf_op jit(solution)/shard_map/ppermute | solution.py:599
  17.2 4.5 %k_first.1 = (bf16[2304,256]{1,0:T(8,128)(2,1)S(1)}, f32[2304,256]{1,0:T(8,128)S(1)}, f32[192,256]{1,0:T(8,128)S(1)}, bf16[256,2304]{1,0:T(8,128)(2,1)S(1)}) custom-call(bf16[2304,256]{1,0:T(8,128)(2,1)S(1)} %bitcast.20, bf16[3,768,256]{2,1,0:T(8,128)(2,1)S(1)} %bitcast.15, bf16[64,256]{1,0:T(8,128)(2,1)S(1)} %collective-permute-done.after.left), custom_call_target="tpu_custom_call" | custom-call | flops 2717908992 | bytes 4194304 | tf_op jit(solution)/shard_map/k_first/pallas_call | solution.py:565
  23.5 2.6 %collective-permute-start.4 = (bf16[64,256]{1,0:T(8,128)(2,1)S(1)}, bf16[64,256]{1,0:T(8,128)(2,1)S(1)}, u32[]{:S(2)}, u32[]{:S(2)}) collective-permute-start(bf16[64,256]{1,0:T(8,128)(2,1)S(1)} %get-tuple-element.102), channel_id=1, source_target_pairs={{0,8},{8,0},{16,24},{24,16},{32,40},{40,32},{48,56},{56,48},{64,72... | collective-permute-start | bytes 98312 | tf_op jit(solution)/shard_map/ppermute | solution.py:592
  27.1 2.4 %collective-permute-done.5.right = bf16[64,256]{1,0:T(8,128)(2,1)S(1)} collective-permute-done((bf16[64,256]{1,0:T(8,128)(2,1)S(1)}, bf16[64,256]{1,0:T(8,128)(2,1)S(1)}, u32[]{:S(2)}, u32[]{:S(2)}) %collective-permute-start.5) | collective-permute-done | bytes 32800 | tf_op jit(solution)/shard_map/ppermute | solution.py:593
  31.5 3.7 %k_second.1 = (bf16[2304,256]{1,0:T(8,128)(2,1)S(1)}, bf16[2304,256]{1,0:T(8,128)(2,1)S(1)}, f32[192,256]{1,0:T(8,128)S(1)}) custom-call(bf16[2400,768]{1,0:T(8,128)(2,1)S(1)} %get-tuple-element.55.frame, bf16[2304,256]{1,0:T(8,128)(2,1)S(1)} %bitcast.19, bf16[3,768,256]{2,1,0:T(8,128)(2,1)S(1)} %bitcast.21, ...), custom_call_target="tpu_custom_call" | custom-call | flops 2717908992 | bytes 4194304 | tf_op jit(solution)/shard_map/k_second/pallas_call | solution.py:565
  36.0 2.4 %k_second_edges.1 = (bf16[192,768]{1,0:T(8,128)(2,1)S(1)}, bf16[192,256]{1,0:T(8,128)(2,1)S(1)}, bf16[192,256]{1,0:T(8,128)(2,1)S(1)}, bf16[256,256]{1,0:T(8,128)(2,1)S(1)}) custom-call(s32[26]{0:T(128)S(1)} %get-tuple-element.49.lk, bf16[64,256]{1,0:T(8,128)(2,1)S(1)} %collective-permute-done.6.up, bf16[64,256]{1,0:T(8,128)(2,1)S(1)} %collective-permute-done.4.after.left, ...), custom_call_target="tpu_custom_call" | custom-call | bytes 4194304 | tf_op jit(solution)/shard_map/k_second_edges/pallas_call | solution.py:565
  38.4 3.7 %collective-permute-start.8 = (bf16[64,256]{1,0:T(8,128)(2,1)S(1)}, bf16[64,256]{1,0:T(8,128)(2,1)S(1)}, u32[]{:S(2)}, u32[]{:S(2)}) collective-permute-start(bf16[64,256]{1,0:T(8,128)(2,1)S(1)} %get-tuple-element.98), channel_id=1, source_target_pairs={{0,8},{8,0},{16,24},{24,16},{32,40},{40,32},{48,56},{56,48},{64,72... | collective-permute-start | bytes 98312 | tf_op jit(solution)/shard_map/ppermute | solution.py:592
  43.0 2.5 %collective-permute-done.9.right = bf16[64,256]{1,0:T(8,128)(2,1)S(1)} collective-permute-done((bf16[64,256]{1,0:T(8,128)(2,1)S(1)}, bf16[64,256]{1,0:T(8,128)(2,1)S(1)}, u32[]{:S(2)}, u32[]{:S(2)}) %collective-permute-start.9) | collective-permute-done | bytes 32800 | tf_op jit(solution)/shard_map/ppermute | solution.py:593
  47.4 6.9 %k_second_back.1 = (bf16[1152,256]{1,0:T(8,128)(2,1)S(1)}, bf16[1152,256]{1,0:T(8,128)(2,1)S(1)}, bf16[2304,256]{1,0:T(8,128)(2,1)S(1)}, f32[192,256]{1,0:T(8,128)S(1)}) custom-call(s32[5]{0:T(128)S(1)} %stack.23.at, bf16[192,256]{1,0:T(8,128)(2,1)S(1)} %get-tuple-element.58.de, bf16[192,768]{1,0:T(8,128)(2,1)S(1)} %get-tuple-element.59.halo, ...), custom_call_target="tpu_custom_call" | custom-call | flops 5435817984 | bytes 4194304 | tf_op jit(solution)/shard_map/k_second_back/pallas_call | solution.py:565
  54.3 2.8 %collective-permute-start.13 = (bf16[1152,256]{1,0:T(8,128)(2,1)S(1)}, bf16[1152,256]{1,0:T(8,128)(2,1)S(1)}, u32[]{:S(2)}, u32[]{:S(2)}) collective-permute-start(bf16[1152,256]{1,0:T(8,128)(2,1)S(1)} %get-tuple-element.72), channel_id=1, source_target_pairs={{0,8},{1,9},{2,10},{3,11},{4,12},{5,13},{6,14},{7,15},{8,0},{9,1},... | collective-permute-start | bytes 1769480 | tf_op jit(solution)/shard_map/ppermute | solution.py:634
  59.0 4.8 %k_first_total.1 = (bf16[1152,256]{1,0:T(8,128)(2,1)S(1)}, bf16[1152,256]{1,0:T(8,128)(2,1)S(1)}) custom-call(s32[5]{0:T(128)S(1)} %stack.23.at, bf16[192,256]{1,0:T(8,128)(2,1)S(1)} %get-tuple-element.65.de, bf16[192,768]{1,0:T(8,128)(2,1)S(1)} %get-tuple-element.66.halo, bf16[2304,256]{1,0:T(8,128)(2,1)S(1)} %get-tuple-element.67.delta0, ...), custom_call_target="tpu_custom_call" | custom-call | flops 2717908992 | bytes 4194304 | tf_op jit(solution)/shard_map/k_first_total/pallas_call | solution.py:565
  72.0 3.7 %k_input_middle.1.after.middle = f32[2304,256]{1,0:T(8,128)S(1)} custom-call(bf16[192,256]{1,0:T(8,128)(2,1)S(1)} %get-tuple-element.65.de, bf16[2304,256]{1,0:T(8,128)(2,1)S(1)} %get-tuple-element.67.delta0, bf16[3,768,256]{2,1,0:T(8,128)(2,1)S(1)} %bitcast.18, f32[576,256]{1,0:T(8,128)S(1)} %get-tuple-element.74.after.own), custom_call_target="tpu_custom_call" | custom-call | flops 2717908992 | bytes 4194304 | tf_op jit(solution)/shard_map/k_input_middle/pallas_call | solution.py:565
  75.7 8.4 %collective-permute-done.15.g3 = bf16[576,256]{1,0:T(8,128)(2,1)S(1)} collective-permute-done((bf16[576,256]{1,0:T(8,128)(2,1)S(1)}, bf16[576,256]{1,0:T(8,128)(2,1)S(1)}, u32[]{:S(2)}, u32[]{:S(2)}) %collective-permute-start.15) | collective-permute-done | bytes 294944 | tf_op jit(solution)/shard_map/ppermute | solution.py:634
  85.2 3.1 %collective-permute-start.23 = (bf16[144,256]{1,0:T(8,128)(2,1)S(1)}, bf16[144,256]{1,0:T(8,128)(2,1)S(1)}, u32[]{:S(2)}, u32[]{:S(2)}) collective-permute-start(bf16[144,256]{1,0:T(8,128)(2,1)S(1)} %get-tuple-element.86), channel_id=1, source_target_pairs={{0,64},{1,65},{2,66},{3,67},{4,68},{5,69},{6,70},{7,71},{8,72},{9,... | collective-permute-start | bytes 221192 | tf_op jit(solution)/shard_map/ppermute | solution.py:634
  88.3 3.3 %collective-permute-start.20 = (bf16[64,256]{1,0:T(8,128)(2,1)S(1)}, bf16[64,256]{1,0:T(8,128)(2,1)S(1)}, u32[]{:S(2)}, u32[]{:S(2)}) collective-permute-start(bf16[64,256]{1,0:T(8,128)(2,1)S(1)} %get-tuple-element.80), channel_id=1, source_target_pairs={{0,7},{1,2},{2,1},{3,4},{4,3},{5,6},{6,5},{7,0},{8,15},{9,10},{10,... | collective-permute-start | bytes 98312 | tf_op jit(solution)/shard_map/ppermute | solution.py:599
  91.7 3.0 %collective-permute-done.20.down = bf16[64,256]{1,0:T(8,128)(2,1)S(1)} collective-permute-done((bf16[64,256]{1,0:T(8,128)(2,1)S(1)}, bf16[64,256]{1,0:T(8,128)(2,1)S(1)}, u32[]{:S(2)}, u32[]{:S(2)}) %collective-permute-start.20) | collective-permute-done | bytes 32800 | tf_op jit(solution)/shard_map/ppermute | solution.py:599
  97.5 2.1 %collective-permute-done.26.g2 = bf16[144,256]{1,0:T(8,128)(2,1)S(1)} collective-permute-done((bf16[144,256]{1,0:T(8,128)(2,1)S(1)}, bf16[144,256]{1,0:T(8,128)(2,1)S(1)}, u32[]{:S(2)}, u32[]{:S(2)}) %collective-permute-start.26) | collective-permute-done | bytes 73760 | tf_op jit(solution)/shard_map/ppermute | solution.py:634
  101.6 2.1 %collective-permute-start.28 = (bf16[144,256]{1,0:T(8,128)(2,1)S(1)}, bf16[144,256]{1,0:T(8,128)(2,1)S(1)}, u32[]{:S(2)}, u32[]{:S(2)}) collective-permute-start(bf16[144,256]{1,0:T(8,128)(2,1)S(1)} %k_x_sum.1.own), channel_id=1, source_target_pairs={{0,96},{1,97},{2,98},{3,99},{4,100},{5,101},{6,102},{7,103},{8,104... | collective-permute-start | bytes 221192 | tf_op jit(solution)/shard_map/ppermute | solution.py:634
  103.9 2.5 %k_input_grad.1 = (bf16[2304,256]{1,0:T(8,128)(2,1)}, bf16[2304,256]{1,0:T(8,128)(2,1)}, f32[8,128]{1,0:T(8,128)S(1)}) custom-call(s32[26]{0:T(128)S(1)} %get-tuple-element.49.lk, bf16[64,256]{1,0:T(8,128)(2,1)S(1)} %collective-permute-done.19.up, bf16[64,256]{1,0:T(8,128)(2,1)S(1)} %collective-permute-done.17.left, ...), custom_call_target="tpu_custom_call" | custom-call | bytes 4194304 | tf_op jit(solution)/shard_map/k_input_grad/pallas_call | solution.py:565
  110.2 6.9 %collective-permute-start.30 = (bf16[576,256]{1,0:T(8,128)(2,1)S(1)}, bf16[576,256]{1,0:T(8,128)(2,1)S(1)}, u32[]{:S(2)}, u32[]{:S(2)}) collective-permute-start(bf16[576,256]{1,0:T(8,128)(2,1)S(1)} %k_join.1.a0.after), channel_id=1, source_target_pairs={{0,8},{1,9},{2,10},{3,11},{4,12},{5,13},{6,14},{7,15},{8,0},{9,1},... | collective-permute-start | bytes 884744 | tf_op jit(solution)/shard_map/ppermute | solution.py:634
  117.1 4.8 %collective-permute-start.36 = (bf16[576,256]{1,0:T(8,128)(2,1)S(1)}, bf16[576,256]{1,0:T(8,128)(2,1)S(1)}, u32[]{:S(2)}, u32[]{:S(2)}) collective-permute-start(bf16[576,256]{1,0:T(8,128)(2,1)S(1)} %collective-permute-done.35.a2), channel_id=1, source_target_pairs={{0,8},{1,9},{2,10},{3,11},{4,12},{5,13},{6,14},{7,15},{8,0},{9,1},... | collective-permute-start | bytes 884744 | tf_op jit(solution)/shard_map/ppermute | solution.py:634
  122.0 2.8 %collective-permute-start.34 = (bf16[576,256]{1,0:T(8,128)(2,1)S(1)}, bf16[576,256]{1,0:T(8,128)(2,1)S(1)}, u32[]{:S(2)}, u32[]{:S(2)}) collective-permute-start(bf16[576,256]{1,0:T(8,128)(2,1)S(1)} %collective-permute-done.33.a3), channel_id=1, source_target_pairs={{0,8},{1,9},{2,10},{3,11},{4,12},{5,13},{6,14},{7,15},{8,0},{9,1},... | collective-permute-start | bytes 884744 | tf_op jit(solution)/shard_map/ppermute | solution.py:634
  124.8 2.0 %k_unpack_own.1 = (f32[2304,256]{1,0:T(8,128)}, f32[2304,256]{1,0:T(8,128)}) custom-call(s32[5]{0:T(128)S(1)} %stack.23.at, bf16[576,256]{1,0:T(8,128)(2,1)S(1)} %k_join.1.a0.after, bf16[576,256]{1,0:T(8,128)(2,1)S(1)} %collective-permute-done.31.a1, bf16[576,256]{1,0:T(8,128)(2,1)S(1)} %collective-permute-done.33.a3, ...), custom_call_target="tpu_custom_call" | custom-call | bytes 4194304 | tf_op jit(solution)/shard_map/k_unpack_own/pallas_call | solution.py:565
  126.9 2.0 %k_unpack_other.1 = (f32[2304,256]{1,0:T(8,128)}, f32[2304,256]{1,0:T(8,128)}) custom-call(s32[5]{0:T(128)S(1)} %stack.23.at, bf16[576,256]{1,0:T(8,128)(2,1)S(1)} %collective-permute-done.30.b0, bf16[576,256]{1,0:T(8,128)(2,1)S(1)} %collective-permute-done.32.b1, ...), custom_call_target="tpu_custom_call", output_to_operand_aliasing={{0}: (5, {}), {1}: (6, {})} | custom-call | bytes 4194304 | tf_op jit(solution)/shard_map/k_unpack_other/pallas_call | solution.py:565
  (102 shorter events, 38.4 us)
Async XLA Ops:
  9.6 12.5 %collective-permute-start.3 = (bf16[64,256]{1,0:T(8,128)(2,1)S(1)}, bf16[64,256]{1,0:T(8,128)(2,1)S(1)}, u32[]{:S(2)}, u32[]{:S(2)}) collective-permute-start(bf16[64,256]{1,0:T(8,128)(2,1)S(1)} %get-tuple-element.124), channel_id=1, source_target_pairs={{0,7},{1,2},{2,1},{3,4},{4,3},{5,6},{6,5},{7,0},{8,15},{9,10},{10,... | collective-permute-start | bytes 98312 | tf_op jit(solution)/shard_map/ppermute | solution.py:599
  15.9 6.1 %collective-permute-start.2 = (bf16[64,256]{1,0:T(8,128)(2,1)S(1)}, bf16[64,256]{1,0:T(8,128)(2,1)S(1)}, u32[]{:S(2)}, u32[]{:S(2)}) collective-permute-start(bf16[64,256]{1,0:T(8,128)(2,1)S(1)} %get-tuple-element.125), channel_id=1, source_target_pairs={{0,1},{1,0},{2,3},{3,2},{4,5},{5,4},{6,7},{7,6},{8,9},{9,8},{10,11... | collective-permute-start | bytes 98312 | tf_op jit(solution)/shard_map/ppermute | solution.py:599
  29.5 6.5 %collective-permute-start.7 = (bf16[64,256]{1,0:T(8,128)(2,1)S(1)}, bf16[64,256]{1,0:T(8,128)(2,1)S(1)}, u32[]{:S(2)}, u32[]{:S(2)}) collective-permute-start(bf16[64,256]{1,0:T(8,128)(2,1)S(1)} %get-tuple-element.122), channel_id=1, source_target_pairs={{0,7},{1,2},{2,1},{3,4},{4,3},{5,6},{6,5},{7,0},{8,15},{9,10},{10,... | collective-permute-start | bytes 98312 | tf_op jit(solution)/shard_map/ppermute | solution.py:599
  30.8 5.2 %collective-permute-start.6 = (bf16[64,256]{1,0:T(8,128)(2,1)S(1)}, bf16[64,256]{1,0:T(8,128)(2,1)S(1)}, u32[]{:S(2)}, u32[]{:S(2)}) collective-permute-start(bf16[64,256]{1,0:T(8,128)(2,1)S(1)} %get-tuple-element.123), channel_id=1, source_target_pairs={{0,1},{1,0},{2,3},{3,2},{4,5},{5,4},{6,7},{7,6},{8,9},{9,8},{10,11... | collective-permute-start | bytes 98312 | tf_op jit(solution)/shard_map/ppermute | solution.py:599
  45.6 11.5 %collective-permute-start.11 = (bf16[64,256]{1,0:T(8,128)(2,1)S(1)}, bf16[64,256]{1,0:T(8,128)(2,1)S(1)}, u32[]{:S(2)}, u32[]{:S(2)}) collective-permute-start(bf16[64,256]{1,0:T(8,128)(2,1)S(1)} %get-tuple-element.120), channel_id=1, source_target_pairs={{0,7},{1,2},{2,1},{3,4},{4,3},{5,6},{6,5},{7,0},{8,15},{9,10},{10,... | collective-permute-start | bytes 98312 | tf_op jit(solution)/shard_map/ppermute | solution.py:599
  47.4 9.7 %collective-permute-start.10 = (bf16[64,256]{1,0:T(8,128)(2,1)S(1)}, bf16[64,256]{1,0:T(8,128)(2,1)S(1)}, u32[]{:S(2)}, u32[]{:S(2)}) collective-permute-start(bf16[64,256]{1,0:T(8,128)(2,1)S(1)} %get-tuple-element.121), channel_id=1, source_target_pairs={{0,1},{1,0},{2,3},{3,2},{4,5},{5,4},{6,7},{7,6},{8,9},{9,8},{10,11... | collective-permute-start | bytes 98312 | tf_op jit(solution)/shard_map/ppermute | solution.py:599
  54.3 9.6 %collective-permute-start.13 = (bf16[1152,256]{1,0:T(8,128)(2,1)S(1)}, bf16[1152,256]{1,0:T(8,128)(2,1)S(1)}, u32[]{:S(2)}, u32[]{:S(2)}) collective-permute-start(bf16[1152,256]{1,0:T(8,128)(2,1)S(1)} %get-tuple-element.72), channel_id=1, source_target_pairs={{0,8},{1,9},{2,10},{3,11},{4,12},{5,13},{6,14},{7,15},{8,0},{9,1},... | collective-permute-start | bytes 1769480 | tf_op jit(solution)/shard_map/ppermute | solution.py:634
  66.7 9.1 %collective-permute-start.14 = (bf16[576,256]{1,0:T(8,128)(2,1)S(1)}, bf16[576,256]{1,0:T(8,128)(2,1)S(1)}, u32[]{:S(2)}, u32[]{:S(2)}) collective-permute-start(bf16[576,256]{1,0:T(8,128)(2,1)S(1)} %get-tuple-element.75), channel_id=1, source_target_pairs={{0,1},{1,0},{2,3},{3,2},{4,5},{5,4},{6,7},{7,6},{8,9},{9,8},{10,11... | collective-permute-start | bytes 884744 | tf_op jit(solution)/shard_map/ppermute | solution.py:634
  68.5 15.7 %collective-permute-start.15 = (bf16[576,256]{1,0:T(8,128)(2,1)S(1)}, bf16[576,256]{1,0:T(8,128)(2,1)S(1)}, u32[]{:S(2)}, u32[]{:S(2)}) collective-permute-start(bf16[576,256]{1,0:T(8,128)(2,1)S(1)} %get-tuple-element.76), channel_id=1, source_target_pairs={{0,3},{1,2},{2,1},{3,0},{4,7},{5,6},{6,5},{7,4},{8,11},{9,10},{10,... | collective-permute-start | bytes 884744 | tf_op jit(solution)/shard_map/ppermute | solution.py:634
  69.5 14.7 %collective-permute-start.16 = (bf16[576,256]{1,0:T(8,128)(2,1)S(1)}, bf16[576,256]{1,0:T(8,128)(2,1)S(1)}, u32[]{:S(2)}, u32[]{:S(2)}) collective-permute-start(bf16[576,256]{1,0:T(8,128)(2,1)S(1)} %get-tuple-element.77), channel_id=1, source_target_pairs={{0,2},{1,3},{2,0},{3,1},{4,6},{5,7},{6,4},{7,5},{8,10},{9,11},{10,... | collective-permute-start | bytes 884744 | tf_op jit(solution)/shard_map/ppermute | solution.py:634
  70.4 5.3 %collective-permute-start.18 = (bf16[64,256]{1,0:T(8,128)(2,1)S(1)}, bf16[64,256]{1,0:T(8,128)(2,1)S(1)}, u32[]{:S(2)}, u32[]{:S(2)}) collective-permute-start(bf16[64,256]{1,0:T(8,128)(2,1)S(1)} %get-tuple-element.94), channel_id=1, source_target_pairs={{0,120},{8,16},{16,8},{24,32},{32,24},{40,48},{48,40},{56,64},{64,... | collective-permute-start | bytes 98312 | tf_op jit(solution)/shard_map/ppermute | solution.py:593
  70.4 5.3 %collective-permute-start.17 = (bf16[64,256]{1,0:T(8,128)(2,1)S(1)}, bf16[64,256]{1,0:T(8,128)(2,1)S(1)}, u32[]{:S(2)}, u32[]{:S(2)}) collective-permute-start(bf16[64,256]{1,0:T(8,128)(2,1)S(1)} %get-tuple-element.95), channel_id=1, source_target_pairs={{0,8},{8,0},{16,24},{24,16},{32,40},{40,32},{48,56},{56,48},{64,72... | collective-permute-start | bytes 98312 | tf_op jit(solution)/shard_map/ppermute | solution.py:592
  85.0 9.7 %collective-permute-start.21 = (bf16[144,256]{1,0:T(8,128)(2,1)S(1)}, bf16[144,256]{1,0:T(8,128)(2,1)S(1)}, u32[]{:S(2)}, u32[]{:S(2)}) collective-permute-start(bf16[144,256]{1,0:T(8,128)(2,1)S(1)} %get-tuple-element.84), channel_id=1, source_target_pairs={{0,32},{1,33},{2,34},{3,35},{4,36},{5,37},{6,38},{7,39},{8,40},{9,... | collective-permute-start | bytes 221192 | tf_op jit(solution)/shard_map/ppermute | solution.py:634
  85.1 9.6 %collective-permute-start.22 = (bf16[144,256]{1,0:T(8,128)(2,1)S(1)}, bf16[144,256]{1,0:T(8,128)(2,1)S(1)}, u32[]{:S(2)}, u32[]{:S(2)}) collective-permute-start(bf16[144,256]{1,0:T(8,128)(2,1)S(1)} %get-tuple-element.85), channel_id=1, source_target_pairs={{0,96},{1,97},{2,98},{3,99},{4,100},{5,101},{6,102},{7,103},{8,104... | collective-permute-start | bytes 221192 | tf_op jit(solution)/shard_map/ppermute | solution.py:634
  85.2 9.5 %collective-permute-start.23 = (bf16[144,256]{1,0:T(8,128)(2,1)S(1)}, bf16[144,256]{1,0:T(8,128)(2,1)S(1)}, u32[]{:S(2)}, u32[]{:S(2)}) collective-permute-start(bf16[144,256]{1,0:T(8,128)(2,1)S(1)} %get-tuple-element.86), channel_id=1, source_target_pairs={{0,64},{1,65},{2,66},{3,67},{4,68},{5,69},{6,70},{7,71},{8,72},{9,... | collective-permute-start | bytes 221192 | tf_op jit(solution)/shard_map/ppermute | solution.py:634
  88.3 6.4 %collective-permute-start.20 = (bf16[64,256]{1,0:T(8,128)(2,1)S(1)}, bf16[64,256]{1,0:T(8,128)(2,1)S(1)}, u32[]{:S(2)}, u32[]{:S(2)}) collective-permute-start(bf16[64,256]{1,0:T(8,128)(2,1)S(1)} %get-tuple-element.80), channel_id=1, source_target_pairs={{0,7},{1,2},{2,1},{3,4},{4,3},{5,6},{6,5},{7,0},{8,15},{9,10},{10,... | collective-permute-start | bytes 98312 | tf_op jit(solution)/shard_map/ppermute | solution.py:599
  101.1 5.3 %collective-permute-start.29 = (bf16[144,256]{1,0:T(8,128)(2,1)S(1)}, bf16[144,256]{1,0:T(8,128)(2,1)S(1)}, u32[]{:S(2)}, u32[]{:S(2)}) collective-permute-start(bf16[144,256]{1,0:T(8,128)(2,1)S(1)} %k_x_sum.1.own), channel_id=1, source_target_pairs={{0,64},{1,65},{2,66},{3,67},{4,68},{5,69},{6,70},{7,71},{8,72},{9,... | collective-permute-start | bytes 221192 | tf_op jit(solution)/shard_map/ppermute | solution.py:634
  101.6 5.1 %collective-permute-start.28 = (bf16[144,256]{1,0:T(8,128)(2,1)S(1)}, bf16[144,256]{1,0:T(8,128)(2,1)S(1)}, u32[]{:S(2)}, u32[]{:S(2)}) collective-permute-start(bf16[144,256]{1,0:T(8,128)(2,1)S(1)} %k_x_sum.1.own), channel_id=1, source_target_pairs={{0,96},{1,97},{2,98},{3,99},{4,100},{5,101},{6,102},{7,103},{8,104... | collective-permute-start | bytes 221192 | tf_op jit(solution)/shard_map/ppermute | solution.py:634
  107.5 9.7 %collective-permute-start.35 = (bf16[576,256]{1,0:T(8,128)(2,1)S(1)}, bf16[576,256]{1,0:T(8,128)(2,1)S(1)}, u32[]{:S(2)}, u32[]{:S(2)}) collective-permute-start(bf16[576,256]{1,0:T(8,128)(2,1)S(1)} %k_join.1.a0.after), channel_id=1, source_target_pairs={{0,2},{1,3},{2,0},{3,1},{4,6},{5,7},{6,4},{7,5},{8,10},{9,11},{10,... | collective-permute-start | bytes 884744 | tf_op jit(solution)/shard_map/ppermute | solution.py:634
  107.6 14.4 %collective-permute-start.33 = (bf16[576,256]{1,0:T(8,128)(2,1)S(1)}, bf16[576,256]{1,0:T(8,128)(2,1)S(1)}, u32[]{:S(2)}, u32[]{:S(2)}) collective-permute-start(bf16[576,256]{1,0:T(8,128)(2,1)S(1)} %k_join.1.a0.after), channel_id=1, source_target_pairs={{0,3},{1,2},{2,1},{3,0},{4,7},{5,6},{6,5},{7,4},{8,11},{9,10},{10,... | collective-permute-start | bytes 884744 | tf_op jit(solution)/shard_map/ppermute | solution.py:634
  109.4 15.4 %collective-permute-start.31 = (bf16[576,256]{1,0:T(8,128)(2,1)S(1)}, bf16[576,256]{1,0:T(8,128)(2,1)S(1)}, u32[]{:S(2)}, u32[]{:S(2)}) collective-permute-start(bf16[576,256]{1,0:T(8,128)(2,1)S(1)} %k_join.1.a0.after), channel_id=1, source_target_pairs={{0,1},{1,0},{2,3},{3,2},{4,5},{5,4},{6,7},{7,6},{8,9},{9,8},{10,11... | collective-permute-start | bytes 884744 | tf_op jit(solution)/shard_map/ppermute | solution.py:634
  110.2 16.7 %collective-permute-start.30 = (bf16[576,256]{1,0:T(8,128)(2,1)S(1)}, bf16[576,256]{1,0:T(8,128)(2,1)S(1)}, u32[]{:S(2)}, u32[]{:S(2)}) collective-permute-start(bf16[576,256]{1,0:T(8,128)(2,1)S(1)} %k_join.1.a0.after), channel_id=1, source_target_pairs={{0,8},{1,9},{2,10},{3,11},{4,12},{5,13},{6,14},{7,15},{8,0},{9,1},... | collective-permute-start | bytes 884744 | tf_op jit(solution)/shard_map/ppermute | solution.py:634
  117.1 9.8 %collective-permute-start.36 = (bf16[576,256]{1,0:T(8,128)(2,1)S(1)}, bf16[576,256]{1,0:T(8,128)(2,1)S(1)}, u32[]{:S(2)}, u32[]{:S(2)}) collective-permute-start(bf16[576,256]{1,0:T(8,128)(2,1)S(1)} %collective-permute-done.35.a2), channel_id=1, source_target_pairs={{0,8},{1,9},{2,10},{3,11},{4,12},{5,13},{6,14},{7,15},{8,0},{9,1},... | collective-permute-start | bytes 884744 | tf_op jit(solution)/shard_map/ppermute | solution.py:634
  122.0 4.9 %collective-permute-start.34 = (bf16[576,256]{1,0:T(8,128)(2,1)S(1)}, bf16[576,256]{1,0:T(8,128)(2,1)S(1)}, u32[]{:S(2)}, u32[]{:S(2)}) collective-permute-start(bf16[576,256]{1,0:T(8,128)(2,1)S(1)} %collective-permute-done.33.a3), channel_id=1, source_target_pairs={{0,8},{1,9},{2,10},{3,11},{4,12},{5,13},{6,14},{7,15},{8,0},{9,1},... | collective-permute-start | bytes 884744 | tf_op jit(solution)/shard_map/ppermute | solution.py:634
  (18 other events, 75.7 us)

commit v4 on v3

--- a/solution.py
+++ b/solution.py
@@ -324,7 +324,8 @@
     )
 
 
-def k_pack_field(at, side, corner, field, pk, links):
+def k_pack_field(at, side, corner, field, pk, links, cells):
+    cells[...] = field[...].reshape(CELLS, C)
     links[24] = 1 - at[3] % 2 * 2
     links[25] = 1 - at[4] % 2 * 2
     for s in range(4):
@@ -353,11 +354,13 @@
     spread_columns(x, frame, 2, 0)
 
 
-def k_first(field, w, after, hidden, slope, e0, xt, x, frame):
+def k_first_frame(field, frame, xt, x):
     x[...] = field[...].astype(F32)
     xt[...] = field[...].T
     spread_columns(x, frame, 0, 2)
 
+
+def k_first(frame, w, after, hidden, slope, e0, x):
     for i in range(N_BLK):
         to = block_of(i)
         z = conv_block(frame, w, i)
@@ -490,22 +493,15 @@
     pk_out[...] = pk[...]
 
 
-def k_z_sum(at, own, g1, g3, g2, pk, left, right, after, o, s1, s3, s2, up_out, down_out, x):
+def k_z_sum(at, own, g2, g3, g1, *refs):
+    o, s1, s3, s2, x = refs[-5:]
     rows = o.shape[0]
     x[...] = (own[...] + g2[...].astype(F32)) + (g1[...].astype(F32) + g3[...].astype(F32))
     for step, out in zip(STEPS, (o, s1, s3, s2)):
         out[...] = x[quarter(at[2], step, rows)].astype(out.dtype)
-    up_out[...] = with_corners(pk[0:PK], left[...], right[...], 0)
-    down_out[...] = with_corners(pk[3 * PK :], left[...], right[...], 1)
-
-
-def with_corners(edge, left, right, k):
-    row = lax.broadcasted_iota(jnp.int32, (PK, C), 0)
-    out = jnp.where(row == S, left[S + k : S + k + 1].astype(F32), edge.astype(F32))
-    return jnp.where(row == S + 1, right[S + k : S + k + 1].astype(F32), out).astype(BF)
-
-
-def k_y_sum(own, g1, g3, g2, up, down, out):
+
+
+def k_y_sum(own, g1, g3, g2, out):
     total = (own[...] + g2[...].astype(F32)) + (g1[...].astype(F32) + g3[...].astype(F32))
     out[...] = total.astype(BF)
 
@@ -649,7 +645,6 @@
     at = jnp.stack([core, z_at, y_at, lat_at, lon_at]).astype(jnp.int32)
     w1 = first_weight.reshape(3, 3 * C, C)
     w2 = second_weight.reshape(3, 3 * C, C)
-    cells = field.reshape(CELLS, C)
     cot = cotangent.reshape(CELLS, C)
     cell_bf, cell_f32 = ((CELLS, C), BF), ((CELLS, C), F32)
     edge_bf, edge_f32 = ((4 * S, C), BF), ((4 * S, C), F32)
@@ -664,21 +659,22 @@
 
     own_side = side_links[lat_at, lon_at]
     own_corner = corner_links[lat_at, lon_at]
-    pk, lk = pl.pallas_call(
+    pk, lk, cells = pl.pallas_call(
         k_pack_field,
-        out_shape=[jax.ShapeDtypeStruct(*packs), jax.ShapeDtypeStruct((26,), jnp.int32)],
+        out_shape=[jax.ShapeDtypeStruct(*packs), jax.ShapeDtypeStruct((26,), jnp.int32), pltpu.VMEM((CELLS, C), BF)],
         in_specs=[SMEM, SMEM, SMEM, VMEM],
-        out_specs=[VMEM, SMEM],
+        out_specs=[VMEM, SMEM, VMEM],
         compiler_params=pltpu.CompilerParams(vmem_limit_bytes=8 * MIB),
         name="k_pack_field",
     )(at, own_side, own_corner, field)
     got = trade(pk)
+    frame, xt1 = call(k_first_frame, [cells], [frame_bf, far_turned], WIDE[:1], limit=12)
     (cot_e,) = call(k_edges, [cotangent], [edge_bf], after=[got[1]])
-    hidden0, slope0, e0, xt1 = call(
+    hidden0, slope0, e0 = call(
         k_first,
-        [cells, w1],
-        [far_bf, far_f32, edge_f32, far_turned],
-        WIDE,
+        [frame, w1],
+        [far_bf, far_f32, edge_f32],
+        WIDE[:1],
         after=[got[1]],
         flops=work,
         limit=18,
@@ -735,26 +731,24 @@
     own, *parts, pk = call(
         k_core_sum, [keep1, got1, keep2, got2, pk], quad_z + [packs], links=at
     )
-    left, right = trade_tile(pk)
+    got = trade(pk)
     (middle,) = call(
-        k_input_middle, [fd_e, fd0, w1], [cell_f32], WIDER, flops=work, after=[own], limit=18
+        k_input_middle, [fd_e, fd0, w1], [cell_f32], WIDER, flops=work, after=[got[1]], limit=18
     )
     quad_y = [((rows_y, C), F32)] + [((rows_y, C), BF)] * 3
-    one_pack = ((PK, C), BF)
-    own, *parts, up, down = call(
+    own, *parts = call(
         k_z_sum,
-        [own, *moves(parts, "z"), pk, left, right],
-        quad_y + [one_pack, one_pack],
+        [own, *moves(parts, "z")[::-1]],
+        quad_y,
         [pltpu.VMEM((rows_z, C), F32)],
         links=at,
-        after=[middle],
-    )
-    up, down = trade_lat(up, down)
+        after=[middle, got[0], got[3]],
+    )
     piece_bf = ((rows_y, C), BF)
-    (part,) = call(k_y_sum, [own, *moves(parts, "y")], [piece_bf], after=[up, down])
+    (part,) = call(k_y_sum, [own, *moves(parts, "y")], [piece_bf])
     grad, mixed, token = call(
         k_input_grad,
-        [up, left, right, down, middle, mixed0, mixed_e],
+        [*got, middle, mixed0, mixed_e],
         [cell_bf, cell_bf, ((8, 128), F32)],
         [WIDE[0], WIDER[2]],
         links=lk,

time: 129 us -> 126 us (0.977)
  waiting for transfers between devices: 25.4 us -> 22.3 us
  local copies, waits for them, and re-layouts: 3.9 us -> 2.55 us
    ppermute x4, waiting for transfers between devices: 0.01 us -> 4.8 us  [trade_lat(): lax.ppermute(to_a, 'lat', pairs_a(n))]
    ppermute x21, waiting for transfers between devices: 14.6 us -> 10.6 us  [move(): return lax.ppermute(x, ('tile', 'lat'), exchange(kind, step))]
    ppermute x4, waiting for transfers between devices: 3.9 us -> 1.1 us  [trade_lat(): lax.ppermute(to_b, 'lat', pairs_b(n))]
    ppermute x4, starting transfers between devices: 12.8 us -> 15 us  [trade_lat(): lax.ppermute(to_b, 'lat', pairs_b(n))]
    ppermute x4, starting transfers between devices: 9.39 us -> 7.44 us  [trade_tile(): from_a = lax.ppermute(pk[PK:2 * PK], 'tile', pairs_a(n))]
    ppermute x21, starting transfers between devices: 32.7 us -> 34.1 us  [move(): return lax.ppermute(x, ('tile', 'lat'), exchange(kind, step))]
    pallas_call x19 -> x20, Pallas kernels: 40.2 us -> 40.2 us  [call(): pl.pallas_call(kernel, out_shape=[(pltpu.VMEM if len(out) > 2 else jax.Sh...]
where the time goes in v4:
time: 126 us
  starting transfers between devices  57.9 us (46%)
  Pallas kernels  41.8 us (33%)
  waiting for transfers between devices  22.3 us (18%)
  local copies, waits for them, and re-layouts  2.55 us (2%)
    pallas_call x20, Pallas kernels, call(): pl.pallas_call(kernel, out_shape=[(pltpu.VMEM if len(out) > 2 else jax.Sh...  40.2 us
    ppermute x21, starting transfers between devices, move(): return lax.ppermute(x, ('tile', 'lat'), exchange(kind, step))  34.1 us
    ppermute x4, starting transfers between devices, trade_lat(): lax.ppermute(to_b, 'lat', pairs_b(n))  15 us
    ppermute x21, waiting for transfers between devices, move(): return lax.ppermute(x, ('tile', 'lat'), exchange(kind, step))  10.6 us
    ppermute x4, starting transfers between devices, trade_tile(): from_a = lax.ppermute(pk[PK:2 * PK], 'tile', pairs_a(n))  7.44 us
    ppermute x4, waiting for transfers between devices, trade_tile(): from_b = lax.ppermute(pk[2 * PK:3 * PK], 'tile', pairs_b(n))  5.76 us
    ppermute x4, waiting for transfers between devices, trade_lat(): lax.ppermute(to_a, 'lat', pairs_a(n))  4.8 us
  transfers between devices with their start and end apart: 37, of which 12 were waited for; matrix products, arithmetic and copies ran while one was open for 0% of the time, Pallas kernels for 25%

profile of v4, /device:TPU:1, one launch (start us, length us, event | category | flops | bytes accessed | tf_op | source)
XLA Modules:
  0.0 126.1 jit_solution(8258600566199252921)
XLA Ops:
  9.5 6.4 %collective-permute-start.3 = (bf16[64,256]{1,0:T(8,128)(2,1)S(1)}, bf16[64,256]{1,0:T(8,128)(2,1)S(1)}, u32[]{:S(2)}, u32[]{:S(2)}) collective-permute-start(bf16[64,256]{1,0:T(8,128)(2,1)S(1)} %get-tuple-element.132), channel_id=1, source_target_pairs={{0,7},{1,2},{2,1},{3,4},{4,3},{5,6},{6,5},{7,0},{8,15},{9,10},{10,... | collective-permute-start | bytes 98312 | tf_op jit(solution)/shard_map/ppermute | solution.py:595
  15.9 3.5 %k_first.1 = (bf16[2304,256]{1,0:T(8,128)(2,1)S(1)}, f32[2304,256]{1,0:T(8,128)S(1)}, f32[192,256]{1,0:T(8,128)S(1)}) custom-call(bf16[2400,768]{1,0:T(8,128)(2,1)S(1)} %get-tuple-element.52.frame, bf16[3,768,256]{2,1,0:T(8,128)(2,1)S(1)} %bitcast.14, bf16[64,256]{1,0:T(8,128)(2,1)S(1)} %collective-permute-done.after.left), custom_call_target="tpu_custom_call" | custom-call | flops 2717908992 | bytes 4194304 | tf_op jit(solution)/shard_map/k_first/pallas_call | solution.py:561
  21.2 2.7 %collective-permute-start.4 = (bf16[64,256]{1,0:T(8,128)(2,1)S(1)}, bf16[64,256]{1,0:T(8,128)(2,1)S(1)}, u32[]{:S(2)}, u32[]{:S(2)}) collective-permute-start(bf16[64,256]{1,0:T(8,128)(2,1)S(1)} %get-tuple-element.104), channel_id=1, source_target_pairs={{0,8},{8,0},{16,24},{24,16},{32,40},{40,32},{48,56},{56,48},{64,72... | collective-permute-start | bytes 98312 | tf_op jit(solution)/shard_map/ppermute | solution.py:588
  24.9 2.4 %collective-permute-done.5.right = bf16[64,256]{1,0:T(8,128)(2,1)S(1)} collective-permute-done((bf16[64,256]{1,0:T(8,128)(2,1)S(1)}, bf16[64,256]{1,0:T(8,128)(2,1)S(1)}, u32[]{:S(2)}, u32[]{:S(2)}) %collective-permute-start.5) | collective-permute-done | bytes 32800 | tf_op jit(solution)/shard_map/ppermute | solution.py:589
  27.3 3.4 %collective-permute-start.7 = (bf16[64,256]{1,0:T(8,128)(2,1)S(1)}, bf16[64,256]{1,0:T(8,128)(2,1)S(1)}, u32[]{:S(2)}, u32[]{:S(2)}) collective-permute-start(bf16[64,256]{1,0:T(8,128)(2,1)S(1)} %get-tuple-element.130), channel_id=1, source_target_pairs={{0,7},{1,2},{2,1},{3,4},{4,3},{5,6},{6,5},{7,0},{8,15},{9,10},{10,... | collective-permute-start | bytes 98312 | tf_op jit(solution)/shard_map/ppermute | solution.py:595
  30.7 3.7 %k_second.1 = (bf16[2304,256]{1,0:T(8,128)(2,1)S(1)}, bf16[2304,256]{1,0:T(8,128)(2,1)S(1)}, f32[192,256]{1,0:T(8,128)S(1)}) custom-call(bf16[2400,768]{1,0:T(8,128)(2,1)S(1)} %get-tuple-element.57.frame, bf16[2304,256]{1,0:T(8,128)(2,1)S(1)} %bitcast.18, bf16[3,768,256]{2,1,0:T(8,128)(2,1)S(1)} %bitcast.19, ...), custom_call_target="tpu_custom_call" | custom-call | flops 2717908992 | bytes 4194304 | tf_op jit(solution)/shard_map/k_second/pallas_call | solution.py:561
  34.5 2.4 %k_second_edges.1 = (bf16[192,768]{1,0:T(8,128)(2,1)S(1)}, bf16[192,256]{1,0:T(8,128)(2,1)S(1)}, bf16[192,256]{1,0:T(8,128)(2,1)S(1)}, bf16[256,256]{1,0:T(8,128)(2,1)S(1)}) custom-call(s32[26]{0:T(128)S(1)} %get-tuple-element.49.lk, bf16[64,256]{1,0:T(8,128)(2,1)S(1)} %collective-permute-done.6.up, bf16[64,256]{1,0:T(8,128)(2,1)S(1)} %collective-permute-done.4.after.left, ...), custom_call_target="tpu_custom_call" | custom-call | bytes 4194304 | tf_op jit(solution)/shard_map/k_second_edges/pallas_call | solution.py:561
  36.9 3.1 %collective-permute-start.8 = (bf16[64,256]{1,0:T(8,128)(2,1)S(1)}, bf16[64,256]{1,0:T(8,128)(2,1)S(1)}, u32[]{:S(2)}, u32[]{:S(2)}) collective-permute-start(bf16[64,256]{1,0:T(8,128)(2,1)S(1)} %get-tuple-element.100), channel_id=1, source_target_pairs={{0,8},{8,0},{16,24},{24,16},{32,40},{40,32},{48,56},{56,48},{64,72... | collective-permute-start | bytes 98312 | tf_op jit(solution)/shard_map/ppermute | solution.py:588
  40.8 2.5 %collective-permute-done.9.right = bf16[64,256]{1,0:T(8,128)(2,1)S(1)} collective-permute-done((bf16[64,256]{1,0:T(8,128)(2,1)S(1)}, bf16[64,256]{1,0:T(8,128)(2,1)S(1)}, u32[]{:S(2)}, u32[]{:S(2)}) %collective-permute-start.9) | collective-permute-done | bytes 32800 | tf_op jit(solution)/shard_map/ppermute | solution.py:589
  43.4 3.4 %collective-permute-start.11 = (bf16[64,256]{1,0:T(8,128)(2,1)S(1)}, bf16[64,256]{1,0:T(8,128)(2,1)S(1)}, u32[]{:S(2)}, u32[]{:S(2)}) collective-permute-start(bf16[64,256]{1,0:T(8,128)(2,1)S(1)} %get-tuple-element.128), channel_id=1, source_target_pairs={{0,7},{1,2},{2,1},{3,4},{4,3},{5,6},{6,5},{7,0},{8,15},{9,10},{10,... | collective-permute-start | bytes 98312 | tf_op jit(solution)/shard_map/ppermute | solution.py:595
  46.8 6.9 %k_second_back.1 = (bf16[1152,256]{1,0:T(8,128)(2,1)S(1)}, bf16[1152,256]{1,0:T(8,128)(2,1)S(1)}, bf16[2304,256]{1,0:T(8,128)(2,1)S(1)}, f32[192,256]{1,0:T(8,128)S(1)}) custom-call(s32[5]{0:T(128)S(1)} %stack.23.at, bf16[192,256]{1,0:T(8,128)(2,1)S(1)} %get-tuple-element.60.de, bf16[192,768]{1,0:T(8,128)(2,1)S(1)} %get-tuple-element.61.halo, ...), custom_call_target="tpu_custom_call" | custom-call | flops 5435817984 | bytes 4194304 | tf_op jit(solution)/shard_map/k_second_back/pallas_call | solution.py:561
  53.7 2.7 %collective-permute-start.13 = (bf16[1152,256]{1,0:T(8,128)(2,1)S(1)}, bf16[1152,256]{1,0:T(8,128)(2,1)S(1)}, u32[]{:S(2)}, u32[]{:S(2)}) collective-permute-start(bf16[1152,256]{1,0:T(8,128)(2,1)S(1)} %get-tuple-element.74), channel_id=1, source_target_pairs={{0,8},{1,9},{2,10},{3,11},{4,12},{5,13},{6,14},{7,15},{8,0},{9,1},... | collective-permute-start | bytes 1769480 | tf_op jit(solution)/shard_map/ppermute | solution.py:630
  58.4 4.8 %k_first_total.1 = (bf16[1152,256]{1,0:T(8,128)(2,1)S(1)}, bf16[1152,256]{1,0:T(8,128)(2,1)S(1)}) custom-call(s32[5]{0:T(128)S(1)} %stack.23.at, bf16[192,256]{1,0:T(8,128)(2,1)S(1)} %get-tuple-element.67.de, bf16[192,768]{1,0:T(8,128)(2,1)S(1)} %get-tuple-element.68.halo, bf16[2304,256]{1,0:T(8,128)(2,1)S(1)} %get-tuple-element.69.delta0, ...), custom_call_target="tpu_custom_call" | custom-call | flops 2717908992 | bytes 4194304 | tf_op jit(solution)/shard_map/k_first_total/pallas_call | solution.py:561
  67.2 3.3 %collective-permute-start.19 = (bf16[576,256]{1,0:T(8,128)(2,1)S(1)}, bf16[576,256]{1,0:T(8,128)(2,1)S(1)}, u32[]{:S(2)}, u32[]{:S(2)}) collective-permute-start(bf16[576,256]{1,0:T(8,128)(2,1)S(1)} %get-tuple-element.81), channel_id=1, source_target_pairs={{0,3},{1,2},{2,1},{3,0},{4,7},{5,6},{6,5},{7,4},{8,11},{9,10},{10,... | collective-permute-start | bytes 884744 | tf_op jit(solution)/shard_map/ppermute | solution.py:630
  72.5 3.7 %k_input_middle.1.refs_0_.middle = f32[2304,256]{1,0:T(8,128)S(1)} custom-call(bf16[192,256]{1,0:T(8,128)(2,1)S(1)} %get-tuple-element.67.de, bf16[2304,256]{1,0:T(8,128)(2,1)S(1)} %get-tuple-element.69.delta0, bf16[3,768,256]{2,1,0:T(8,128)(2,1)S(1)} %bitcast.17, bf16[64,256]{1,0:T(8,128)(2,1)S(1)} %collective-permute-done.14.after.left), custom_call_target="tpu_custom_call" | custom-call | flops 2717908992 | bytes 4194304 | tf_op jit(solution)/shard_map/k_input_middle/pallas_call | solution.py:561
  77.3 4.8 %collective-permute-done.16.refs_1_.up = bf16[64,256]{1,0:T(8,128)(2,1)S(1)} collective-permute-done((bf16[64,256]{1,0:T(8,128)(2,1)S(1)}, bf16[64,256]{1,0:T(8,128)(2,1)S(1)}, u32[]{:S(2)}, u32[]{:S(2)}) %collective-permute-start.16) | collective-permute-done | bytes 32800 | tf_op jit(solution)/shard_map/ppermute | solution.py:595
  84.8 3.1 %collective-permute-start.23 = (bf16[144,256]{1,0:T(8,128)(2,1)S(1)}, bf16[144,256]{1,0:T(8,128)(2,1)S(1)}, u32[]{:S(2)}, u32[]{:S(2)}) collective-permute-start(bf16[144,256]{1,0:T(8,128)(2,1)S(1)} %get-tuple-element.86), channel_id=1, source_target_pairs={{0,64},{1,65},{2,66},{3,67},{4,68},{5,69},{6,70},{7,71},{8,72},{9,... | collective-permute-start | bytes 221192 | tf_op jit(solution)/shard_map/ppermute | solution.py:630
  88.0 3.3 %collective-permute-done.22.g3 = bf16[144,256]{1,0:T(8,128)(2,1)S(1)} collective-permute-done((bf16[144,256]{1,0:T(8,128)(2,1)S(1)}, bf16[144,256]{1,0:T(8,128)(2,1)S(1)}, u32[]{:S(2)}, u32[]{:S(2)}) %collective-permute-start.22) | collective-permute-done | bytes 73760 | tf_op jit(solution)/shard_map/ppermute | solution.py:630
  94.1 2.2 %collective-permute-done.26.g2 = bf16[144,256]{1,0:T(8,128)(2,1)S(1)} collective-permute-done((bf16[144,256]{1,0:T(8,128)(2,1)S(1)}, bf16[144,256]{1,0:T(8,128)(2,1)S(1)}, u32[]{:S(2)}, u32[]{:S(2)}) %collective-permute-start.26) | collective-permute-done | bytes 73760 | tf_op jit(solution)/shard_map/ppermute | solution.py:630
  98.3 2.2 %collective-permute-start.28 = (bf16[144,256]{1,0:T(8,128)(2,1)S(1)}, bf16[144,256]{1,0:T(8,128)(2,1)S(1)}, u32[]{:S(2)}, u32[]{:S(2)}) collective-permute-start(bf16[144,256]{1,0:T(8,128)(2,1)S(1)} %k_x_sum.1.own), channel_id=1, source_target_pairs={{0,96},{1,97},{2,98},{3,99},{4,100},{5,101},{6,102},{7,103},{8,104... | collective-permute-start | bytes 221192 | tf_op jit(solution)/shard_map/ppermute | solution.py:630
  100.5 2.5 %k_input_grad.1 = (bf16[2304,256]{1,0:T(8,128)(2,1)}, bf16[2304,256]{1,0:T(8,128)(2,1)}, f32[8,128]{1,0:T(8,128)S(1)}) custom-call(s32[26]{0:T(128)S(1)} %get-tuple-element.49.lk, bf16[64,256]{1,0:T(8,128)(2,1)S(1)} %collective-permute-done.16.refs_1_.up, bf16[64,256]{1,0:T(8,128)(2,1)S(1)} %collective-permute-done.14.after.left, ...), custom_call_target="tpu_custom_call" | custom-call | bytes 4194304 | tf_op jit(solution)/shard_map/k_input_grad/pallas_call | solution.py:561
  107.7 4.9 %collective-permute-start.30 = (bf16[576,256]{1,0:T(8,128)(2,1)S(1)}, bf16[576,256]{1,0:T(8,128)(2,1)S(1)}, u32[]{:S(2)}, u32[]{:S(2)}) collective-permute-start(bf16[576,256]{1,0:T(8,128)(2,1)S(1)} %k_join.1.a0.after), channel_id=1, source_target_pairs={{0,8},{1,9},{2,10},{3,11},{4,12},{5,13},{6,14},{7,15},{8,0},{9,1},... | collective-permute-start | bytes 884744 | tf_op jit(solution)/shard_map/ppermute | solution.py:630
  112.6 6.2 %collective-permute-start.36 = (bf16[576,256]{1,0:T(8,128)(2,1)S(1)}, bf16[576,256]{1,0:T(8,128)(2,1)S(1)}, u32[]{:S(2)}, u32[]{:S(2)}) collective-permute-start(bf16[576,256]{1,0:T(8,128)(2,1)S(1)} %collective-permute-done.35.a2), channel_id=1, source_target_pairs={{0,8},{1,9},{2,10},{3,11},{4,12},{5,13},{6,14},{7,15},{8,0},{9,1},... | collective-permute-start | bytes 884744 | tf_op jit(solution)/shard_map/ppermute | solution.py:630
  118.7 3.0 %collective-permute-start.34 = (bf16[576,256]{1,0:T(8,128)(2,1)S(1)}, bf16[576,256]{1,0:T(8,128)(2,1)S(1)}, u32[]{:S(2)}, u32[]{:S(2)}) collective-permute-start(bf16[576,256]{1,0:T(8,128)(2,1)S(1)} %collective-permute-done.33.a3), channel_id=1, source_target_pairs={{0,8},{1,9},{2,10},{3,11},{4,12},{5,13},{6,14},{7,15},{8,0},{9,1},... | collective-permute-start | bytes 884744 | tf_op jit(solution)/shard_map/ppermute | solution.py:630
  (105 shorter events, 37.8 us)
Async XLA Ops:
  9.5 10.2 %collective-permute-start.3 = (bf16[64,256]{1,0:T(8,128)(2,1)S(1)}, bf16[64,256]{1,0:T(8,128)(2,1)S(1)}, u32[]{:S(2)}, u32[]{:S(2)}) collective-permute-start(bf16[64,256]{1,0:T(8,128)(2,1)S(1)} %get-tuple-element.132), channel_id=1, source_target_pairs={{0,7},{1,2},{2,1},{3,4},{4,3},{5,6},{6,5},{7,0},{8,15},{9,10},{10,... | collective-permute-start | bytes 98312 | tf_op jit(solution)/shard_map/ppermute | solution.py:595
  27.3 7.1 %collective-permute-start.7 = (bf16[64,256]{1,0:T(8,128)(2,1)S(1)}, bf16[64,256]{1,0:T(8,128)(2,1)S(1)}, u32[]{:S(2)}, u32[]{:S(2)}) collective-permute-start(bf16[64,256]{1,0:T(8,128)(2,1)S(1)} %get-tuple-element.130), channel_id=1, source_target_pairs={{0,7},{1,2},{2,1},{3,4},{4,3},{5,6},{6,5},{7,0},{8,15},{9,10},{10,... | collective-permute-start | bytes 98312 | tf_op jit(solution)/shard_map/ppermute | solution.py:595
  43.4 13.1 %collective-permute-start.11 = (bf16[64,256]{1,0:T(8,128)(2,1)S(1)}, bf16[64,256]{1,0:T(8,128)(2,1)S(1)}, u32[]{:S(2)}, u32[]{:S(2)}) collective-permute-start(bf16[64,256]{1,0:T(8,128)(2,1)S(1)} %get-tuple-element.128), channel_id=1, source_target_pairs={{0,7},{1,2},{2,1},{3,4},{4,3},{5,6},{6,5},{7,0},{8,15},{9,10},{10,... | collective-permute-start | bytes 98312 | tf_op jit(solution)/shard_map/ppermute | solution.py:595
  46.8 9.7 %collective-permute-start.10 = (bf16[64,256]{1,0:T(8,128)(2,1)S(1)}, bf16[64,256]{1,0:T(8,128)(2,1)S(1)}, u32[]{:S(2)}, u32[]{:S(2)}) collective-permute-start(bf16[64,256]{1,0:T(8,128)(2,1)S(1)} %get-tuple-element.129), channel_id=1, source_target_pairs={{0,1},{1,0},{2,3},{3,2},{4,5},{5,4},{6,7},{7,6},{8,9},{9,8},{10,11... | collective-permute-start | bytes 98312 | tf_op jit(solution)/shard_map/ppermute | solution.py:595
  53.7 9.6 %collective-permute-start.13 = (bf16[1152,256]{1,0:T(8,128)(2,1)S(1)}, bf16[1152,256]{1,0:T(8,128)(2,1)S(1)}, u32[]{:S(2)}, u32[]{:S(2)}) collective-permute-start(bf16[1152,256]{1,0:T(8,128)(2,1)S(1)} %get-tuple-element.74), channel_id=1, source_target_pairs={{0,8},{1,9},{2,10},{3,11},{4,12},{5,13},{6,14},{7,15},{8,0},{9,1},... | collective-permute-start | bytes 1769480 | tf_op jit(solution)/shard_map/ppermute | solution.py:630
  66.1 4.4 %collective-permute-start.14 = (bf16[64,256]{1,0:T(8,128)(2,1)S(1)}, bf16[64,256]{1,0:T(8,128)(2,1)S(1)}, u32[]{:S(2)}, u32[]{:S(2)}) collective-permute-start(bf16[64,256]{1,0:T(8,128)(2,1)S(1)} %get-tuple-element.96), channel_id=1, source_target_pairs={{0,8},{8,0},{16,24},{24,16},{32,40},{40,32},{48,56},{56,48},{64,72... | collective-permute-start | bytes 98312 | tf_op jit(solution)/shard_map/ppermute | solution.py:588
  66.3 4.2 %collective-permute-start.15 = (bf16[64,256]{1,0:T(8,128)(2,1)S(1)}, bf16[64,256]{1,0:T(8,128)(2,1)S(1)}, u32[]{:S(2)}, u32[]{:S(2)}) collective-permute-start(bf16[64,256]{1,0:T(8,128)(2,1)S(1)} %get-tuple-element.97), channel_id=1, source_target_pairs={{0,120},{8,16},{16,8},{24,32},{32,24},{40,48},{48,40},{56,64},{64,... | collective-permute-start | bytes 98312 | tf_op jit(solution)/shard_map/ppermute | solution.py:589
  66.3 15.8 %collective-permute-start.18 = (bf16[576,256]{1,0:T(8,128)(2,1)S(1)}, bf16[576,256]{1,0:T(8,128)(2,1)S(1)}, u32[]{:S(2)}, u32[]{:S(2)}) collective-permute-start(bf16[576,256]{1,0:T(8,128)(2,1)S(1)} %get-tuple-element.80), channel_id=1, source_target_pairs={{0,2},{1,3},{2,0},{3,1},{4,6},{5,7},{6,4},{7,5},{8,10},{9,11},{10,... | collective-permute-start | bytes 884744 | tf_op jit(solution)/shard_map/ppermute | solution.py:630
  67.2 16.7 %collective-permute-start.19 = (bf16[576,256]{1,0:T(8,128)(2,1)S(1)}, bf16[576,256]{1,0:T(8,128)(2,1)S(1)}, u32[]{:S(2)}, u32[]{:S(2)}) collective-permute-start(bf16[576,256]{1,0:T(8,128)(2,1)S(1)} %get-tuple-element.81), channel_id=1, source_target_pairs={{0,3},{1,2},{2,1},{3,0},{4,7},{5,6},{6,5},{7,4},{8,11},{9,10},{10,... | collective-permute-start | bytes 884744 | tf_op jit(solution)/shard_map/ppermute | solution.py:630
  70.5 13.3 %collective-permute-start.20 = (bf16[576,256]{1,0:T(8,128)(2,1)S(1)}, bf16[576,256]{1,0:T(8,128)(2,1)S(1)}, u32[]{:S(2)}, u32[]{:S(2)}) collective-permute-start(bf16[576,256]{1,0:T(8,128)(2,1)S(1)} %get-tuple-element.82), channel_id=1, source_target_pairs={{0,1},{1,0},{2,3},{3,2},{4,5},{5,4},{6,7},{7,6},{8,9},{9,8},{10,11... | collective-permute-start | bytes 884744 | tf_op jit(solution)/shard_map/ppermute | solution.py:630
  70.6 6.6 %collective-permute-start.17 = (bf16[64,256]{1,0:T(8,128)(2,1)S(1)}, bf16[64,256]{1,0:T(8,128)(2,1)S(1)}, u32[]{:S(2)}, u32[]{:S(2)}) collective-permute-start(bf16[64,256]{1,0:T(8,128)(2,1)S(1)} %get-tuple-element.126), channel_id=1, source_target_pairs={{0,7},{1,2},{2,1},{3,4},{4,3},{5,6},{6,5},{7,0},{8,15},{9,10},{10,... | collective-permute-start | bytes 98312 | tf_op jit(solution)/shard_map/ppermute | solution.py:595
  72.5 9.6 %collective-permute-start.16 = (bf16[64,256]{1,0:T(8,128)(2,1)S(1)}, bf16[64,256]{1,0:T(8,128)(2,1)S(1)}, u32[]{:S(2)}, u32[]{:S(2)}) collective-permute-start(bf16[64,256]{1,0:T(8,128)(2,1)S(1)} %get-tuple-element.127), channel_id=1, source_target_pairs={{0,1},{1,0},{2,3},{3,2},{4,5},{5,4},{6,7},{7,6},{8,9},{9,8},{10,11... | collective-permute-start | bytes 98312 | tf_op jit(solution)/shard_map/ppermute | solution.py:595
  84.7 6.6 %collective-permute-start.22 = (bf16[144,256]{1,0:T(8,128)(2,1)S(1)}, bf16[144,256]{1,0:T(8,128)(2,1)S(1)}, u32[]{:S(2)}, u32[]{:S(2)}) collective-permute-start(bf16[144,256]{1,0:T(8,128)(2,1)S(1)} %get-tuple-element.85), channel_id=1, source_target_pairs={{0,96},{1,97},{2,98},{3,99},{4,100},{5,101},{6,102},{7,103},{8,104... | collective-permute-start | bytes 221192 | tf_op jit(solution)/shard_map/ppermute | solution.py:630
  84.8 6.5 %collective-permute-start.23 = (bf16[144,256]{1,0:T(8,128)(2,1)S(1)}, bf16[144,256]{1,0:T(8,128)(2,1)S(1)}, u32[]{:S(2)}, u32[]{:S(2)}) collective-permute-start(bf16[144,256]{1,0:T(8,128)(2,1)S(1)} %get-tuple-element.86), channel_id=1, source_target_pairs={{0,64},{1,65},{2,66},{3,67},{4,68},{5,69},{6,70},{7,71},{8,72},{9,... | collective-permute-start | bytes 221192 | tf_op jit(solution)/shard_map/ppermute | solution.py:630
  91.4 4.9 %collective-permute-start.26 = (bf16[144,256]{1,0:T(8,128)(2,1)S(1)}, bf16[144,256]{1,0:T(8,128)(2,1)S(1)}, u32[]{:S(2)}, u32[]{:S(2)}) collective-permute-start(bf16[144,256]{1,0:T(8,128)(2,1)S(1)} %k_y_sum.1.after.own), channel_id=1, source_target_pairs={{0,4},{1,5},{2,6},{3,7},{4,0},{5,1},{6,2},{7,3},{8,12},{9,13},{10,... | collective-permute-start | bytes 221192 | tf_op jit(solution)/shard_map/ppermute | solution.py:630
  91.5 5.3 %collective-permute-start.25 = (bf16[144,256]{1,0:T(8,128)(2,1)S(1)}, bf16[144,256]{1,0:T(8,128)(2,1)S(1)}, u32[]{:S(2)}, u32[]{:S(2)}) collective-permute-start(bf16[144,256]{1,0:T(8,128)(2,1)S(1)} %k_y_sum.1.after.own), channel_id=1, source_target_pairs={{0,20},{1,21},{2,22},{3,23},{4,16},{5,17},{6,18},{7,19},{8,28},{9,... | collective-permute-start | bytes 221192 | tf_op jit(solution)/shard_map/ppermute | solution.py:630
  96.8 6.2 %collective-permute-start.29 = (bf16[144,256]{1,0:T(8,128)(2,1)S(1)}, bf16[144,256]{1,0:T(8,128)(2,1)S(1)}, u32[]{:S(2)}, u32[]{:S(2)}) collective-permute-start(bf16[144,256]{1,0:T(8,128)(2,1)S(1)} %k_x_sum.1.own), channel_id=1, source_target_pairs={{0,64},{1,65},{2,66},{3,67},{4,68},{5,69},{6,70},{7,71},{8,72},{9,... | collective-permute-start | bytes 221192 | tf_op jit(solution)/shard_map/ppermute | solution.py:630
  98.3 4.8 %collective-permute-start.28 = (bf16[144,256]{1,0:T(8,128)(2,1)S(1)}, bf16[144,256]{1,0:T(8,128)(2,1)S(1)}, u32[]{:S(2)}, u32[]{:S(2)}) collective-permute-start(bf16[144,256]{1,0:T(8,128)(2,1)S(1)} %k_x_sum.1.own), channel_id=1, source_target_pairs={{0,96},{1,97},{2,98},{3,99},{4,100},{5,101},{6,102},{7,103},{8,104... | collective-permute-start | bytes 221192 | tf_op jit(solution)/shard_map/ppermute | solution.py:630
  104.4 8.1 %collective-permute-start.35 = (bf16[576,256]{1,0:T(8,128)(2,1)S(1)}, bf16[576,256]{1,0:T(8,128)(2,1)S(1)}, u32[]{:S(2)}, u32[]{:S(2)}) collective-permute-start(bf16[576,256]{1,0:T(8,128)(2,1)S(1)} %k_join.1.a0.after), channel_id=1, source_target_pairs={{0,2},{1,3},{2,0},{3,1},{4,6},{5,7},{6,4},{7,5},{8,10},{9,11},{10,... | collective-permute-start | bytes 884744 | tf_op jit(solution)/shard_map/ppermute | solution.py:630
  106.2 12.5 %collective-permute-start.33 = (bf16[576,256]{1,0:T(8,128)(2,1)S(1)}, bf16[576,256]{1,0:T(8,128)(2,1)S(1)}, u32[]{:S(2)}, u32[]{:S(2)}) collective-permute-start(bf16[576,256]{1,0:T(8,128)(2,1)S(1)} %k_join.1.a0.after), channel_id=1, source_target_pairs={{0,3},{1,2},{2,1},{3,0},{4,7},{5,6},{6,5},{7,4},{8,11},{9,10},{10,... | collective-permute-start | bytes 884744 | tf_op jit(solution)/shard_map/ppermute | solution.py:630
  107.7 14.1 %collective-permute-start.31 = (bf16[576,256]{1,0:T(8,128)(2,1)S(1)}, bf16[576,256]{1,0:T(8,128)(2,1)S(1)}, u32[]{:S(2)}, u32[]{:S(2)}) collective-permute-start(bf16[576,256]{1,0:T(8,128)(2,1)S(1)} %k_join.1.a0.after), channel_id=1, source_target_pairs={{0,1},{1,0},{2,3},{3,2},{4,5},{5,4},{6,7},{7,6},{8,9},{9,8},{10,11... | collective-permute-start | bytes 884744 | tf_op jit(solution)/shard_map/ppermute | solution.py:630
  107.7 16.1 %collective-permute-start.30 = (bf16[576,256]{1,0:T(8,128)(2,1)S(1)}, bf16[576,256]{1,0:T(8,128)(2,1)S(1)}, u32[]{:S(2)}, u32[]{:S(2)}) collective-permute-start(bf16[576,256]{1,0:T(8,128)(2,1)S(1)} %k_join.1.a0.after), channel_id=1, source_target_pairs={{0,8},{1,9},{2,10},{3,11},{4,12},{5,13},{6,14},{7,15},{8,0},{9,1},... | collective-permute-start | bytes 884744 | tf_op jit(solution)/shard_map/ppermute | solution.py:630
  112.6 11.3 %collective-permute-start.36 = (bf16[576,256]{1,0:T(8,128)(2,1)S(1)}, bf16[576,256]{1,0:T(8,128)(2,1)S(1)}, u32[]{:S(2)}, u32[]{:S(2)}) collective-permute-start(bf16[576,256]{1,0:T(8,128)(2,1)S(1)} %collective-permute-done.35.a2), channel_id=1, source_target_pairs={{0,8},{1,9},{2,10},{3,11},{4,12},{5,13},{6,14},{7,15},{8,0},{9,1},... | collective-permute-start | bytes 884744 | tf_op jit(solution)/shard_map/ppermute | solution.py:630
  118.7 5.1 %collective-permute-start.34 = (bf16[576,256]{1,0:T(8,128)(2,1)S(1)}, bf16[576,256]{1,0:T(8,128)(2,1)S(1)}, u32[]{:S(2)}, u32[]{:S(2)}) collective-permute-start(bf16[576,256]{1,0:T(8,128)(2,1)S(1)} %collective-permute-done.33.a3), channel_id=1, source_target_pairs={{0,8},{1,9},{2,10},{3,11},{4,12},{5,13},{6,14},{7,15},{8,0},{9,1},... | collective-permute-start | bytes 884744 | tf_op jit(solution)/shard_map/ppermute | solution.py:630
  (17 other events, 70.3 us)

commit v5 on v4

--- a/solution.py
+++ b/solution.py
@@ -134,9 +134,8 @@
 
 def halo_rows(lk, got):
     row, col = grid_of(S, 4 * PK)
-    sides = []
+    hits = []
     for s in range(4):
-        taps = []
         for t in range(3):
             at = row + (t - 1)
             cell = jnp.where(side_flip(lk, s) == 1, S - 1 - at, at)
@@ -145,21 +144,23 @@
                 for end, c in ((-1, 2 * s), (S, 2 * s + 1)):
                     home = jnp.where(corner_keep(lk, c) != 0, corner_home(lk, c), -1)
                     want = jnp.where(at == end, home, want)
-            taps.append(pick(col == want, got).astype(BF))
-        sides.append(jnp.concatenate(taps, axis=1))
-    return sides
+            hits.append(col == want)
+    cells = pick(jnp.concatenate(hits, axis=0), got).astype(BF)
+    taps = [cells[n * S : (n + 1) * S] for n in range(12)]
+    return [jnp.concatenate(taps[3 * s : 3 * s + 3], axis=1) for s in range(4)]
 
 
 def rim_adds(lk, got):
     row, col = grid_of(S, 4 * PK)
-    adds = []
+    hits = []
     for s in range(4):
         hit = col == side_home(lk, s) + row
         if s < 2:
             for end, c in ((0, 2 * s), (S - 1, 2 * s + 1)):
                 hit = hit | ((row == end) & (col == corner_home(lk, c)))
-        adds.append(pick(hit, got))
-    return adds
+        hits.append(hit)
+    adds = pick(jnp.concatenate(hits, axis=0), got)
+    return [adds[s * S : (s + 1) * S] for s in range(4)]
 
 
 def cross(adds):
@@ -206,21 +207,25 @@
 
 def rims_of(edges, w):
     row, col = grid_of(PK, 4 * S)
+    hits = []
+    for s in range(4):
+        for t in range(3):
+            if s < 2:
+                pos = jnp.where(row < S, row + 1, jnp.where(row == S, 0, S + 1))
+                used = row < S + 2
+            else:
+                pos = row + 1
+                used = row < S
+            src = pos - t
+            hits.append(used & (src >= 0) & (src < S) & (col == s * S + src))
+    cells = pick(jnp.concatenate(hits, axis=0), edges).astype(BF)
     out = []
     for s in range(4):
         total = None
         for t in range(3):
-            if s < 2:
-                pos = jnp.where(row < S, row + 1, jnp.where(row == S, 0, S + 1))
-                used = row < S + 2
-                a, b = (0, 2)[s], t
-            else:
-                pos = row + 1
-                used = row < S
-                a, b = t, (0, 2)[s - 2]
-            src = pos - t
-            hit = used & (src >= 0) & (src < S) & (col == s * S + src)
-            term = dot_nt(pick(hit, edges).astype(BF), w[a, b * C : (b + 1) * C])
+            a, b = ((0, 2)[s], t) if s < 2 else (t, (0, 2)[s - 2])
+            n = 3 * s + t
+            term = dot_nt(cells[n * PK : (n + 1) * PK], w[a, b * C : (b + 1) * C])
             total = term if total is None else total + term
         out.append(total.astype(BF))
     return jnp.concatenate(out, axis=0)
@@ -438,18 +443,38 @@
     pk[...] = pack_rims(lk, rims_of(edges, w))
 
 
-def k_first_total(at, de, halo, delta0, xt, keep, send, x, frame, edges, tv):
+def half_sums(h, xt, frame, side, out):
+    for n in range(4):
+        tap = h * 5 + n
+        a, b = tap // 3, tap % 3
+        rows = pl.ds(pl.multiple_of((2 - a) * S, 16), CELLS)
+        lanes = pl.ds(pl.multiple_of(b * C, C), C)
+        part = dot(xt[...], frame[rows, lanes])
+        for k, (used, at) in enumerate(((a == 0, b), (a == 2, b), (b == 0, a), (b == 2, a))):
+            term = side[pl.ds(pl.multiple_of(k * 3 * C + at * C, C), C)]
+            part = part + jnp.where(used, term, 0.0)
+        out[pl.ds(pl.multiple_of(n * C + h * (C // 2), C // 2), C)] = part.astype(BF)
+    part = dot(xt[pl.ds(pl.multiple_of(h * (C // 2), C // 2), C // 2)], frame[pl.ds(S, CELLS), C : 2 * C])
+    out[pl.ds(pl.multiple_of((1 - h) * 4 * C, C), C // 2)] = part.astype(BF)
+
+
+def k_first_send(at, de, halo, delta0, xt, send, frame, side, x, edges):
     edges[...] = de[...].astype(F32)
     x[...] = delta0[...].astype(F32)
     put_edges(x, edges)
     spread_columns(x, frame, 2, 0)
-
-    def store(row, part):
-        tv[pl.ds(row, C)] = part
-
-    weight_sums(xt, frame, halo, de, store)
-    keep[...] = tv[half(at[0])]
-    send[...] = tv[half(1 - at[0])]
+    for s in range(4):
+        side[pl.ds(s * 3 * C, 3 * C)] = lax.dot_general(
+            halo[s * S : (s + 1) * S],
+            de[s * S : (s + 1) * S],
+            (((0,), (0,)), ((), ())),
+            preferred_element_type=F32,
+        )
+    half_sums(1 - at[0], xt, frame, side, send)
+
+
+def k_first_keep(at, xt, frame, side, keep):
+    half_sums(at[0], xt, frame, side, keep)
 
 
 def k_input_middle(de, delta0, w, after, out, x, frame, edges):
@@ -716,16 +741,19 @@
     fd_e, pk = call(
         k_first_delta_edges, [*got, e0, slope_e, w1], [edge_bf, packs], links=lk
     )
-    keep1, send1 = call(
-        k_first_total,
+    send1, frame, side = call(
+        k_first_send,
         [fd_e, halo1, fd0, xt1],
-        [half_bf, half_bf],
-        WIDER + [CELL_BF],
+        [half_bf, frame_bf, ((12 * C, C), F32, 1)],
+        [WIDE[0], WIDER[2]],
         links=at,
         flops=work,
         limit=20,
     )
     got1 = move(send1, "core", 1)
+    (keep1,) = call(
+        k_first_keep, [xt1, frame, side], [half_bf], links=at, flops=work, limit=14
+    )
     rows_z, rows_y = CELLS // 4, CELLS // 16
     quad_z = [((rows_z, C), F32)] + [((rows_z, C), BF)] * 3
     own, *parts, pk = call(

time: 126 us -> 125 us (level)
  waiting for transfers between devices: 22.3 us -> 20.3 us
    ppermute x21, waiting for transfers between devices: 10.6 us -> 8.29 us  [move(): return lax.ppermute(x, ('tile', 'lat'), exchange(kind, step))]
    pallas_call x20 -> x21, Pallas kernels: 40.2 us -> 40.3 us  [call(): pl.pallas_call(kernel, out_shape=[(pltpu.VMEM if len(out) > 2 else jax.Sh...]
  transfers between devices with their start and end apart: 37 -> 37, of which waited for: 12 -> 11; matrix products, arithmetic and copies ran while one was open for 0% -> 0% of each run, Pallas kernels for 25% -> 26%
where the time goes in v5:
time: 125 us
  starting transfers between devices  58.3 us (47%)
  Pallas kernels  41.8 us (33%)
  waiting for transfers between devices  20.3 us (16%)
  local copies, waits for them, and re-layouts  2.55 us (2%)
    pallas_call x21, Pallas kernels, call(): pl.pallas_call(kernel, out_shape=[(pltpu.VMEM if len(out) > 2 else jax.Sh...  40.3 us
    ppermute x21, starting transfers between devices, move(): return lax.ppermute(x, ('tile', 'lat'), exchange(kind, step))  33.9 us
    ppermute x4, starting transfers between devices, trade_lat(): lax.ppermute(to_b, 'lat', pairs_b(n))  15.2 us
    ppermute x21, waiting for transfers between devices, move(): return lax.ppermute(x, ('tile', 'lat'), exchange(kind, step))  8.29 us
    ppermute x4, starting transfers between devices, trade_tile(): from_a = lax.ppermute(pk[PK:2 * PK], 'tile', pairs_a(n))  7.79 us
    ppermute x4, waiting for transfers between devices, trade_tile(): from_b = lax.ppermute(pk[2 * PK:3 * PK], 'tile', pairs_b(n))  5.76 us
    ppermute x4, waiting for transfers between devices, trade_lat(): lax.ppermute(to_a, 'lat', pairs_a(n))  5.1 us
  transfers between devices with their start and end apart: 37, of which 11 were waited for; matrix products, arithmetic and copies ran while one was open for 0% of the time, Pallas kernels for 26%

profile of v5, /device:TPU:1, one launch (start us, length us, event | category | flops | bytes accessed | tf_op | source)
XLA Modules:
  0.0 124.5 jit_solution(3193793349901545665)
XLA Ops:
  9.5 6.4 %collective-permute-start.3 = (bf16[64,256]{1,0:T(8,128)(2,1)S(1)}, bf16[64,256]{1,0:T(8,128)(2,1)S(1)}, u32[]{:S(2)}, u32[]{:S(2)}) collective-permute-start(bf16[64,256]{1,0:T(8,128)(2,1)S(1)} %get-tuple-element.134), channel_id=1, source_target_pairs={{0,7},{1,2},{2,1},{3,4},{4,3},{5,6},{6,5},{7,0},{8,15},{9,10},{10,... | collective-permute-start | bytes 98312 | tf_op jit(solution)/shard_map/ppermute | solution.py:620
  15.9 3.5 %k_first.1 = (bf16[2304,256]{1,0:T(8,128)(2,1)S(1)}, f32[2304,256]{1,0:T(8,128)S(1)}, f32[192,256]{1,0:T(8,128)S(1)}) custom-call(bf16[2400,768]{1,0:T(8,128)(2,1)S(1)} %get-tuple-element.54.frame, bf16[3,768,256]{2,1,0:T(8,128)(2,1)S(1)} %bitcast.14, bf16[64,256]{1,0:T(8,128)(2,1)S(1)} %collective-permute-done.after.left), custom_call_target="tpu_custom_call" | custom-call | flops 2717908992 | bytes 4194304 | tf_op jit(solution)/shard_map/k_first/pallas_call | solution.py:586
  21.1 2.7 %collective-permute-start.4 = (bf16[64,256]{1,0:T(8,128)(2,1)S(1)}, bf16[64,256]{1,0:T(8,128)(2,1)S(1)}, u32[]{:S(2)}, u32[]{:S(2)}) collective-permute-start(bf16[64,256]{1,0:T(8,128)(2,1)S(1)} %get-tuple-element.106), channel_id=1, source_target_pairs={{0,8},{8,0},{16,24},{24,16},{32,40},{40,32},{48,56},{56,48},{64,72... | collective-permute-start | bytes 98312 | tf_op jit(solution)/shard_map/ppermute | solution.py:613
  24.7 2.4 %collective-permute-done.5.right = bf16[64,256]{1,0:T(8,128)(2,1)S(1)} collective-permute-done((bf16[64,256]{1,0:T(8,128)(2,1)S(1)}, bf16[64,256]{1,0:T(8,128)(2,1)S(1)}, u32[]{:S(2)}, u32[]{:S(2)}) %collective-permute-start.5) | collective-permute-done | bytes 32800 | tf_op jit(solution)/shard_map/ppermute | solution.py:614
  27.2 3.4 %collective-permute-start.7 = (bf16[64,256]{1,0:T(8,128)(2,1)S(1)}, bf16[64,256]{1,0:T(8,128)(2,1)S(1)}, u32[]{:S(2)}, u32[]{:S(2)}) collective-permute-start(bf16[64,256]{1,0:T(8,128)(2,1)S(1)} %get-tuple-element.132), channel_id=1, source_target_pairs={{0,7},{1,2},{2,1},{3,4},{4,3},{5,6},{6,5},{7,0},{8,15},{9,10},{10,... | collective-permute-start | bytes 98312 | tf_op jit(solution)/shard_map/ppermute | solution.py:620
  30.6 3.7 %k_second.1 = (bf16[2304,256]{1,0:T(8,128)(2,1)S(1)}, bf16[2304,256]{1,0:T(8,128)(2,1)S(1)}, f32[192,256]{1,0:T(8,128)S(1)}) custom-call(bf16[2400,768]{1,0:T(8,128)(2,1)S(1)} %get-tuple-element.59.frame, bf16[2304,256]{1,0:T(8,128)(2,1)S(1)} %bitcast.18, bf16[3,768,256]{2,1,0:T(8,128)(2,1)S(1)} %bitcast.19, ...), custom_call_target="tpu_custom_call" | custom-call | flops 2717908992 | bytes 4194304 | tf_op jit(solution)/shard_map/k_second/pallas_call | solution.py:586
  36.4 3.1 %collective-permute-start.8 = (bf16[64,256]{1,0:T(8,128)(2,1)S(1)}, bf16[64,256]{1,0:T(8,128)(2,1)S(1)}, u32[]{:S(2)}, u32[]{:S(2)}) collective-permute-start(bf16[64,256]{1,0:T(8,128)(2,1)S(1)} %get-tuple-element.102), channel_id=1, source_target_pairs={{0,8},{8,0},{16,24},{24,16},{32,40},{40,32},{48,56},{56,48},{64,72... | collective-permute-start | bytes 98312 | tf_op jit(solution)/shard_map/ppermute | solution.py:613
  40.3 2.5 %collective-permute-done.9.right = bf16[64,256]{1,0:T(8,128)(2,1)S(1)} collective-permute-done((bf16[64,256]{1,0:T(8,128)(2,1)S(1)}, bf16[64,256]{1,0:T(8,128)(2,1)S(1)}, u32[]{:S(2)}, u32[]{:S(2)}) %collective-permute-start.9) | collective-permute-done | bytes 32800 | tf_op jit(solution)/shard_map/ppermute | solution.py:614
  42.9 3.6 %collective-permute-start.11 = (bf16[64,256]{1,0:T(8,128)(2,1)S(1)}, bf16[64,256]{1,0:T(8,128)(2,1)S(1)}, u32[]{:S(2)}, u32[]{:S(2)}) collective-permute-start(bf16[64,256]{1,0:T(8,128)(2,1)S(1)} %get-tuple-element.130), channel_id=1, source_target_pairs={{0,7},{1,2},{2,1},{3,4},{4,3},{5,6},{6,5},{7,0},{8,15},{9,10},{10,... | collective-permute-start | bytes 98312 | tf_op jit(solution)/shard_map/ppermute | solution.py:620
  46.5 6.9 %k_second_back.1 = (bf16[1152,256]{1,0:T(8,128)(2,1)S(1)}, bf16[1152,256]{1,0:T(8,128)(2,1)S(1)}, bf16[2304,256]{1,0:T(8,128)(2,1)S(1)}, f32[192,256]{1,0:T(8,128)S(1)}) custom-call(s32[5]{0:T(128)S(1)} %stack.23.at, bf16[192,256]{1,0:T(8,128)(2,1)S(1)} %get-tuple-element.62.de, bf16[192,768]{1,0:T(8,128)(2,1)S(1)} %get-tuple-element.63.halo, ...), custom_call_target="tpu_custom_call" | custom-call | flops 5435817984 | bytes 4194304 | tf_op jit(solution)/shard_map/k_second_back/pallas_call | solution.py:586
  53.4 2.6 %collective-permute-start.13 = (bf16[1152,256]{1,0:T(8,128)(2,1)S(1)}, bf16[1152,256]{1,0:T(8,128)(2,1)S(1)}, u32[]{:S(2)}, u32[]{:S(2)}) collective-permute-start(bf16[1152,256]{1,0:T(8,128)(2,1)S(1)} %get-tuple-element.76), channel_id=1, source_target_pairs={{0,8},{1,9},{2,10},{3,11},{4,12},{5,13},{6,14},{7,15},{8,0},{9,1},... | collective-permute-start | bytes 1769480 | tf_op jit(solution)/shard_map/ppermute | solution.py:655
  57.6 3.4 %k_first_send.1 = (bf16[1152,256]{1,0:T(8,128)(2,1)S(1)}, bf16[2400,768]{1,0:T(8,128)(2,1)S(1)}, f32[3072,256]{1,0:T(8,128)S(1)}) custom-call(s32[5]{0:T(128)S(1)} %stack.23.at, bf16[192,256]{1,0:T(8,128)(2,1)S(1)} %get-tuple-element.69.de, bf16[192,768]{1,0:T(8,128)(2,1)S(1)} %get-tuple-element.70.halo, bf16[2304,256]{1,0:T(8,128)(2,1)S(1)} %get-tuple-element.71.delta0, ...), custom_call_target="tpu_custom_call" | custom-call | flops 2717908992 | bytes 4194304 | tf_op jit(solution)/shard_map/k_first_send/pallas_call | solution.py:586
  61.2 2.2 %k_first_keep.1.keep1 = bf16[1152,256]{1,0:T(8,128)(2,1)S(1)} custom-call(s32[5]{0:T(128)S(1)} %stack.23.at, bf16[256,2304]{1,0:T(8,128)(2,1)S(1)} %get-tuple-element.52.xt, bf16[2400,768]{1,0:T(8,128)(2,1)S(1)} %get-tuple-element.72.frame, f32[3072,256]{1,0:T(8,128)S(1)} %get-tuple-element.73.side), custom_call_target="tpu_custom_call" | custom-call | flops 2717908992 | bytes 4194304 | tf_op jit(solution)/shard_map/k_first_keep/pallas_call | solution.py:586
  65.7 3.3 %collective-permute-start.19 = (bf16[576,256]{1,0:T(8,128)(2,1)S(1)}, bf16[576,256]{1,0:T(8,128)(2,1)S(1)}, u32[]{:S(2)}, u32[]{:S(2)}) collective-permute-start(bf16[576,256]{1,0:T(8,128)(2,1)S(1)} %get-tuple-element.83), channel_id=1, source_target_pairs={{0,3},{1,2},{2,1},{3,0},{4,7},{5,6},{6,5},{7,4},{8,11},{9,10},{10,... | collective-permute-start | bytes 884744 | tf_op jit(solution)/shard_map/ppermute | solution.py:655
  71.0 3.7 %k_input_middle.1.refs_0_.middle = f32[2304,256]{1,0:T(8,128)S(1)} custom-call(bf16[192,256]{1,0:T(8,128)(2,1)S(1)} %get-tuple-element.69.de, bf16[2304,256]{1,0:T(8,128)(2,1)S(1)} %get-tuple-element.71.delta0, bf16[3,768,256]{2,1,0:T(8,128)(2,1)S(1)} %bitcast.17, bf16[64,256]{1,0:T(8,128)(2,1)S(1)} %collective-permute-done.14.after.left), custom_call_target="tpu_custom_call" | custom-call | flops 2717908992 | bytes 4194304 | tf_op jit(solution)/shard_map/k_input_middle/pallas_call | solution.py:586
  75.8 5.1 %collective-permute-done.16.refs_1_.up = bf16[64,256]{1,0:T(8,128)(2,1)S(1)} collective-permute-done((bf16[64,256]{1,0:T(8,128)(2,1)S(1)}, bf16[64,256]{1,0:T(8,128)(2,1)S(1)}, u32[]{:S(2)}, u32[]{:S(2)}) %collective-permute-start.16) | collective-permute-done | bytes 32800 | tf_op jit(solution)/shard_map/ppermute | solution.py:620
  83.3 3.1 %collective-permute-start.23 = (bf16[144,256]{1,0:T(8,128)(2,1)S(1)}, bf16[144,256]{1,0:T(8,128)(2,1)S(1)}, u32[]{:S(2)}, u32[]{:S(2)}) collective-permute-start(bf16[144,256]{1,0:T(8,128)(2,1)S(1)} %get-tuple-element.88), channel_id=1, source_target_pairs={{0,64},{1,65},{2,66},{3,67},{4,68},{5,69},{6,70},{7,71},{8,72},{9,... | collective-permute-start | bytes 221192 | tf_op jit(solution)/shard_map/ppermute | solution.py:655
  86.5 3.3 %collective-permute-done.22.g3 = bf16[144,256]{1,0:T(8,128)(2,1)S(1)} collective-permute-done((bf16[144,256]{1,0:T(8,128)(2,1)S(1)}, bf16[144,256]{1,0:T(8,128)(2,1)S(1)}, u32[]{:S(2)}, u32[]{:S(2)}) %collective-permute-start.22) | collective-permute-done | bytes 73760 | tf_op jit(solution)/shard_map/ppermute | solution.py:655
  90.0 2.1 %collective-permute-start.25 = (bf16[144,256]{1,0:T(8,128)(2,1)S(1)}, bf16[144,256]{1,0:T(8,128)(2,1)S(1)}, u32[]{:S(2)}, u32[]{:S(2)}) collective-permute-start(bf16[144,256]{1,0:T(8,128)(2,1)S(1)} %k_y_sum.1.after.own), channel_id=1, source_target_pairs={{0,20},{1,21},{2,22},{3,23},{4,16},{5,17},{6,18},{7,19},{8,28},{9,... | collective-permute-start | bytes 221192 | tf_op jit(solution)/shard_map/ppermute | solution.py:655
  92.6 2.2 %collective-permute-done.26.g2 = bf16[144,256]{1,0:T(8,128)(2,1)S(1)} collective-permute-done((bf16[144,256]{1,0:T(8,128)(2,1)S(1)}, bf16[144,256]{1,0:T(8,128)(2,1)S(1)}, u32[]{:S(2)}, u32[]{:S(2)}) %collective-permute-start.26) | collective-permute-done | bytes 73760 | tf_op jit(solution)/shard_map/ppermute | solution.py:655
  99.0 2.5 %k_input_grad.1 = (bf16[2304,256]{1,0:T(8,128)(2,1)}, bf16[2304,256]{1,0:T(8,128)(2,1)}, f32[8,128]{1,0:T(8,128)S(1)}) custom-call(s32[26]{0:T(128)S(1)} %get-tuple-element.50.lk, bf16[64,256]{1,0:T(8,128)(2,1)S(1)} %collective-permute-done.16.refs_1_.up, bf16[64,256]{1,0:T(8,128)(2,1)S(1)} %collective-permute-done.14.after.left, ...), custom_call_target="tpu_custom_call" | custom-call | bytes 4194304 | tf_op jit(solution)/shard_map/k_input_grad/pallas_call | solution.py:586
  106.0 5.2 %collective-permute-start.30 = (bf16[576,256]{1,0:T(8,128)(2,1)S(1)}, bf16[576,256]{1,0:T(8,128)(2,1)S(1)}, u32[]{:S(2)}, u32[]{:S(2)}) collective-permute-start(bf16[576,256]{1,0:T(8,128)(2,1)S(1)} %k_join.1.a0.after), channel_id=1, source_target_pairs={{0,8},{1,9},{2,10},{3,11},{4,12},{5,13},{6,14},{7,15},{8,0},{9,1},... | collective-permute-start | bytes 884744 | tf_op jit(solution)/shard_map/ppermute | solution.py:655
  111.2 6.0 %collective-permute-start.36 = (bf16[576,256]{1,0:T(8,128)(2,1)S(1)}, bf16[576,256]{1,0:T(8,128)(2,1)S(1)}, u32[]{:S(2)}, u32[]{:S(2)}) collective-permute-start(bf16[576,256]{1,0:T(8,128)(2,1)S(1)} %collective-permute-done.35.a2), channel_id=1, source_target_pairs={{0,8},{1,9},{2,10},{3,11},{4,12},{5,13},{6,14},{7,15},{8,0},{9,1},... | collective-permute-start | bytes 884744 | tf_op jit(solution)/shard_map/ppermute | solution.py:655
  117.2 3.0 %collective-permute-start.34 = (bf16[576,256]{1,0:T(8,128)(2,1)S(1)}, bf16[576,256]{1,0:T(8,128)(2,1)S(1)}, u32[]{:S(2)}, u32[]{:S(2)}) collective-permute-start(bf16[576,256]{1,0:T(8,128)(2,1)S(1)} %collective-permute-done.33.a3), channel_id=1, source_target_pairs={{0,8},{1,9},{2,10},{3,11},{4,12},{5,13},{6,14},{7,15},{8,0},{9,1},... | collective-permute-start | bytes 884744 | tf_op jit(solution)/shard_map/ppermute | solution.py:655
  (106 shorter events, 37.6 us)
Async XLA Ops:
  9.5 10.2 %collective-permute-start.3 = (bf16[64,256]{1,0:T(8,128)(2,1)S(1)}, bf16[64,256]{1,0:T(8,128)(2,1)S(1)}, u32[]{:S(2)}, u32[]{:S(2)}) collective-permute-start(bf16[64,256]{1,0:T(8,128)(2,1)S(1)} %get-tuple-element.134), channel_id=1, source_target_pairs={{0,7},{1,2},{2,1},{3,4},{4,3},{5,6},{6,5},{7,0},{8,15},{9,10},{10,... | collective-permute-start | bytes 98312 | tf_op jit(solution)/shard_map/ppermute | solution.py:620
  27.2 7.1 %collective-permute-start.7 = (bf16[64,256]{1,0:T(8,128)(2,1)S(1)}, bf16[64,256]{1,0:T(8,128)(2,1)S(1)}, u32[]{:S(2)}, u32[]{:S(2)}) collective-permute-start(bf16[64,256]{1,0:T(8,128)(2,1)S(1)} %get-tuple-element.132), channel_id=1, source_target_pairs={{0,7},{1,2},{2,1},{3,4},{4,3},{5,6},{6,5},{7,0},{8,15},{9,10},{10,... | collective-permute-start | bytes 98312 | tf_op jit(solution)/shard_map/ppermute | solution.py:620
  42.9 13.1 %collective-permute-start.11 = (bf16[64,256]{1,0:T(8,128)(2,1)S(1)}, bf16[64,256]{1,0:T(8,128)(2,1)S(1)}, u32[]{:S(2)}, u32[]{:S(2)}) collective-permute-start(bf16[64,256]{1,0:T(8,128)(2,1)S(1)} %get-tuple-element.130), channel_id=1, source_target_pairs={{0,7},{1,2},{2,1},{3,4},{4,3},{5,6},{6,5},{7,0},{8,15},{9,10},{10,... | collective-permute-start | bytes 98312 | tf_op jit(solution)/shard_map/ppermute | solution.py:620
  46.5 9.5 %collective-permute-start.10 = (bf16[64,256]{1,0:T(8,128)(2,1)S(1)}, bf16[64,256]{1,0:T(8,128)(2,1)S(1)}, u32[]{:S(2)}, u32[]{:S(2)}) collective-permute-start(bf16[64,256]{1,0:T(8,128)(2,1)S(1)} %get-tuple-element.131), channel_id=1, source_target_pairs={{0,1},{1,0},{2,3},{3,2},{4,5},{5,4},{6,7},{7,6},{8,9},{9,8},{10,11... | collective-permute-start | bytes 98312 | tf_op jit(solution)/shard_map/ppermute | solution.py:620
  53.4 10.0 %collective-permute-start.13 = (bf16[1152,256]{1,0:T(8,128)(2,1)S(1)}, bf16[1152,256]{1,0:T(8,128)(2,1)S(1)}, u32[]{:S(2)}, u32[]{:S(2)}) collective-permute-start(bf16[1152,256]{1,0:T(8,128)(2,1)S(1)} %get-tuple-element.76), channel_id=1, source_target_pairs={{0,8},{1,9},{2,10},{3,11},{4,12},{5,13},{6,14},{7,15},{8,0},{9,1},... | collective-permute-start | bytes 1769480 | tf_op jit(solution)/shard_map/ppermute | solution.py:655
  64.2 4.8 %collective-permute-start.14 = (bf16[64,256]{1,0:T(8,128)(2,1)S(1)}, bf16[64,256]{1,0:T(8,128)(2,1)S(1)}, u32[]{:S(2)}, u32[]{:S(2)}) collective-permute-start(bf16[64,256]{1,0:T(8,128)(2,1)S(1)} %get-tuple-element.98), channel_id=1, source_target_pairs={{0,8},{8,0},{16,24},{24,16},{32,40},{40,32},{48,56},{56,48},{64,72... | collective-permute-start | bytes 98312 | tf_op jit(solution)/shard_map/ppermute | solution.py:613
  64.8 4.2 %collective-permute-start.15 = (bf16[64,256]{1,0:T(8,128)(2,1)S(1)}, bf16[64,256]{1,0:T(8,128)(2,1)S(1)}, u32[]{:S(2)}, u32[]{:S(2)}) collective-permute-start(bf16[64,256]{1,0:T(8,128)(2,1)S(1)} %get-tuple-element.99), channel_id=1, source_target_pairs={{0,120},{8,16},{16,8},{24,32},{32,24},{40,48},{48,40},{56,64},{64,... | collective-permute-start | bytes 98312 | tf_op jit(solution)/shard_map/ppermute | solution.py:614
  64.8 16.1 %collective-permute-start.18 = (bf16[576,256]{1,0:T(8,128)(2,1)S(1)}, bf16[576,256]{1,0:T(8,128)(2,1)S(1)}, u32[]{:S(2)}, u32[]{:S(2)}) collective-permute-start(bf16[576,256]{1,0:T(8,128)(2,1)S(1)} %get-tuple-element.82), channel_id=1, source_target_pairs={{0,2},{1,3},{2,0},{3,1},{4,6},{5,7},{6,4},{7,5},{8,10},{9,11},{10,... | collective-permute-start | bytes 884744 | tf_op jit(solution)/shard_map/ppermute | solution.py:655
  65.7 16.7 %collective-permute-start.19 = (bf16[576,256]{1,0:T(8,128)(2,1)S(1)}, bf16[576,256]{1,0:T(8,128)(2,1)S(1)}, u32[]{:S(2)}, u32[]{:S(2)}) collective-permute-start(bf16[576,256]{1,0:T(8,128)(2,1)S(1)} %get-tuple-element.83), channel_id=1, source_target_pairs={{0,3},{1,2},{2,1},{3,0},{4,7},{5,6},{6,5},{7,4},{8,11},{9,10},{10,... | collective-permute-start | bytes 884744 | tf_op jit(solution)/shard_map/ppermute | solution.py:655
  69.0 13.3 %collective-permute-start.20 = (bf16[576,256]{1,0:T(8,128)(2,1)S(1)}, bf16[576,256]{1,0:T(8,128)(2,1)S(1)}, u32[]{:S(2)}, u32[]{:S(2)}) collective-permute-start(bf16[576,256]{1,0:T(8,128)(2,1)S(1)} %get-tuple-element.84), channel_id=1, source_target_pairs={{0,1},{1,0},{2,3},{3,2},{4,5},{5,4},{6,7},{7,6},{8,9},{9,8},{10,11... | collective-permute-start | bytes 884744 | tf_op jit(solution)/shard_map/ppermute | solution.py:655
  69.2 6.6 %collective-permute-start.17 = (bf16[64,256]{1,0:T(8,128)(2,1)S(1)}, bf16[64,256]{1,0:T(8,128)(2,1)S(1)}, u32[]{:S(2)}, u32[]{:S(2)}) collective-permute-start(bf16[64,256]{1,0:T(8,128)(2,1)S(1)} %get-tuple-element.128), channel_id=1, source_target_pairs={{0,7},{1,2},{2,1},{3,4},{4,3},{5,6},{6,5},{7,0},{8,15},{9,10},{10,... | collective-permute-start | bytes 98312 | tf_op jit(solution)/shard_map/ppermute | solution.py:620
  71.0 9.9 %collective-permute-start.16 = (bf16[64,256]{1,0:T(8,128)(2,1)S(1)}, bf16[64,256]{1,0:T(8,128)(2,1)S(1)}, u32[]{:S(2)}, u32[]{:S(2)}) collective-permute-start(bf16[64,256]{1,0:T(8,128)(2,1)S(1)} %get-tuple-element.129), channel_id=1, source_target_pairs={{0,1},{1,0},{2,3},{3,2},{4,5},{5,4},{6,7},{7,6},{8,9},{9,8},{10,11... | collective-permute-start | bytes 98312 | tf_op jit(solution)/shard_map/ppermute | solution.py:620
  83.3 6.6 %collective-permute-start.22 = (bf16[144,256]{1,0:T(8,128)(2,1)S(1)}, bf16[144,256]{1,0:T(8,128)(2,1)S(1)}, u32[]{:S(2)}, u32[]{:S(2)}) collective-permute-start(bf16[144,256]{1,0:T(8,128)(2,1)S(1)} %get-tuple-element.87), channel_id=1, source_target_pairs={{0,96},{1,97},{2,98},{3,99},{4,100},{5,101},{6,102},{7,103},{8,104... | collective-permute-start | bytes 221192 | tf_op jit(solution)/shard_map/ppermute | solution.py:655
  83.3 6.5 %collective-permute-start.23 = (bf16[144,256]{1,0:T(8,128)(2,1)S(1)}, bf16[144,256]{1,0:T(8,128)(2,1)S(1)}, u32[]{:S(2)}, u32[]{:S(2)}) collective-permute-start(bf16[144,256]{1,0:T(8,128)(2,1)S(1)} %get-tuple-element.88), channel_id=1, source_target_pairs={{0,64},{1,65},{2,66},{3,67},{4,68},{5,69},{6,70},{7,71},{8,72},{9,... | collective-permute-start | bytes 221192 | tf_op jit(solution)/shard_map/ppermute | solution.py:655
  89.9 4.9 %collective-permute-start.26 = (bf16[144,256]{1,0:T(8,128)(2,1)S(1)}, bf16[144,256]{1,0:T(8,128)(2,1)S(1)}, u32[]{:S(2)}, u32[]{:S(2)}) collective-permute-start(bf16[144,256]{1,0:T(8,128)(2,1)S(1)} %k_y_sum.1.after.own), channel_id=1, source_target_pairs={{0,4},{1,5},{2,6},{3,7},{4,0},{5,1},{6,2},{7,3},{8,12},{9,13},{10,... | collective-permute-start | bytes 221192 | tf_op jit(solution)/shard_map/ppermute | solution.py:655
  90.0 5.3 %collective-permute-start.25 = (bf16[144,256]{1,0:T(8,128)(2,1)S(1)}, bf16[144,256]{1,0:T(8,128)(2,1)S(1)}, u32[]{:S(2)}, u32[]{:S(2)}) collective-permute-start(bf16[144,256]{1,0:T(8,128)(2,1)S(1)} %k_y_sum.1.after.own), channel_id=1, source_target_pairs={{0,20},{1,21},{2,22},{3,23},{4,16},{5,17},{6,18},{7,19},{8,28},{9,... | collective-permute-start | bytes 221192 | tf_op jit(solution)/shard_map/ppermute | solution.py:655
  95.3 6.2 %collective-permute-start.29 = (bf16[144,256]{1,0:T(8,128)(2,1)S(1)}, bf16[144,256]{1,0:T(8,128)(2,1)S(1)}, u32[]{:S(2)}, u32[]{:S(2)}) collective-permute-start(bf16[144,256]{1,0:T(8,128)(2,1)S(1)} %k_x_sum.1.own), channel_id=1, source_target_pairs={{0,64},{1,65},{2,66},{3,67},{4,68},{5,69},{6,70},{7,71},{8,72},{9,... | collective-permute-start | bytes 221192 | tf_op jit(solution)/shard_map/ppermute | solution.py:655
  97.0 4.6 %collective-permute-start.28 = (bf16[144,256]{1,0:T(8,128)(2,1)S(1)}, bf16[144,256]{1,0:T(8,128)(2,1)S(1)}, u32[]{:S(2)}, u32[]{:S(2)}) collective-permute-start(bf16[144,256]{1,0:T(8,128)(2,1)S(1)} %k_x_sum.1.own), channel_id=1, source_target_pairs={{0,96},{1,97},{2,98},{3,99},{4,100},{5,101},{6,102},{7,103},{8,104... | collective-permute-start | bytes 221192 | tf_op jit(solution)/shard_map/ppermute | solution.py:655
  102.9 8.3 %collective-permute-start.35 = (bf16[576,256]{1,0:T(8,128)(2,1)S(1)}, bf16[576,256]{1,0:T(8,128)(2,1)S(1)}, u32[]{:S(2)}, u32[]{:S(2)}) collective-permute-start(bf16[576,256]{1,0:T(8,128)(2,1)S(1)} %k_join.1.a0.after), channel_id=1, source_target_pairs={{0,2},{1,3},{2,0},{3,1},{4,6},{5,7},{6,4},{7,5},{8,10},{9,11},{10,... | collective-permute-start | bytes 884744 | tf_op jit(solution)/shard_map/ppermute | solution.py:655
  104.7 12.5 %collective-permute-start.33 = (bf16[576,256]{1,0:T(8,128)(2,1)S(1)}, bf16[576,256]{1,0:T(8,128)(2,1)S(1)}, u32[]{:S(2)}, u32[]{:S(2)}) collective-permute-start(bf16[576,256]{1,0:T(8,128)(2,1)S(1)} %k_join.1.a0.after), channel_id=1, source_target_pairs={{0,3},{1,2},{2,1},{3,0},{4,7},{5,6},{6,5},{7,4},{8,11},{9,10},{10,... | collective-permute-start | bytes 884744 | tf_op jit(solution)/shard_map/ppermute | solution.py:655
  106.0 14.2 %collective-permute-start.31 = (bf16[576,256]{1,0:T(8,128)(2,1)S(1)}, bf16[576,256]{1,0:T(8,128)(2,1)S(1)}, u32[]{:S(2)}, u32[]{:S(2)}) collective-permute-start(bf16[576,256]{1,0:T(8,128)(2,1)S(1)} %k_join.1.a0.after), channel_id=1, source_target_pairs={{0,1},{1,0},{2,3},{3,2},{4,5},{5,4},{6,7},{7,6},{8,9},{9,8},{10,11... | collective-permute-start | bytes 884744 | tf_op jit(solution)/shard_map/ppermute | solution.py:655
  106.0 16.2 %collective-permute-start.30 = (bf16[576,256]{1,0:T(8,128)(2,1)S(1)}, bf16[576,256]{1,0:T(8,128)(2,1)S(1)}, u32[]{:S(2)}, u32[]{:S(2)}) collective-permute-start(bf16[576,256]{1,0:T(8,128)(2,1)S(1)} %k_join.1.a0.after), channel_id=1, source_target_pairs={{0,8},{1,9},{2,10},{3,11},{4,12},{5,13},{6,14},{7,15},{8,0},{9,1},... | collective-permute-start | bytes 884744 | tf_op jit(solution)/shard_map/ppermute | solution.py:655
  111.2 11.1 %collective-permute-start.36 = (bf16[576,256]{1,0:T(8,128)(2,1)S(1)}, bf16[576,256]{1,0:T(8,128)(2,1)S(1)}, u32[]{:S(2)}, u32[]{:S(2)}) collective-permute-start(bf16[576,256]{1,0:T(8,128)(2,1)S(1)} %collective-permute-done.35.a2), channel_id=1, source_target_pairs={{0,8},{1,9},{2,10},{3,11},{4,12},{5,13},{6,14},{7,15},{8,0},{9,1},... | collective-permute-start | bytes 884744 | tf_op jit(solution)/shard_map/ppermute | solution.py:655
  117.2 5.1 %collective-permute-start.34 = (bf16[576,256]{1,0:T(8,128)(2,1)S(1)}, bf16[576,256]{1,0:T(8,128)(2,1)S(1)}, u32[]{:S(2)}, u32[]{:S(2)}) collective-permute-start(bf16[576,256]{1,0:T(8,128)(2,1)S(1)} %collective-permute-done.33.a3), channel_id=1, source_target_pairs={{0,8},{1,9},{2,10},{3,11},{4,12},{5,13},{6,14},{7,15},{8,0},{9,1},... | collective-permute-start | bytes 884744 | tf_op jit(solution)/shard_map/ppermute | solution.py:655
  (17 other events, 70.5 us)

commit v6 on v5

--- a/solution.py
+++ b/solution.py
@@ -450,9 +450,7 @@
         rows = pl.ds(pl.multiple_of((2 - a) * S, 16), CELLS)
         lanes = pl.ds(pl.multiple_of(b * C, C), C)
         part = dot(xt[...], frame[rows, lanes])
-        for k, (used, at) in enumerate(((a == 0, b), (a == 2, b), (b == 0, a), (b == 2, a))):
-            term = side[pl.ds(pl.multiple_of(k * 3 * C + at * C, C), C)]
-            part = part + jnp.where(used, term, 0.0)
+        part = part + side[pl.ds(pl.multiple_of(tap * C, C), C)]
         out[pl.ds(pl.multiple_of(n * C + h * (C // 2), C // 2), C)] = part.astype(BF)
     part = dot(xt[pl.ds(pl.multiple_of(h * (C // 2), C // 2), C // 2)], frame[pl.ds(S, CELLS), C : 2 * C])
     out[pl.ds(pl.multiple_of((1 - h) * 4 * C, C), C // 2)] = part.astype(BF)
@@ -463,13 +461,24 @@
     x[...] = delta0[...].astype(F32)
     put_edges(x, edges)
     spread_columns(x, frame, 2, 0)
-    for s in range(4):
-        side[pl.ds(s * 3 * C, 3 * C)] = lax.dot_general(
+    terms = [
+        lax.dot_general(
             halo[s * S : (s + 1) * S],
             de[s * S : (s + 1) * S],
             (((0,), (0,)), ((), ())),
             preferred_element_type=F32,
         )
+        for s in range(4)
+    ]
+    for a in range(3):
+        for b in range(3):
+            total = None
+            for s, used, n in ((0, a == 0, b), (1, a == 2, b), (2, b == 0, a), (3, b == 2, a)):
+                if used:
+                    term = terms[s][n * C : (n + 1) * C]
+                    total = term if total is None else total + term
+            if total is not None:
+                side[pl.ds((a * 3 + b) * C, C)] = total
     half_sums(1 - at[0], xt, frame, side, send)
 
 
@@ -744,7 +753,7 @@
     send1, frame, side = call(
         k_first_send,
         [fd_e, halo1, fd0, xt1],
-        [half_bf, frame_bf, ((12 * C, C), F32, 1)],
+        [half_bf, frame_bf, ((9 * C, C), F32, 1)],
         [WIDE[0], WIDER[2]],
         links=at,
         flops=work,

time: 125 us -> 125 us (level)
  no operation moved by 1% of the time
where the time goes in v6:
time: 125 us; the launch traced here: 124 us
  starting transfers between devices  58.3 us (47%)
  Pallas kernels  41.7 us (33%)
  waiting for transfers between devices  20.3 us (16%)
  local copies, waits for them, and re-layouts  2.55 us (2%)
    pallas_call x21, Pallas kernels, call(): pl.pallas_call(kernel, out_shape=[(pltpu.VMEM if len(out) > 2 else jax.Sh...  40.2 us
    ppermute x21, starting transfers between devices, move(): return lax.ppermute(x, ('tile', 'lat'), exchange(kind, step))  33.9 us
    ppermute x4, starting transfers between devices, trade_lat(): lax.ppermute(to_b, 'lat', pairs_b(n))  15.2 us
    ppermute x21, waiting for transfers between devices, move(): return lax.ppermute(x, ('tile', 'lat'), exchange(kind, step))  8.31 us
    ppermute x4, starting transfers between devices, trade_tile(): from_a = lax.ppermute(pk[PK:2 * PK], 'tile', pairs_a(n))  7.79 us
    ppermute x4, waiting for transfers between devices, trade_tile(): from_b = lax.ppermute(pk[2 * PK:3 * PK], 'tile', pairs_b(n))  5.76 us
    ppermute x4, waiting for transfers between devices, trade_lat(): lax.ppermute(to_a, 'lat', pairs_a(n))  5.1 us
  transfers between devices with their start and end apart: 37, of which 11 were waited for; matrix products, arithmetic and copies ran while one was open for 0% of the time, Pallas kernels for 26%

profile of v6, /device:TPU:1, one launch (start us, length us, event | category | flops | bytes accessed | tf_op | source)
XLA Modules:
  0.0 124.4 jit_solution(4019337061810664342)
XLA Ops:
  9.5 6.4 %collective-permute-start.3 = (bf16[64,256]{1,0:T(8,128)(2,1)S(1)}, bf16[64,256]{1,0:T(8,128)(2,1)S(1)}, u32[]{:S(2)}, u32[]{:S(2)}) collective-permute-start(bf16[64,256]{1,0:T(8,128)(2,1)S(1)} %get-tuple-element.134), channel_id=1, source_target_pairs={{0,7},{1,2},{2,1},{3,4},{4,3},{5,6},{6,5},{7,0},{8,15},{9,10},{10,... | collective-permute-start | bytes 98312 | tf_op jit(solution)/shard_map/ppermute | solution.py:629
  15.9 3.5 %k_first.1 = (bf16[2304,256]{1,0:T(8,128)(2,1)S(1)}, f32[2304,256]{1,0:T(8,128)S(1)}, f32[192,256]{1,0:T(8,128)S(1)}) custom-call(bf16[2400,768]{1,0:T(8,128)(2,1)S(1)} %get-tuple-element.54.frame, bf16[3,768,256]{2,1,0:T(8,128)(2,1)S(1)} %bitcast.14, bf16[64,256]{1,0:T(8,128)(2,1)S(1)} %collective-permute-done.after.left), custom_call_target="tpu_custom_call" | custom-call | flops 2717908992 | bytes 4194304 | tf_op jit(solution)/shard_map/k_first/pallas_call | solution.py:595
  21.1 2.7 %collective-permute-start.4 = (bf16[64,256]{1,0:T(8,128)(2,1)S(1)}, bf16[64,256]{1,0:T(8,128)(2,1)S(1)}, u32[]{:S(2)}, u32[]{:S(2)}) collective-permute-start(bf16[64,256]{1,0:T(8,128)(2,1)S(1)} %get-tuple-element.106), channel_id=1, source_target_pairs={{0,8},{8,0},{16,24},{24,16},{32,40},{40,32},{48,56},{56,48},{64,72... | collective-permute-start | bytes 98312 | tf_op jit(solution)/shard_map/ppermute | solution.py:622
  24.7 2.4 %collective-permute-done.5.right = bf16[64,256]{1,0:T(8,128)(2,1)S(1)} collective-permute-done((bf16[64,256]{1,0:T(8,128)(2,1)S(1)}, bf16[64,256]{1,0:T(8,128)(2,1)S(1)}, u32[]{:S(2)}, u32[]{:S(2)}) %collective-permute-start.5) | collective-permute-done | bytes 32800 | tf_op jit(solution)/shard_map/ppermute | solution.py:623
  27.2 3.4 %collective-permute-start.7 = (bf16[64,256]{1,0:T(8,128)(2,1)S(1)}, bf16[64,256]{1,0:T(8,128)(2,1)S(1)}, u32[]{:S(2)}, u32[]{:S(2)}) collective-permute-start(bf16[64,256]{1,0:T(8,128)(2,1)S(1)} %get-tuple-element.132), channel_id=1, source_target_pairs={{0,7},{1,2},{2,1},{3,4},{4,3},{5,6},{6,5},{7,0},{8,15},{9,10},{10,... | collective-permute-start | bytes 98312 | tf_op jit(solution)/shard_map/ppermute | solution.py:629
  30.6 3.7 %k_second.1 = (bf16[2304,256]{1,0:T(8,128)(2,1)S(1)}, bf16[2304,256]{1,0:T(8,128)(2,1)S(1)}, f32[192,256]{1,0:T(8,128)S(1)}) custom-call(bf16[2400,768]{1,0:T(8,128)(2,1)S(1)} %get-tuple-element.59.frame, bf16[2304,256]{1,0:T(8,128)(2,1)S(1)} %bitcast.18, bf16[3,768,256]{2,1,0:T(8,128)(2,1)S(1)} %bitcast.19, ...), custom_call_target="tpu_custom_call" | custom-call | flops 2717908992 | bytes 4194304 | tf_op jit(solution)/shard_map/k_second/pallas_call | solution.py:595
  36.4 3.1 %collective-permute-start.8 = (bf16[64,256]{1,0:T(8,128)(2,1)S(1)}, bf16[64,256]{1,0:T(8,128)(2,1)S(1)}, u32[]{:S(2)}, u32[]{:S(2)}) collective-permute-start(bf16[64,256]{1,0:T(8,128)(2,1)S(1)} %get-tuple-element.102), channel_id=1, source_target_pairs={{0,8},{8,0},{16,24},{24,16},{32,40},{40,32},{48,56},{56,48},{64,72... | collective-permute-start | bytes 98312 | tf_op jit(solution)/shard_map/ppermute | solution.py:622
  40.3 2.5 %collective-permute-done.9.right = bf16[64,256]{1,0:T(8,128)(2,1)S(1)} collective-permute-done((bf16[64,256]{1,0:T(8,128)(2,1)S(1)}, bf16[64,256]{1,0:T(8,128)(2,1)S(1)}, u32[]{:S(2)}, u32[]{:S(2)}) %collective-permute-start.9) | collective-permute-done | bytes 32800 | tf_op jit(solution)/shard_map/ppermute | solution.py:623
  42.9 3.6 %collective-permute-start.11 = (bf16[64,256]{1,0:T(8,128)(2,1)S(1)}, bf16[64,256]{1,0:T(8,128)(2,1)S(1)}, u32[]{:S(2)}, u32[]{:S(2)}) collective-permute-start(bf16[64,256]{1,0:T(8,128)(2,1)S(1)} %get-tuple-element.130), channel_id=1, source_target_pairs={{0,7},{1,2},{2,1},{3,4},{4,3},{5,6},{6,5},{7,0},{8,15},{9,10},{10,... | collective-permute-start | bytes 98312 | tf_op jit(solution)/shard_map/ppermute | solution.py:629
  46.5 6.9 %k_second_back.1 = (bf16[1152,256]{1,0:T(8,128)(2,1)S(1)}, bf16[1152,256]{1,0:T(8,128)(2,1)S(1)}, bf16[2304,256]{1,0:T(8,128)(2,1)S(1)}, f32[192,256]{1,0:T(8,128)S(1)}) custom-call(s32[5]{0:T(128)S(1)} %stack.23.at, bf16[192,256]{1,0:T(8,128)(2,1)S(1)} %get-tuple-element.62.de, bf16[192,768]{1,0:T(8,128)(2,1)S(1)} %get-tuple-element.63.halo, ...), custom_call_target="tpu_custom_call" | custom-call | flops 5435817984 | bytes 4194304 | tf_op jit(solution)/shard_map/k_second_back/pallas_call | solution.py:595
  53.4 2.6 %collective-permute-start.13 = (bf16[1152,256]{1,0:T(8,128)(2,1)S(1)}, bf16[1152,256]{1,0:T(8,128)(2,1)S(1)}, u32[]{:S(2)}, u32[]{:S(2)}) collective-permute-start(bf16[1152,256]{1,0:T(8,128)(2,1)S(1)} %get-tuple-element.76), channel_id=1, source_target_pairs={{0,8},{1,9},{2,10},{3,11},{4,12},{5,13},{6,14},{7,15},{8,0},{9,1},... | collective-permute-start | bytes 1769480 | tf_op jit(solution)/shard_map/ppermute | solution.py:664
  57.6 3.4 %k_first_send.1 = (bf16[1152,256]{1,0:T(8,128)(2,1)S(1)}, bf16[2400,768]{1,0:T(8,128)(2,1)S(1)}, f32[2304,256]{1,0:T(8,128)S(1)}) custom-call(s32[5]{0:T(128)S(1)} %stack.23.at, bf16[192,256]{1,0:T(8,128)(2,1)S(1)} %get-tuple-element.69.de, bf16[192,768]{1,0:T(8,128)(2,1)S(1)} %get-tuple-element.70.halo, bf16[2304,256]{1,0:T(8,128)(2,1)S(1)} %get-tuple-element.71.delta0, ...), custom_call_target="tpu_custom_call" | custom-call | flops 2717908992 | bytes 4194304 | tf_op jit(solution)/shard_map/k_first_send/pallas_call | solution.py:595
  61.1 2.2 %k_first_keep.1.keep1 = bf16[1152,256]{1,0:T(8,128)(2,1)S(1)} custom-call(s32[5]{0:T(128)S(1)} %stack.23.at, bf16[256,2304]{1,0:T(8,128)(2,1)S(1)} %get-tuple-element.52.xt, bf16[2400,768]{1,0:T(8,128)(2,1)S(1)} %get-tuple-element.72.frame, f32[2304,256]{1,0:T(8,128)S(1)} %get-tuple-element.73.side), custom_call_target="tpu_custom_call" | custom-call | flops 2717908992 | bytes 4194304 | tf_op jit(solution)/shard_map/k_first_keep/pallas_call | solution.py:595
  65.6 3.3 %collective-permute-start.19 = (bf16[576,256]{1,0:T(8,128)(2,1)S(1)}, bf16[576,256]{1,0:T(8,128)(2,1)S(1)}, u32[]{:S(2)}, u32[]{:S(2)}) collective-permute-start(bf16[576,256]{1,0:T(8,128)(2,1)S(1)} %get-tuple-element.83), channel_id=1, source_target_pairs={{0,3},{1,2},{2,1},{3,0},{4,7},{5,6},{6,5},{7,4},{8,11},{9,10},{10,... | collective-permute-start | bytes 884744 | tf_op jit(solution)/shard_map/ppermute | solution.py:664
  70.9 3.7 %k_input_middle.1.refs_0_.middle = f32[2304,256]{1,0:T(8,128)S(1)} custom-call(bf16[192,256]{1,0:T(8,128)(2,1)S(1)} %get-tuple-element.69.de, bf16[2304,256]{1,0:T(8,128)(2,1)S(1)} %get-tuple-element.71.delta0, bf16[3,768,256]{2,1,0:T(8,128)(2,1)S(1)} %bitcast.17, bf16[64,256]{1,0:T(8,128)(2,1)S(1)} %collective-permute-done.14.after.left), custom_call_target="tpu_custom_call" | custom-call | flops 2717908992 | bytes 4194304 | tf_op jit(solution)/shard_map/k_input_middle/pallas_call | solution.py:595
  75.7 5.1 %collective-permute-done.16.refs_1_.up = bf16[64,256]{1,0:T(8,128)(2,1)S(1)} collective-permute-done((bf16[64,256]{1,0:T(8,128)(2,1)S(1)}, bf16[64,256]{1,0:T(8,128)(2,1)S(1)}, u32[]{:S(2)}, u32[]{:S(2)}) %collective-permute-start.16) | collective-permute-done | bytes 32800 | tf_op jit(solution)/shard_map/ppermute | solution.py:629
  83.2 3.1 %collective-permute-start.23 = (bf16[144,256]{1,0:T(8,128)(2,1)S(1)}, bf16[144,256]{1,0:T(8,128)(2,1)S(1)}, u32[]{:S(2)}, u32[]{:S(2)}) collective-permute-start(bf16[144,256]{1,0:T(8,128)(2,1)S(1)} %get-tuple-element.88), channel_id=1, source_target_pairs={{0,64},{1,65},{2,66},{3,67},{4,68},{5,69},{6,70},{7,71},{8,72},{9,... | collective-permute-start | bytes 221192 | tf_op jit(solution)/shard_map/ppermute | solution.py:664
  86.4 3.3 %collective-permute-done.22.g3 = bf16[144,256]{1,0:T(8,128)(2,1)S(1)} collective-permute-done((bf16[144,256]{1,0:T(8,128)(2,1)S(1)}, bf16[144,256]{1,0:T(8,128)(2,1)S(1)}, u32[]{:S(2)}, u32[]{:S(2)}) %collective-permute-start.22) | collective-permute-done | bytes 73760 | tf_op jit(solution)/shard_map/ppermute | solution.py:664
  89.8 2.1 %collective-permute-start.25 = (bf16[144,256]{1,0:T(8,128)(2,1)S(1)}, bf16[144,256]{1,0:T(8,128)(2,1)S(1)}, u32[]{:S(2)}, u32[]{:S(2)}) collective-permute-start(bf16[144,256]{1,0:T(8,128)(2,1)S(1)} %k_y_sum.1.after.own), channel_id=1, source_target_pairs={{0,20},{1,21},{2,22},{3,23},{4,16},{5,17},{6,18},{7,19},{8,28},{9,... | collective-permute-start | bytes 221192 | tf_op jit(solution)/shard_map/ppermute | solution.py:664
  92.5 2.2 %collective-permute-done.26.g2 = bf16[144,256]{1,0:T(8,128)(2,1)S(1)} collective-permute-done((bf16[144,256]{1,0:T(8,128)(2,1)S(1)}, bf16[144,256]{1,0:T(8,128)(2,1)S(1)}, u32[]{:S(2)}, u32[]{:S(2)}) %collective-permute-start.26) | collective-permute-done | bytes 73760 | tf_op jit(solution)/shard_map/ppermute | solution.py:664
  98.9 2.5 %k_input_grad.1 = (bf16[2304,256]{1,0:T(8,128)(2,1)}, bf16[2304,256]{1,0:T(8,128)(2,1)}, f32[8,128]{1,0:T(8,128)S(1)}) custom-call(s32[26]{0:T(128)S(1)} %get-tuple-element.50.lk, bf16[64,256]{1,0:T(8,128)(2,1)S(1)} %collective-permute-done.16.refs_1_.up, bf16[64,256]{1,0:T(8,128)(2,1)S(1)} %collective-permute-done.14.after.left, ...), custom_call_target="tpu_custom_call" | custom-call | bytes 4194304 | tf_op jit(solution)/shard_map/k_input_grad/pallas_call | solution.py:595
  105.9 5.2 %collective-permute-start.30 = (bf16[576,256]{1,0:T(8,128)(2,1)S(1)}, bf16[576,256]{1,0:T(8,128)(2,1)S(1)}, u32[]{:S(2)}, u32[]{:S(2)}) collective-permute-start(bf16[576,256]{1,0:T(8,128)(2,1)S(1)} %k_join.1.a0.after), channel_id=1, source_target_pairs={{0,8},{1,9},{2,10},{3,11},{4,12},{5,13},{6,14},{7,15},{8,0},{9,1},... | collective-permute-start | bytes 884744 | tf_op jit(solution)/shard_map/ppermute | solution.py:664
  111.1 6.0 %collective-permute-start.36 = (bf16[576,256]{1,0:T(8,128)(2,1)S(1)}, bf16[576,256]{1,0:T(8,128)(2,1)S(1)}, u32[]{:S(2)}, u32[]{:S(2)}) collective-permute-start(bf16[576,256]{1,0:T(8,128)(2,1)S(1)} %collective-permute-done.35.a2), channel_id=1, source_target_pairs={{0,8},{1,9},{2,10},{3,11},{4,12},{5,13},{6,14},{7,15},{8,0},{9,1},... | collective-permute-start | bytes 884744 | tf_op jit(solution)/shard_map/ppermute | solution.py:664
  117.1 3.0 %collective-permute-start.34 = (bf16[576,256]{1,0:T(8,128)(2,1)S(1)}, bf16[576,256]{1,0:T(8,128)(2,1)S(1)}, u32[]{:S(2)}, u32[]{:S(2)}) collective-permute-start(bf16[576,256]{1,0:T(8,128)(2,1)S(1)} %collective-permute-done.33.a3), channel_id=1, source_target_pairs={{0,8},{1,9},{2,10},{3,11},{4,12},{5,13},{6,14},{7,15},{8,0},{9,1},... | collective-permute-start | bytes 884744 | tf_op jit(solution)/shard_map/ppermute | solution.py:664
  (106 shorter events, 37.5 us)
Async XLA Ops:
  9.5 10.2 %collective-permute-start.3 = (bf16[64,256]{1,0:T(8,128)(2,1)S(1)}, bf16[64,256]{1,0:T(8,128)(2,1)S(1)}, u32[]{:S(2)}, u32[]{:S(2)}) collective-permute-start(bf16[64,256]{1,0:T(8,128)(2,1)S(1)} %get-tuple-element.134), channel_id=1, source_target_pairs={{0,7},{1,2},{2,1},{3,4},{4,3},{5,6},{6,5},{7,0},{8,15},{9,10},{10,... | collective-permute-start | bytes 98312 | tf_op jit(solution)/shard_map/ppermute | solution.py:629
  27.2 7.1 %collective-permute-start.7 = (bf16[64,256]{1,0:T(8,128)(2,1)S(1)}, bf16[64,256]{1,0:T(8,128)(2,1)S(1)}, u32[]{:S(2)}, u32[]{:S(2)}) collective-permute-start(bf16[64,256]{1,0:T(8,128)(2,1)S(1)} %get-tuple-element.132), channel_id=1, source_target_pairs={{0,7},{1,2},{2,1},{3,4},{4,3},{5,6},{6,5},{7,0},{8,15},{9,10},{10,... | collective-permute-start | bytes 98312 | tf_op jit(solution)/shard_map/ppermute | solution.py:629
  42.9 13.1 %collective-permute-start.11 = (bf16[64,256]{1,0:T(8,128)(2,1)S(1)}, bf16[64,256]{1,0:T(8,128)(2,1)S(1)}, u32[]{:S(2)}, u32[]{:S(2)}) collective-permute-start(bf16[64,256]{1,0:T(8,128)(2,1)S(1)} %get-tuple-element.130), channel_id=1, source_target_pairs={{0,7},{1,2},{2,1},{3,4},{4,3},{5,6},{6,5},{7,0},{8,15},{9,10},{10,... | collective-permute-start | bytes 98312 | tf_op jit(solution)/shard_map/ppermute | solution.py:629
  46.5 9.5 %collective-permute-start.10 = (bf16[64,256]{1,0:T(8,128)(2,1)S(1)}, bf16[64,256]{1,0:T(8,128)(2,1)S(1)}, u32[]{:S(2)}, u32[]{:S(2)}) collective-permute-start(bf16[64,256]{1,0:T(8,128)(2,1)S(1)} %get-tuple-element.131), channel_id=1, source_target_pairs={{0,1},{1,0},{2,3},{3,2},{4,5},{5,4},{6,7},{7,6},{8,9},{9,8},{10,11... | collective-permute-start | bytes 98312 | tf_op jit(solution)/shard_map/ppermute | solution.py:629
  53.4 9.9 %collective-permute-start.13 = (bf16[1152,256]{1,0:T(8,128)(2,1)S(1)}, bf16[1152,256]{1,0:T(8,128)(2,1)S(1)}, u32[]{:S(2)}, u32[]{:S(2)}) collective-permute-start(bf16[1152,256]{1,0:T(8,128)(2,1)S(1)} %get-tuple-element.76), channel_id=1, source_target_pairs={{0,8},{1,9},{2,10},{3,11},{4,12},{5,13},{6,14},{7,15},{8,0},{9,1},... | collective-permute-start | bytes 1769480 | tf_op jit(solution)/shard_map/ppermute | solution.py:664
  64.1 4.8 %collective-permute-start.14 = (bf16[64,256]{1,0:T(8,128)(2,1)S(1)}, bf16[64,256]{1,0:T(8,128)(2,1)S(1)}, u32[]{:S(2)}, u32[]{:S(2)}) collective-permute-start(bf16[64,256]{1,0:T(8,128)(2,1)S(1)} %get-tuple-element.98), channel_id=1, source_target_pairs={{0,8},{8,0},{16,24},{24,16},{32,40},{40,32},{48,56},{56,48},{64,72... | collective-permute-start | bytes 98312 | tf_op jit(solution)/shard_map/ppermute | solution.py:622
  64.7 4.2 %collective-permute-start.15 = (bf16[64,256]{1,0:T(8,128)(2,1)S(1)}, bf16[64,256]{1,0:T(8,128)(2,1)S(1)}, u32[]{:S(2)}, u32[]{:S(2)}) collective-permute-start(bf16[64,256]{1,0:T(8,128)(2,1)S(1)} %get-tuple-element.99), channel_id=1, source_target_pairs={{0,120},{8,16},{16,8},{24,32},{32,24},{40,48},{48,40},{56,64},{64,... | collective-permute-start | bytes 98312 | tf_op jit(solution)/shard_map/ppermute | solution.py:623
  64.7 16.1 %collective-permute-start.18 = (bf16[576,256]{1,0:T(8,128)(2,1)S(1)}, bf16[576,256]{1,0:T(8,128)(2,1)S(1)}, u32[]{:S(2)}, u32[]{:S(2)}) collective-permute-start(bf16[576,256]{1,0:T(8,128)(2,1)S(1)} %get-tuple-element.82), channel_id=1, source_target_pairs={{0,2},{1,3},{2,0},{3,1},{4,6},{5,7},{6,4},{7,5},{8,10},{9,11},{10,... | collective-permute-start | bytes 884744 | tf_op jit(solution)/shard_map/ppermute | solution.py:664
  65.6 16.7 %collective-permute-start.19 = (bf16[576,256]{1,0:T(8,128)(2,1)S(1)}, bf16[576,256]{1,0:T(8,128)(2,1)S(1)}, u32[]{:S(2)}, u32[]{:S(2)}) collective-permute-start(bf16[576,256]{1,0:T(8,128)(2,1)S(1)} %get-tuple-element.83), channel_id=1, source_target_pairs={{0,3},{1,2},{2,1},{3,0},{4,7},{5,6},{6,5},{7,4},{8,11},{9,10},{10,... | collective-permute-start | bytes 884744 | tf_op jit(solution)/shard_map/ppermute | solution.py:664
  68.9 13.3 %collective-permute-start.20 = (bf16[576,256]{1,0:T(8,128)(2,1)S(1)}, bf16[576,256]{1,0:T(8,128)(2,1)S(1)}, u32[]{:S(2)}, u32[]{:S(2)}) collective-permute-start(bf16[576,256]{1,0:T(8,128)(2,1)S(1)} %get-tuple-element.84), channel_id=1, source_target_pairs={{0,1},{1,0},{2,3},{3,2},{4,5},{5,4},{6,7},{7,6},{8,9},{9,8},{10,11... | collective-permute-start | bytes 884744 | tf_op jit(solution)/shard_map/ppermute | solution.py:664
  69.0 6.6 %collective-permute-start.17 = (bf16[64,256]{1,0:T(8,128)(2,1)S(1)}, bf16[64,256]{1,0:T(8,128)(2,1)S(1)}, u32[]{:S(2)}, u32[]{:S(2)}) collective-permute-start(bf16[64,256]{1,0:T(8,128)(2,1)S(1)} %get-tuple-element.128), channel_id=1, source_target_pairs={{0,7},{1,2},{2,1},{3,4},{4,3},{5,6},{6,5},{7,0},{8,15},{9,10},{10,... | collective-permute-start | bytes 98312 | tf_op jit(solution)/shard_map/ppermute | solution.py:629
  70.9 9.9 %collective-permute-start.16 = (bf16[64,256]{1,0:T(8,128)(2,1)S(1)}, bf16[64,256]{1,0:T(8,128)(2,1)S(1)}, u32[]{:S(2)}, u32[]{:S(2)}) collective-permute-start(bf16[64,256]{1,0:T(8,128)(2,1)S(1)} %get-tuple-element.129), channel_id=1, source_target_pairs={{0,1},{1,0},{2,3},{3,2},{4,5},{5,4},{6,7},{7,6},{8,9},{9,8},{10,11... | collective-permute-start | bytes 98312 | tf_op jit(solution)/shard_map/ppermute | solution.py:629
  83.1 6.6 %collective-permute-start.22 = (bf16[144,256]{1,0:T(8,128)(2,1)S(1)}, bf16[144,256]{1,0:T(8,128)(2,1)S(1)}, u32[]{:S(2)}, u32[]{:S(2)}) collective-permute-start(bf16[144,256]{1,0:T(8,128)(2,1)S(1)} %get-tuple-element.87), channel_id=1, source_target_pairs={{0,96},{1,97},{2,98},{3,99},{4,100},{5,101},{6,102},{7,103},{8,104... | collective-permute-start | bytes 221192 | tf_op jit(solution)/shard_map/ppermute | solution.py:664
  83.2 6.5 %collective-permute-start.23 = (bf16[144,256]{1,0:T(8,128)(2,1)S(1)}, bf16[144,256]{1,0:T(8,128)(2,1)S(1)}, u32[]{:S(2)}, u32[]{:S(2)}) collective-permute-start(bf16[144,256]{1,0:T(8,128)(2,1)S(1)} %get-tuple-element.88), channel_id=1, source_target_pairs={{0,64},{1,65},{2,66},{3,67},{4,68},{5,69},{6,70},{7,71},{8,72},{9,... | collective-permute-start | bytes 221192 | tf_op jit(solution)/shard_map/ppermute | solution.py:664
  89.8 4.9 %collective-permute-start.26 = (bf16[144,256]{1,0:T(8,128)(2,1)S(1)}, bf16[144,256]{1,0:T(8,128)(2,1)S(1)}, u32[]{:S(2)}, u32[]{:S(2)}) collective-permute-start(bf16[144,256]{1,0:T(8,128)(2,1)S(1)} %k_y_sum.1.after.own), channel_id=1, source_target_pairs={{0,4},{1,5},{2,6},{3,7},{4,0},{5,1},{6,2},{7,3},{8,12},{9,13},{10,... | collective-permute-start | bytes 221192 | tf_op jit(solution)/shard_map/ppermute | solution.py:664
  89.8 5.3 %collective-permute-start.25 = (bf16[144,256]{1,0:T(8,128)(2,1)S(1)}, bf16[144,256]{1,0:T(8,128)(2,1)S(1)}, u32[]{:S(2)}, u32[]{:S(2)}) collective-permute-start(bf16[144,256]{1,0:T(8,128)(2,1)S(1)} %k_y_sum.1.after.own), channel_id=1, source_target_pairs={{0,20},{1,21},{2,22},{3,23},{4,16},{5,17},{6,18},{7,19},{8,28},{9,... | collective-permute-start | bytes 221192 | tf_op jit(solution)/shard_map/ppermute | solution.py:664
  95.2 6.2 %collective-permute-start.29 = (bf16[144,256]{1,0:T(8,128)(2,1)S(1)}, bf16[144,256]{1,0:T(8,128)(2,1)S(1)}, u32[]{:S(2)}, u32[]{:S(2)}) collective-permute-start(bf16[144,256]{1,0:T(8,128)(2,1)S(1)} %k_x_sum.1.own), channel_id=1, source_target_pairs={{0,64},{1,65},{2,66},{3,67},{4,68},{5,69},{6,70},{7,71},{8,72},{9,... | collective-permute-start | bytes 221192 | tf_op jit(solution)/shard_map/ppermute | solution.py:664
  96.8 4.6 %collective-permute-start.28 = (bf16[144,256]{1,0:T(8,128)(2,1)S(1)}, bf16[144,256]{1,0:T(8,128)(2,1)S(1)}, u32[]{:S(2)}, u32[]{:S(2)}) collective-permute-start(bf16[144,256]{1,0:T(8,128)(2,1)S(1)} %k_x_sum.1.own), channel_id=1, source_target_pairs={{0,96},{1,97},{2,98},{3,99},{4,100},{5,101},{6,102},{7,103},{8,104... | collective-permute-start | bytes 221192 | tf_op jit(solution)/shard_map/ppermute | solution.py:664
  102.8 8.3 %collective-permute-start.35 = (bf16[576,256]{1,0:T(8,128)(2,1)S(1)}, bf16[576,256]{1,0:T(8,128)(2,1)S(1)}, u32[]{:S(2)}, u32[]{:S(2)}) collective-permute-start(bf16[576,256]{1,0:T(8,128)(2,1)S(1)} %k_join.1.a0.after), channel_id=1, source_target_pairs={{0,2},{1,3},{2,0},{3,1},{4,6},{5,7},{6,4},{7,5},{8,10},{9,11},{10,... | collective-permute-start | bytes 884744 | tf_op jit(solution)/shard_map/ppermute | solution.py:664
  104.6 12.5 %collective-permute-start.33 = (bf16[576,256]{1,0:T(8,128)(2,1)S(1)}, bf16[576,256]{1,0:T(8,128)(2,1)S(1)}, u32[]{:S(2)}, u32[]{:S(2)}) collective-permute-start(bf16[576,256]{1,0:T(8,128)(2,1)S(1)} %k_join.1.a0.after), channel_id=1, source_target_pairs={{0,3},{1,2},{2,1},{3,0},{4,7},{5,6},{6,5},{7,4},{8,11},{9,10},{10,... | collective-permute-start | bytes 884744 | tf_op jit(solution)/shard_map/ppermute | solution.py:664
  105.9 14.2 %collective-permute-start.31 = (bf16[576,256]{1,0:T(8,128)(2,1)S(1)}, bf16[576,256]{1,0:T(8,128)(2,1)S(1)}, u32[]{:S(2)}, u32[]{:S(2)}) collective-permute-start(bf16[576,256]{1,0:T(8,128)(2,1)S(1)} %k_join.1.a0.after), channel_id=1, source_target_pairs={{0,1},{1,0},{2,3},{3,2},{4,5},{5,4},{6,7},{7,6},{8,9},{9,8},{10,11... | collective-permute-start | bytes 884744 | tf_op jit(solution)/shard_map/ppermute | solution.py:664
  105.9 16.3 %collective-permute-start.30 = (bf16[576,256]{1,0:T(8,128)(2,1)S(1)}, bf16[576,256]{1,0:T(8,128)(2,1)S(1)}, u32[]{:S(2)}, u32[]{:S(2)}) collective-permute-start(bf16[576,256]{1,0:T(8,128)(2,1)S(1)} %k_join.1.a0.after), channel_id=1, source_target_pairs={{0,8},{1,9},{2,10},{3,11},{4,12},{5,13},{6,14},{7,15},{8,0},{9,1},... | collective-permute-start | bytes 884744 | tf_op jit(solution)/shard_map/ppermute | solution.py:664
  111.1 11.1 %collective-permute-start.36 = (bf16[576,256]{1,0:T(8,128)(2,1)S(1)}, bf16[576,256]{1,0:T(8,128)(2,1)S(1)}, u32[]{:S(2)}, u32[]{:S(2)}) collective-permute-start(bf16[576,256]{1,0:T(8,128)(2,1)S(1)} %collective-permute-done.35.a2), channel_id=1, source_target_pairs={{0,8},{1,9},{2,10},{3,11},{4,12},{5,13},{6,14},{7,15},{8,0},{9,1},... | collective-permute-start | bytes 884744 | tf_op jit(solution)/shard_map/ppermute | solution.py:664
  117.1 5.1 %collective-permute-start.34 = (bf16[576,256]{1,0:T(8,128)(2,1)S(1)}, bf16[576,256]{1,0:T(8,128)(2,1)S(1)}, u32[]{:S(2)}, u32[]{:S(2)}) collective-permute-start(bf16[576,256]{1,0:T(8,128)(2,1)S(1)} %collective-permute-done.33.a3), channel_id=1, source_target_pairs={{0,8},{1,9},{2,10},{3,11},{4,12},{5,13},{6,14},{7,15},{8,0},{9,1},... | collective-permute-start | bytes 884744 | tf_op jit(solution)/shard_map/ppermute | solution.py:664
  (17 other events, 70.4 us)
